TPU v7x, 512 devices: a whole 4x8x8 slice. The times are simulated.
512 devices in a mesh: ctx: 64 (over y_lo, z, core), tp: 8 (over x, y_hi).
Axes of the slice: x: 4, y: 8 (y_hi: 2, y_lo: 4; y = y_hi * 4 + y_lo), z: 8, core: 2. Of those that a mesh axis runs over, the one named last changes fastest.
Arguments:
- latent_tokens: float32 [8192, 64], P('ctx'), may hold values from -6 to 6
- positions: int32 [8192], P('ctx'), may hold values from 0 to 8191, as said below
- queries: bfloat16 [8192, 2048], P('ctx', 'tp'), may hold values from -12 to 12
- key_states: bfloat16 [8192, 2048], P('ctx', 'tp'), may hold values from -12 to 12
- value_states: bfloat16 [8192, 2048], P('ctx', 'tp'), may hold values from -6 to 6
- attention_out: bfloat16 [8192, 2048], P('ctx', 'tp'), may hold values from -6 to 6
- projection: bfloat16 [2048, 128], P('tp'), may hold values from -0.125 to 0.125
Outputs:
- query_grad: bfloat16 [8192, 2048], P('ctx', 'tp')
- key_grad: bfloat16 [8192, 2048], P('ctx', 'tp')
- value_grad: bfloat16 [8192, 2048], P('ctx', 'tp')
Inputs may be any that keep to these rules, and one draw needn't show every extreme that they name: A permutation of the positions 0 to 8191. The sequence is cut into 128 blocks of 64 consecutive positions, block b holding positions b * 64 to (b + 1) * 64 - 1. Rows k * 128 to (k + 1) * 128 - 1 hold one block b below 64 in increasing order, then block 127 - b in increasing order; each such b appears in exactly one such group of rows.
All inputs are finite; a program needn't handle non-finite values.
Results may differ from a plain program's by a relative error of at most 0.022.
Values may be sent and summed in bfloat16 or wider, within the bound.
No kernel may reach another device: no remote copies, remote signals or barrier semaphores. Data moves between devices by JAX's collectives and lax.ppermute only.
A program may use at most 128 MiB of HBM per device.

v0:
```python
import jax
import jax.numpy as jnp
from jax import lax
from jax.sharding import PartitionSpec as P

HEAD = 128


def coupling_grad(latent_tokens, coupled, projection, latent_width):
    shifts = coupled[:, :latent_width]
    log_scale = coupled[:, latent_width:]
    damping = jnp.exp(-log_scale)
    normed = (latent_tokens - shifts) * damping
    upstream = jnp.concatenate([-normed * damping, 1.0 - normed * normed], axis=1).astype(
        jnp.bfloat16
    )
    return jnp.dot(upstream, projection.T, preferred_element_type=jnp.float32).astype(jnp.bfloat16)


def query_update(
    carried, query_heads, dout_heads, delta_rows, query_pos, key_heads, value_heads, key_pos, factor
):
    row_top, totals, accumulated = carried
    scores = (
        jnp.einsum("qhd,khd->hqk", query_heads, key_heads, preferred_element_type=jnp.float32)
        * factor
    )
    allowed = key_pos[None, None, :] <= query_pos[None, :, None]
    piece_top = jnp.max(jnp.where(allowed, scores, -1e30), axis=2)
    top_new = jnp.maximum(row_top, piece_top)
    lifted = jnp.where(allowed, scores, top_new[:, :, None]) - top_new[:, :, None]
    weight = jnp.where(allowed, jnp.exp(lifted), 0.0)
    totals_new = jnp.sum(weight, axis=2)
    prob_grad = jnp.einsum(
        "qhd,khd->hqk", dout_heads, value_heads, preferred_element_type=jnp.float32
    )
    mixture = weight * (prob_grad - delta_rows.T[:, :, None])
    gained = jnp.einsum(
        "hqk,khd->hqd", mixture, key_heads.astype(jnp.float32), precision=lax.Precision.HIGHEST
    )
    return (top_new, totals_new, gained)


def key_update(
    key_heads,
    value_heads,
    key_pos,
    query_heads,
    grad_heads,
    query_pos,
    lse_rows,
    delta_rows,
    factor,
):
    scores = (
        jnp.einsum("khd,qhd->hkq", key_heads, query_heads, preferred_element_type=jnp.float32)
        * factor
    )
    allowed = key_pos[None, :, None] <= query_pos[None, None, :]
    probs = jnp.exp(jnp.where(allowed, scores - lse_rows.T[:, None, :], -1e30))
    prob_grad = jnp.einsum(
        "khd,qhd->hkq", value_heads, grad_heads, preferred_element_type=jnp.float32
    )
    score_grad = probs * (prob_grad - delta_rows.T[:, None, :])
    value_sum = jnp.einsum(
        "hkq,qhd->khd", probs.astype(jnp.bfloat16), grad_heads, preferred_element_type=jnp.float32
    )
    key_sum = jnp.einsum(
        "hkq,qhd->khd",
        score_grad.astype(jnp.bfloat16),
        query_heads,
        preferred_element_type=jnp.float32,
    )
    return (key_sum, value_sum)


def local(latent_tokens, positions, queries, key_states, value_states, attention_out, projection):
    row_count = queries.shape[0]
    head_size = HEAD
    head_count = queries.shape[1] // head_size
    latent_width = latent_tokens.shape[1]
    factor = head_size ** (-0.5)
    partial_coupled = jnp.dot(attention_out, projection, preferred_element_type=jnp.float32)
    coupled = lax.psum(partial_coupled, "tp")
    out_grad = coupling_grad(latent_tokens, coupled, projection, latent_width)
    product = out_grad.astype(jnp.float32) * attention_out.astype(jnp.float32)
    row_delta = jnp.sum(product.reshape(row_count, head_count, head_size), axis=2)
    every_position = lax.all_gather(positions, "ctx", axis=0, tiled=True)
    query_heads = queries.reshape(row_count, head_count, head_size)
    dout_heads = out_grad.reshape(row_count, head_count, head_size)
    key_heads = key_states.reshape(row_count, head_count, head_size)
    value_heads = value_states.reshape(row_count, head_count, head_size)
    portions = 1
    half_rows = row_count // portions
    start_state = tuple(
        (
            (
                jnp.full((head_count, half_rows), -1e30, jnp.float32),
                jnp.zeros((head_count, half_rows), jnp.float32),
                jnp.zeros((head_count, half_rows, head_size), jnp.float32),
            )
            for portion in range(portions)
        )
    )
    key_block = lax.all_gather(key_states, "ctx", axis=0, tiled=True)
    value_block = lax.all_gather(value_states, "ctx", axis=0, tiled=True)
    block_rows = key_block.shape[0]
    key_pos = every_position
    key_part = key_block.reshape(block_rows, head_count, head_size)
    value_part = value_block.reshape(block_rows, head_count, head_size)
    updated = []
    first_row = 0
    query_pos = positions

    def key_advance(state, first_row=first_row, query_pos=query_pos):
        return query_update(
            state,
            query_heads,
            dout_heads,
            row_delta,
            query_pos,
            key_part,
            value_part,
            key_pos,
            factor,
        )

    updated.append(key_advance(start_state[0]))
    finished = tuple(updated)
    row_top = jnp.concatenate([state[0] for state in finished], axis=1)
    totals = jnp.concatenate([state[1] for state in finished], axis=1)
    accumulated = jnp.concatenate([state[2] for state in finished], axis=1)
    lse = row_top + jnp.log(totals)
    query_out = (
        (accumulated / totals[:, :, None] * factor)
        .transpose(1, 0, 2)
        .reshape(row_count, head_count * head_size)
    )
    all_lse, all_delta = (
        lax.all_gather(lse.T, "ctx", axis=0, tiled=True),
        lax.all_gather(row_delta, "ctx", axis=0, tiled=True),
    )

    def query_fold(carried, block_in):
        query_block, grad_block = block_in
        block_rows = query_block.shape[0]
        query_part = query_block.reshape(block_rows, head_count, head_size)
        grad_part = grad_block.reshape(block_rows, head_count, head_size)
        first_row = 0
        key_pos = positions

        def query_advance(state, first_row=first_row, key_pos=key_pos):
            return key_update(
                key_heads,
                value_heads,
                key_pos,
                query_part,
                grad_part,
                every_position,
                all_lse,
                all_delta,
                factor,
            )

        updated = [query_advance(carried[0])]
        return tuple(updated)

    zero_state = tuple(
        (
            (
                jnp.zeros((half_rows, head_count, head_size), jnp.float32),
                jnp.zeros((half_rows, head_count, head_size), jnp.float32),
            )
            for portion in range(portions)
        )
    )
    key_done = query_fold(
        zero_state,
        (
            lax.all_gather(queries, "ctx", axis=0, tiled=True),
            lax.all_gather(out_grad, "ctx", axis=0, tiled=True),
        ),
    )
    key_out = jnp.concatenate([state[0] for state in key_done], axis=0) * factor
    value_out = jnp.concatenate([state[1] for state in key_done], axis=0)
    width = head_count * head_size
    return (
        query_out.astype(jnp.bfloat16),
        key_out.reshape(row_count, width).astype(jnp.bfloat16),
        value_out.reshape(row_count, width).astype(jnp.bfloat16),
    )


def solution(mesh):
    placed = (
        P("ctx", None),
        P("ctx"),
        P("ctx", "tp"),
        P("ctx", "tp"),
        P("ctx", "tp"),
        P("ctx", "tp"),
        P("tp", None),
    )
    return jax.shard_map(
        local,
        mesh=mesh,
        in_specs=placed,
        out_specs=(P("ctx", "tp"), P("ctx", "tp"), P("ctx", "tp")),
        check_vma=False,
    )
```

profile of v0, /device:TPU:1, one launch (start us, length us, event | category | flops | bytes accessed | tf_op | source)
XLA Modules:
  0.0 540.2 jit_solution(6063910312888940623)
XLA Ops:
  8.0 0.0 copy-start
  8.0 0.0 copy-start.4
  8.0 0.0 all-reduce.2.cloned.1.call-start
  8.1 0.8 copy-done
  8.8 1.7 fusion.35
  10.5 0.0 all-reduce.2.cloned.1.call-update
  10.6 0.0 all-gather.6.cloned.1.call-start
  10.6 1.6 copy.66
  12.2 0.0 all-gather.6.cloned.1.call-update
  12.2 0.0 all-gather.8.cloned.1.call-start
  12.3 1.6 copy.70
  13.8 0.0 all-gather.8.cloned.1.call-update
  13.9 0.0 all-gather.10.cloned.1.call-start
  13.9 1.6 copy.74
  15.5 0.0 all-gather.10.cloned.1.call-update
  15.5 0.0 all-gather.12.cloned.1.call-start
  15.6 108.1 %all-reduce.2.cloned.1.call-done = f32[128,128]{0,1:T(8,128)} async-done(((f32[128,128]{0,1:T(8,128)}), f32[128,128]{0,1:T(8,128)}) %all-reduce.2.cloned.1.call-update) | async-done | bytes 65552 | tf_op jit(solution)/shard_map/psum | solution.py:84
  123.7 0.8 multiply_convert_fusion
  124.5 1.7 convert_multiply_fusion
  126.2 0.0 all-gather.12.cloned.1.call-update
  126.2 83.2 %all-gather = s32[64,1,128]{2,1,0:T(1,128)S(1)} all-gather(s32[1,1,128]{2,1,0:T(1,128)} %bitcast.98), channel_id=1, replica_groups=mesh['ctx'=64,'tp'=8] {'ctx'}, dimensions={0}, use_global_device_ids=true | all-gather | bytes 33280 | tf_op jit(solution)/shard_map/all_gather | solution.py:88
  209.4 2.0 broadcast_compare_fusion
  211.5 0.1 reshape.106
  211.5 0.2 reduce_sum.18
  211.8 0.1 copy.73
  211.8 95.4 %all_gather.27 = f32[8192,2]{1,0:T(8,128)} all-gather(f32[128,2]{1,0:T(8,128)S(1)} %reduce_sum.18), channel_id=1, replica_groups=mesh['ctx'=64,'tp'=8] {'ctx'}, dimensions={0}, use_global_device_ids=true | all-gather | bytes 66560 | tf_op jit(solution)/shard_map/all_gather | solution.py:141
  307.2 2.8 copy.79
  310.1 0.0 all-gather.6.cloned.1.call-done
  310.1 0.0 copy-done.4
  310.1 4.6 select_reduce_fusion
  314.7 0.0 copy-start.1
  314.7 0.0 copy-start.3
  314.7 3.2 copy-done.1
  317.9 2.5 fusion.7
  320.4 0.0 all-gather.8.cloned.1.call-done
  320.4 0.0 copy-done.3
  320.5 0.0 copy-start.2
  320.5 7.4 %fusion.3 = f32[2,128,8192]{2,1,0:T(8,128)S(1)} fusion(bf16[8192,2,128]{0,2,1:T(8,128)(2,1)} %bitcast.88, f32[2,128,8192]{2,1,0:T(8,128)} %copy-done.1, f32[2,128]{1,0:T(2,128)S(1)} %copy.73, f32[2,128]{1,0:T(2,128)S(1)} %broadcast_maximum_fusion, pred[128,8192]{1,0:T(8,128)(4,1)S(1)} %get-tuple-element.21, bf16[128,256]{1,0:T(8,128)(2,1)S(1)} %copy-done.3), kind=kOutput, calls=%fused_computation.6 | convolution fusion | flops 547356672 | bytes 22087680 | tf_op jit(solution)/shard_map/qhd,khd->hqk/dot_general | solution.py:34
  327.9 0.0 copy-start.6
  327.9 0.0 copy-done.2
  327.9 4.2 fusion.14
  332.1 0.7 copy.82
  332.9 74.2 %all_gather.25 = f32[8192,2]{0,1:T(2,128)S(1)} all-gather(f32[128,2]{0,1:T(2,128)S(1)} %bitcast_add_fusion), channel_id=1, replica_groups=mesh['ctx'=64,'tp'=8] {'ctx'}, dimensions={0}, use_global_device_ids=true | all-gather | bytes 66560 | tf_op jit(solution)/shard_map/all_gather | solution.py:140
  407.1 0.0 all-gather.10.cloned.1.call-done
  407.1 0.0 copy-done.6
  407.1 8.3 %fusion.5 = f32[2,128,8192]{2,1,0:T(8,128)} fusion(bf16[8192,2,128]{0,2,1:T(8,128)(2,1)} %bitcast.89, f32[2,8192]{1,0:T(2,128)S(1)} %bitcast.96, pred[128,8192]{1,0:T(8,128)(4,1)S(1)} %get-tuple-element.20, bf16[128,256]{1,0:T(8,128)(2,1)S(1)} %copy-done.6), kind=kOutput, calls=%fused_computation.9 | convolution fusion | flops 543162368 | bytes 13762560 | tf_op jit(solution)/shard_map/khd,qhd->hkq/dot_general | solution.py:56
  415.4 95.3 %all-gather.12.cloned.1.call-done = bf16[8192,256]{1,0:T(8,128)(2,1)} async-done(((bf16[128,256]{1,0:T(8,128)(2,1)}), bf16[8192,256]{1,0:T(8,128)(2,1)}) %all-gather.12.cloned.1.call-update) | async-done | bytes 4194320 | tf_op jit(solution)/shard_map/all_gather | solution.py:181
  510.7 6.4 %copy.90 = bf16[8192,256]{0,1:T(8,128)(2,1)} copy(bf16[8192,256]{1,0:T(8,128)(2,1)} %all-gather.12.cloned.1.call-done) | data formatting | bytes 8388608 | tf_op jit(solution)/shard_map/reshape | solution.py:148
  517.1 0.0 copy-start.5
  517.1 5.9 %fusion.15 = bf16[2,128,128]{2,1,0:T(8,128)(2,1)S(1)} fusion(bf16[8192,2,128]{0,2,1:T(8,128)(2,1)} %bitcast.83, f32[2,128,8192]{2,1,0:T(8,128)} %fusion.5), kind=kOutput, calls=%fused_computation.24 | convolution fusion | flops 539000832 | bytes 12648448 | tf_op jit(solution)/shard_map/hkq,qhd->khd/dot_general | solution.py:65
  523.0 0.0 copy-done.5
  523.0 8.1 %fusion.18 = bf16[2,128,128]{1,2,0:T(8,128)(2,1)S(1)} fusion(bf16[8192,2,128]{0,2,1:T(8,128)(2,1)} %bitcast.90, f32[2,128,8192]{2,1,0:T(8,128)} %fusion.5, bf16[8192,2,128]{0,2,1:T(8,128)(2,1)} %bitcast.84, f32[2,8192]{1,0:T(2,128)S(1)} %copy.79, bf16[128,256]{1,0:T(8,128)(2,1)S(1)} %copy-done.5), kind=kOutput, calls=%fused_computation.26 | convolution fusion | flops 1080098816 | bytes 16973824 | tf_op jit(solution)/shard_map/hkq,qhd->khd/dot_general | solution.py:68
  531.1 0.7 copy.83
  531.9 0.7 copy.84
  (2 shorter events, 0.0 us)
Async XLA Ops:
  8.0 0.8 copy-start
  8.0 302.1 %copy-start.4 = (bf16[128,256]{1,0:T(8,128)(2,1)S(1)}, bf16[128,256]{1,0:T(8,128)(2,1)}, u32[]{:S(2)}) copy-start(bf16[128,256]{1,0:T(8,128)(2,1)} %param.9) | copy-start | bytes 196612
  8.0 115.7 %all-reduce.2.cloned.1.call-start = ((), (), s32[]{:S(2)}) async-start(), calls=%async_computation.1 | async-start | bytes 131072 | tf_op jit(solution)/shard_map/psum | solution.py:84
  10.6 299.5 %all-gather.6.cloned.1.call-start = ((), (), s32[]{:S(2)}) async-start(), calls=%async_computation | async-start | bytes 4259840 | tf_op jit(solution)/shard_map/all_gather | solution.py:105
  12.2 308.2 %all-gather.8.cloned.1.call-start = ((), (), s32[]{:S(2)}) async-start(), calls=%async_computation.2 | async-start | bytes 4259840 | tf_op jit(solution)/shard_map/all_gather | solution.py:106
  13.9 393.3 %all-gather.10.cloned.1.call-start = ((), (), s32[]{:S(2)}) async-start(), calls=%async_computation.3 | async-start | bytes 4259840 | tf_op jit(solution)/shard_map/all_gather | solution.py:180
  15.5 495.2 %all-gather.12.cloned.1.call-start = ((), (), s32[]{:S(2)}) async-start(), calls=%async_computation.4 | async-start | bytes 4259840 | tf_op jit(solution)/shard_map/all_gather | solution.py:181
  314.7 3.2 copy-start.1
  314.7 5.8 %copy-start.3 = (bf16[128,256]{1,0:T(8,128)(2,1)S(1)}, bf16[128,256]{1,0:T(8,128)(2,1)}, u32[]{:S(2)}) copy-start(bf16[128,256]{1,0:T(8,128)(2,1)} %get-tuple-element.23) | copy-start | bytes 196612
  320.5 7.5 %copy-start.2 = (bf16[8192,256]{0,1:T(8,128)(2,1)S(1)}, bf16[8192,256]{0,1:T(8,128)(2,1)}, u32[]{:S(2)}) copy-start(bf16[8192,256]{0,1:T(8,128)(2,1)} %all-gather.6.cloned.1.call-done) | copy-start | bytes 12582916
  327.9 79.2 %copy-start.6 = (bf16[128,256]{1,0:T(8,128)(2,1)S(1)}, bf16[128,256]{1,0:T(8,128)(2,1)}, u32[]{:S(2)}) copy-start(bf16[128,256]{1,0:T(8,128)(2,1)} %param.10) | copy-start | bytes 196612
  517.1 5.9 %copy-start.5 = (bf16[128,256]{1,0:T(8,128)(2,1)S(1)}, bf16[128,256]{1,0:T(8,128)(2,1)}, u32[]{:S(2)}) copy-start(bf16[128,256]{1,0:T(8,128)(2,1)} %param.11) | copy-start | bytes 196612
Sparse Core Ops, SparseCore 0:
  12.3 111.3 all-reduce.1
Sparse Core Ops, SparseCore 1:
  13.7 129.2 all-gather.5
  145.4 121.2 all-gather.7
  268.8 123.4 all-gather.9
  394.7 115.9 all-gather.11
where the time goes:
time: 541 us; the launch traced here: 540 us
  blocking collectives  253 us (47%)
  waiting for transfers between devices  204 us (38%)
  matrix products  41.9 us (8%)
  local copies, waits for them, and re-layouts  20.3 us (4%)
  between operations  15.8 us (3%)
  other arithmetic  5.53 us (1%)
    psum x1, waiting for transfers between devices, local(): coupled = lax.psum(partial_coupled, 'tp')  108 us
    all_gather x1, blocking collectives, local(): lax.all_gather(row_delta, 'ctx', axis=0, tiled=True)  95.4 us
    all_gather x1, waiting for transfers between devices, local(): lax.all_gather(out_grad, 'ctx', axis=0, tiled=True)  95.3 us
    all_gather x1, blocking collectives, local(): every_position = lax.all_gather(positions, 'ctx', axis=0, tiled=True)  83.2 us
    all_gather x1, blocking collectives, local(): lax.all_gather(lse.T, 'ctx', axis=0, tiled=True)  74.2 us
    unnamed x20, local copies, waits for them, and re-layouts  11 us
  transfers between devices with their start and end apart: 5, of which 2 were waited for; matrix products, arithmetic and copies ran while one was open for 7% of the time, Pallas kernels for 0%

commit v1 on v0

v1 whole, which is shorter than its diff:
```python
import functools

import jax
import jax.numpy as jnp
from jax import lax
from jax.experimental import pallas as pl
from jax.experimental.pallas import tpu as pltpu
from jax.sharding import Mesh, PartitionSpec as P

HEAD = 128
SPAN = 64
NZ, NY, NC = 8, 4, 2
LOG2E = 1.4426950408889634
FACTOR = HEAD ** (-0.5)
SCALE = FACTOR * LOG2E
MASKED = -(2.0**100)
F32 = jnp.float32
BF16 = jnp.bfloat16
NT = (((1,), (1,)), ((), ()))
MIB = 1 << 20


def dot_nt(a, b):
    return lax.dot_general(a, b, NT, preferred_element_type=F32)


def dot(a, b):
    return jnp.dot(a, b, preferred_element_type=F32)


def prep_kernel(pos_ref, q_ref, k_ref, v_ref, o_ref, proj_ref, qpay_ref, kvpay_ref, part_ref):
    block = lax.shift_right_logical(pos_ref[0], 6).astype(F32)
    tag = jnp.full((16, 256), block, F32).astype(BF16)
    q = q_ref[...]
    for i in range(NZ):
        qpay_ref[i, 0:128, :] = q
        qpay_ref[i, 128:144, :] = tag
    kvpay_ref[0:128, :] = k_ref[...]
    kvpay_ref[128:256, :] = v_ref[...]
    kvpay_ref[256:272, :] = tag
    part_ref[...] = dot(o_ref[...], proj_ref[...])


def query_positions(qg_ref):
    lane = lax.broadcasted_iota(jnp.int32, (1, 128), 1)
    low = lane < SPAN
    row = (lane & (SPAN - 1)).astype(F32)
    early, late = [], []
    for p in range(NZ // 2):
        first = qg_ref[2 * p, 128:144, 0:128].astype(F32)[0:1, :]
        second = qg_ref[2 * p + 1, 128:144, 0:128].astype(F32)[0:1, :]
        block = jnp.where(low, first, second)
        early.append(block * SPAN + row)
        late.append((127.0 - block) * SPAN + row)
    return jnp.concatenate(early, axis=1), jnp.concatenate(late, axis=1)


def key_positions(kv_ref, late):
    row = lax.broadcasted_iota(jnp.int32, (SPAN, 128), 0).astype(F32)
    out = []
    for j in range(NY):
        block = kv_ref[j, 256:272, 0:128].astype(F32)[0:1, :]
        base = (127.0 - block) * SPAN if late else block * SPAN
        out.append(base + row)
    column = jnp.concatenate(out, axis=0)
    return jnp.concatenate([column] * 4, axis=1)


def rows_of(ref, start, head):
    part = ref[:, start : start + SPAN, head * HEAD : (head + 1) * HEAD]
    return part.reshape(part.shape[0] * SPAN, HEAD)


def stats_kernel(qg_ref, kva_ref, kvb_ref, out_ref, s_ref, st_ref):
    q_early, q_late = query_positions(qg_ref)
    sides = (kva_ref, kvb_ref)
    for head in range(2):
        for part in range(2):
            q = rows_of(qg_ref, part * SPAN, head)
            top = None
            units = []
            for n, kv in enumerate(sides):
                units.append((n, kv, 0, part == 0))
                if part == 1:
                    units.append((n + 2, kv, SPAN, True))
            for slot, kv, start, masked in units:
                s = dot_nt(rows_of(kv, start, head), q) * SCALE
                if masked:
                    qp = q_late if start else q_early
                    s = jnp.where(key_positions(kv, start > 0) <= qp, s, MASKED)
                s_ref[slot] = s
                here = jnp.max(s.reshape(32, 8, 512), axis=0)
                top = here if top is None else jnp.maximum(top, here)
            top = jnp.max(top, axis=0, keepdims=True).astype(BF16).astype(F32)
            total = jnp.zeros((8, 512), F32)
            for slot, kv, start, masked in units:
                p = jnp.exp2(s_ref[slot] - top)
                total = total + jnp.sum(p.reshape(32, 8, 512), axis=0)
            total = jnp.sum(total, axis=0, keepdims=True)
            high = total.astype(BF16).astype(F32)
            low = total - high
            base = (head * 2 + part) * 12
            for r in range(4):
                lanes = slice(r * 128, (r + 1) * 128)
                st_ref[base + r : base + r + 1, :] = top[:, lanes]
                st_ref[base + 4 + r : base + 5 + r, :] = high[:, lanes]
                st_ref[base + 8 + r : base + 9 + r, :] = low[:, lanes]
    out_ref[...] = st_ref[...].astype(BF16)


def pack_kernel(acc_ref, recv_ref, lat_ref, proj_ref, o_ref, st_ref, out_ref, d_ref):
    coupled = acc_ref[...] + recv_ref[...]
    shifts = coupled[:, 0:64]
    log_scale = coupled[:, 64:128]
    damping = jnp.exp(-log_scale)
    normed = (lat_ref[...] - shifts) * damping
    upstream = jnp.concatenate([-normed * damping, 1.0 - normed * normed], axis=1).astype(BF16)
    d_ref[...] = jnp.zeros((16, 128), F32)
    for head in range(2):
        cols = slice(head * HEAD, (head + 1) * HEAD)
        grad = dot_nt(upstream, proj_ref[cols, :]).astype(BF16)
        product = grad.astype(F32) * o_ref[:, cols].astype(F32)
        delta = jnp.sum(product.T, axis=0, keepdims=True)
        high = delta.astype(BF16).astype(F32)
        d_ref[2 * head : 2 * head + 1, :] = high
        d_ref[2 * head + 1 : 2 * head + 2, :] = delta - high
    deltas = d_ref[...].astype(BF16)
    stats = st_ref[...]
    for i in range(NZ):
        out_ref[i, 0:128, :] = upstream
        out_ref[i, 128:144, :] = deltas
        out_ref[i, 144:192, :] = stats


def main_kernel(qg_ref, kva_ref, kvb_ref, g_ref, proj_ref, dq_ref, da_ref, db_ref, ds_ref):
    q_early, q_late = query_positions(qg_ref)
    lane = lax.broadcasted_iota(jnp.int32, (1, 128), 1)
    low = lane < SPAN
    upstream = [
        g_ref[:, part * SPAN : (part + 1) * SPAN, :].reshape(NZ * SPAN, HEAD) for part in range(2)
    ]
    tails = [g_ref[i, 128:144, :].astype(F32) for i in range(NZ)]
    turned = [pltpu.roll(t, SPAN, 1) for t in tails]
    stats = g_ref[:, 144:192, :].astype(F32)
    sides = (kva_ref, kvb_ref)
    grads = (da_ref, db_ref)
    for head in range(2):
        cols = slice(head * HEAD, (head + 1) * HEAD)
        proj = proj_ref[cols, :]
        lse, delta, q, dout = [], [], [], []
        for part in range(2):
            base = (head * 2 + part) * 12
            tops = stats[:, base : base + 4, :]
            sums = stats[:, base + 4 : base + 8, :] + stats[:, base + 8 : base + 12, :]
            top = jnp.max(tops, axis=0)
            total = jnp.sum(sums * jnp.exp2(tops - top[None]), axis=0)
            value = top + jnp.log(total) * LOG2E
            lse.append(jnp.concatenate([value[r : r + 1, :] for r in range(4)], axis=1))
            pieces = []
            for p in range(NZ // 2):
                left = (tails if part == 0 else turned)[2 * p]
                right = (turned if part == 0 else tails)[2 * p + 1]
                both = jnp.where(low, left, right)
                pieces.append(both[2 * head : 2 * head + 1, :] + both[2 * head + 1 : 2 * head + 2, :])
            delta.append(jnp.concatenate(pieces, axis=1))
            q.append(rows_of(qg_ref, part * SPAN, head))
            dout.append(dot_nt(upstream[part], proj).astype(BF16))

        def unit(keys, values, kp, part):
            t = dot_nt(keys, q[part]) * SCALE - lse[part]
            if kp is not None:
                t = jnp.where(kp <= (q_late if part else q_early), t, MASKED)
            p = jnp.exp2(t)
            ds = p * (dot_nt(values, dout[part]) - delta[part])
            return p.astype(BF16), ds.astype(BF16)

        for n in range(2):
            kv, grad = sides[n], grads[n]
            keys = rows_of(kv, 0, head)
            values = rows_of(kv, 128, head)
            pe, se = unit(keys, values, key_positions(kv, False), 0)
            ds_ref[n * 256 : (n + 1) * 256, 0:512] = se
            dv = dot(pe, dout[0])
            dk = dot(se, q[0])
            pd, sd = unit(keys, values, None, 1)
            ds_ref[n * 256 : (n + 1) * 256, 512:1024] = sd
            dv = dv + dot(pd, dout[1])
            dk = dk + dot(sd, q[1])
            grad[:, 0:64, cols] = (dk * FACTOR).astype(BF16).reshape(NY, SPAN, HEAD)
            grad[:, 128:192, cols] = dv.astype(BF16).reshape(NY, SPAN, HEAD)
            keys = rows_of(kv, 64, head)
            values = rows_of(kv, 192, head)
            pd, sd = unit(keys, values, key_positions(kv, True), 1)
            ds_ref[512 + n * 256 : 512 + (n + 1) * 256, 512:1024] = sd
            dv = dot(pd, dout[1])
            dk = dot(sd, q[1])
            grad[:, 64:128, cols] = (dk * FACTOR).astype(BF16).reshape(NY, SPAN, HEAD)
            grad[:, 192:256, cols] = dv.astype(BF16).reshape(NY, SPAN, HEAD)
        early_t = jnp.concatenate([rows_of(kv, 0, head) for kv in sides], axis=0).T
        late_t = jnp.concatenate([rows_of(kv, 64, head) for kv in sides], axis=0).T
        dqe = dot(early_t, ds_ref[0:512, 0:512])
        dql = dot(early_t, ds_ref[0:512, 512:1024]) + dot(late_t, ds_ref[512:1024, 512:1024])
        dq_ref[:, 0:64, cols] = (dqe * FACTOR).T.astype(BF16).reshape(NZ, SPAN, HEAD)
        dq_ref[:, 64:128, cols] = (dql * FACTOR).T.astype(BF16).reshape(NZ, SPAN, HEAD)


def fold_kernel(own_ref, recv_ref, o0_ref, o1_ref, o2_ref, o3_ref):
    o0_ref[...] = own_ref[0].astype(F32) + recv_ref[0].astype(F32)
    for k, ref in ((1, o1_ref), (2, o2_ref), (3, o3_ref)):
        ref[...] = (own_ref[k].astype(F32) + recv_ref[k].astype(F32)).astype(BF16)


def final_kernel(own_ref, r1_ref, r2_ref, r3_ref, dq_ref, qo_ref, ko_ref, vo_ref):
    total = own_ref[...]
    for ref in (r1_ref, r2_ref, r3_ref):
        total = total + ref[...].astype(F32)
    ko_ref[...] = total[0:128, :].astype(BF16)
    vo_ref[...] = total[128:256, :].astype(BF16)
    dq = dq_ref[0].astype(F32)
    for i in range(1, NZ):
        dq = dq + dq_ref[i].astype(F32)
    qo_ref[...] = dq.astype(BF16)


def call(kernel, outs, cost, scratch=(), smem=0, limit=48):
    vmem = pl.BlockSpec(memory_space=pltpu.VMEM)

    def run(*args):
        specs = [vmem] * len(args)
        if smem:
            specs[0] = pl.BlockSpec(memory_space=pltpu.SMEM)
        return pl.pallas_call(
            kernel,
            out_shape=[jax.ShapeDtypeStruct(s, d) for s, d in outs],
            in_specs=specs,
            out_specs=[vmem] * len(outs),
            scratch_shapes=list(scratch),
            compiler_params=pltpu.CompilerParams(vmem_limit_bytes=limit * MIB),
            cost_estimate=pl.CostEstimate(flops=cost, bytes_accessed=2 * MIB, transcendentals=0),
        )(*args)

    return run


def swap(x, axis, size, k):
    return lax.ppermute(x, axis, [(i, i ^ k) for i in range(size)])


def local(n_tp, latent, positions, queries, keys, values, attention_out, projection):
    with jax.named_scope("prep"):
        qpay, kvpay, total = call(
            prep_kernel,
            [((NZ, 144, 256), BF16), ((272, 256), BF16), ((128, 128), F32)],
            10_000_000,
            smem=1,
        )(positions, queries, keys, values, attention_out, projection)
    with jax.named_scope("kv_over_y"):
        arrived = [swap(kvpay, "y", NY, k) for k in (1, 2, 3)]
    rounds = [k for k in (2, 4, 1) if k < n_tp]
    extra = jnp.zeros_like(total)
    for n, k in enumerate(rounds):
        with jax.named_scope("coupled_over_tp"):
            extra = swap(total, "tp", n_tp, k)
            if n < len(rounds) - 1:
                total = total + extra
    with jax.named_scope("q_over_z"):
        qg = lax.all_to_all(qpay, "z", 0, 0)
    with jax.named_scope("kv_over_core"):
        kva = jnp.stack([kvpay] + arrived)
        kvb = swap(kva, "c", NC, 1)
    with jax.named_scope("stats"):
        (stats,) = call(
            stats_kernel,
            [((48, 128), BF16)],
            1_000_000_000,
            [pltpu.VMEM((4, 256, 512), F32), pltpu.VMEM((48, 128), F32)],
        )(qg, kva, kvb)
    with jax.named_scope("pack"):
        (pay,) = call(
            pack_kernel, [((NZ, 192, 128), BF16)], 10_000_000, [pltpu.VMEM((16, 128), F32)]
        )(total, extra, latent, projection, attention_out, stats)
    with jax.named_scope("upstream_over_z"):
        gathered = lax.all_to_all(pay, "z", 0, 0)
    with jax.named_scope("main"):
        dq, da, db = call(
            main_kernel,
            [((NZ, 128, 256), BF16), ((NY, 256, 256), BF16), ((NY, 256, 256), BF16)],
            4_000_000_000,
            [pltpu.VMEM((1024, 1024), BF16)],
        )(qg, kva, kvb, gathered, projection)
    with jax.named_scope("dkv_over_core"):
        other = swap(db, "c", NC, 1)
        own, *send = call(fold_kernel, [((256, 256), F32)] + [((256, 256), BF16)] * 3, 1_000_000)(
            da, other
        )
    with jax.named_scope("dkv_over_y"):
        back = [swap(s, "y", NY, k) for k, s in zip((1, 2, 3), send)]
    with jax.named_scope("dq_over_z"):
        dqs = lax.all_to_all(dq, "z", 0, 0)
    with jax.named_scope("final"):
        return tuple(
            call(final_kernel, [((128, 256), BF16)] * 3, 1_000_000)(own, *back, dqs)
        )


def solution(mesh):
    n_tp = mesh.shape["tp"]
    fine = Mesh(mesh.devices.reshape(NY, NZ, NC, n_tp), ("y", "z", "c", "tp"))
    ctx = ("y", "z", "c")
    placed = (
        P(ctx, None),
        P(ctx),
        P(ctx, "tp"),
        P(ctx, "tp"),
        P(ctx, "tp"),
        P(ctx, "tp"),
        P("tp", None),
    )
    return jax.shard_map(
        functools.partial(local, n_tp),
        mesh=fine,
        in_specs=placed,
        out_specs=(P(ctx, "tp"), P(ctx, "tp"), P(ctx, "tp")),
        check_vma=False,
    )
```

time: 541 us -> 112 us (0.21)
  the two profiles are of different devices: /device:TPU:1 before, /device:TPU:12 now
where the time goes in v1:
time: 112 us
  starting transfers between devices  48.4 us (43%)
  waiting for transfers between devices  28.8 us (26%)
  blocking collectives  18.8 us (17%)
  Pallas kernels  9.72 us (9%)
  local copies, waits for them, and re-layouts  4.96 us (4%)
    ppermute x11, starting transfers between devices, swap(): return lax.ppermute(x, axis, [(i, i ^ k) for i in range(size)])  34.6 us
    ppermute x11, waiting for transfers between devices, swap(): return lax.ppermute(x, axis, [(i, i ^ k) for i in range(size)])  28.7 us
    all_to_all x1, blocking collectives, local(): gathered = lax.all_to_all(pay, 'z', 0, 0)  18.8 us
    all_to_all x1, starting transfers between devices, local(): qg = lax.all_to_all(qpay, 'z', 0, 0)  10.3 us
    pallas_call x6, Pallas kernels, run(): pl.pallas_call(kernel, out_shape=[jax.ShapeDtypeStruct(s, d) for s, d in...  9.72 us
    unnamed x19, local copies, waits for them, and re-layouts  4.96 us
    all_to_all x1, starting transfers between devices, local(): dqs = lax.all_to_all(dq, 'z', 0, 0)  3.49 us
  transfers between devices with their start and end apart: 13, of which 9 were waited for; matrix products, arithmetic and copies ran while one was open for 0% of the time, Pallas kernels for 2%

profile of v1, /device:TPU:12, one launch (start us, length us, event | category | flops | bytes accessed | tf_op | source)
XLA Modules:
  0.0 111.5 jit_solution(8233777971928385186)
XLA Ops:
  0.6 0.0 copy-start
  0.6 0.8 copy-done
  1.5 0.0 copy-start.2
  1.5 0.8 copy-done.2
  2.3 0.0 copy-start.4
  2.3 0.8 copy-done.4
  3.2 0.0 copy-start.5
  3.2 0.8 copy-done.5
  4.0 0.0 copy-start.6
  4.0 0.8 copy-done.6
  4.8 0.0 copy-start.7
  4.8 0.7 copy-done.7
  5.5 1.5 %prep.1 = (bf16[8,144,256]{2,1,0:T(8,128)(2,1)}, bf16[272,256]{1,0:T(8,128)(2,1)S(1)}, f32[128,128]{1,0:T(8,128)S(1)}) custom-call(s32[128]{0:T(128)S(1)} %copy-done.7, bf16[128,256]{1,0:T(8,128)(2,1)S(1)} %copy-done.4, bf16[128,256]{1,0:T(8,128)(2,1)S(1)} %copy-done.5, bf16[128,256]{1,0:T(8,128)(2,1)S(1)} %copy-done.6, bf16[128,256]{1,0:T(8,128)(2,1)S(1)} %copy-done, ...), custom_call_target="tpu_custom_call" | custom-call | flops 10000000 | bytes 2097152 | tf_op jit(solution)/shard_map/prep/pallas_call | solution.py:232
  6.9 10.3 %all-to-all-start = ((bf16[8,144,256]{2,1,0:T(8,128)(2,1)}), bf16[8,144,256]{2,1,0:T(8,128)(2,1)S(1)}, u32[]{:S(2)}, u32[]{:S(2)}) async-start(bf16[8,144,256]{2,1,0:T(8,128)(2,1)} %get-tuple-element.13), calls=%async_computation | async-start | bytes 1179648 | tf_op jit(solution)/shard_map/q_over_z/all_to_all | solution.py:267
  17.3 3.5 %collective-permute-start.2 = (bf16[272,256]{1,0:T(8,128)(2,1)S(1)}, bf16[272,256]{1,0:T(8,128)(2,1)S(1)}, u32[]{:S(2)}, u32[]{:S(2)}) collective-permute-start(bf16[272,256]{1,0:T(8,128)(2,1)S(1)} %get-tuple-element.14), channel_id=1, source_target_pairs={{0,384},{128,256},{256,128},{384,0},{1,385},{129,257},{257,129},{3... | collective-permute-start | bytes 417800 | tf_op jit(solution)/shard_map/kv_over_y/ppermute | solution.py:246
  20.7 3.1 %collective-permute-start.1 = (bf16[272,256]{1,0:T(8,128)(2,1)S(1)}, bf16[272,256]{1,0:T(8,128)(2,1)S(1)}, u32[]{:S(2)}, u32[]{:S(2)}) collective-permute-start(bf16[272,256]{1,0:T(8,128)(2,1)S(1)} %get-tuple-element.14), channel_id=1, source_target_pairs={{0,256},{128,384},{256,0},{384,128},{1,257},{129,385},{257,1},{385... | collective-permute-start | bytes 417800 | tf_op jit(solution)/shard_map/kv_over_y/ppermute | solution.py:246
  23.9 3.2 %collective-permute-start = (bf16[272,256]{1,0:T(8,128)(2,1)S(1)}, bf16[272,256]{1,0:T(8,128)(2,1)S(1)}, u32[]{:S(2)}, u32[]{:S(2)}) collective-permute-start(bf16[272,256]{1,0:T(8,128)(2,1)S(1)} %get-tuple-element.14), channel_id=1, source_target_pairs={{0,128},{128,0},{256,384},{384,256},{1,129},{129,1},{257,385},{385... | collective-permute-start | bytes 417800 | tf_op jit(solution)/shard_map/kv_over_y/ppermute | solution.py:246
  27.1 4.2 %collective-permute-done.2 = bf16[272,256]{1,0:T(8,128)(2,1)S(1)} collective-permute-done((bf16[272,256]{1,0:T(8,128)(2,1)S(1)}, bf16[272,256]{1,0:T(8,128)(2,1)S(1)}, u32[]{:S(2)}, u32[]{:S(2)}) %collective-permute-start.2) | collective-permute-done | bytes 139296 | tf_op jit(solution)/shard_map/kv_over_y/ppermute | solution.py:246
  31.3 1.1 %collective-permute-done.1 = bf16[272,256]{1,0:T(8,128)(2,1)S(1)} collective-permute-done((bf16[272,256]{1,0:T(8,128)(2,1)S(1)}, bf16[272,256]{1,0:T(8,128)(2,1)S(1)}, u32[]{:S(2)}, u32[]{:S(2)}) %collective-permute-start.1) | collective-permute-done | bytes 139296 | tf_op jit(solution)/shard_map/kv_over_y/ppermute | solution.py:246
  32.4 0.3 collective-permute-done
  32.6 0.1 pad_maximum_fusion.kva_ref
  32.7 1.9 %collective-permute-start.3 = (bf16[4,272,256]{2,1,0:T(8,128)(2,1)S(1)}, bf16[4,272,256]{2,1,0:T(8,128)(2,1)S(1)}, u32[]{:S(2)}, u32[]{:S(2)}) collective-permute-start(bf16[4,272,256]{2,1,0:T(8,128)(2,1)S(1)} %pad_maximum_fusion.kva_ref), channel_id=1, source_target_pairs={{0,8},{8,0},{1,9},{9,1},{2,10},{10,2},{3,11},{11,3},{4,12},{12,4},... | collective-permute-start | bytes 1671176 | tf_op jit(solution)/shard_map/kv_over_core/ppermute | solution.py:246
  34.6 0.0 copy-start.8
  34.6 3.1 %collective-permute-start.4 = (f32[128,128]{1,0:T(8,128)S(1)}, f32[128,128]{1,0:T(8,128)S(1)}, u32[]{:S(2)}, u32[]{:S(2)}) collective-permute-start(f32[128,128]{1,0:T(8,128)S(1)} %get-tuple-element.15), channel_id=1, source_target_pairs={{0,2},{1,3},{2,0},{3,1},{4,6},{5,7},{6,4},{7,5},{8,10},{9,11},{10,... | collective-permute-start | bytes 196616 | tf_op jit(solution)/shard_map/coupled_over_tp/ppermute | solution.py:246
  37.8 3.3 %collective-permute-done.4 = f32[128,128]{1,0:T(8,128)S(1)} collective-permute-done((f32[128,128]{1,0:T(8,128)S(1)}, f32[128,128]{1,0:T(8,128)S(1)}, u32[]{:S(2)}, u32[]{:S(2)}) %collective-permute-start.4) | collective-permute-done | bytes 65568 | tf_op jit(solution)/shard_map/coupled_over_tp/ppermute | solution.py:246
  41.1 2.4 %collective-permute-start.5 = (f32[128,128]{1,0:T(8,128)S(1)}, f32[128,128]{1,0:T(8,128)S(1)}, u32[]{:S(2)}, u32[]{:S(2)}) collective-permute-start(f32[128,128]{1,0:T(8,128)S(1)} %add.6), channel_id=1, source_target_pairs={{0,4},{1,5},{2,6},{3,7},{4,0},{5,1},{6,2},{7,3},{8,12},{9,13},{10,... | collective-permute-start | bytes 196616 | tf_op jit(solution)/shard_map/coupled_over_tp/ppermute | solution.py:246
  43.5 0.0 copy-done.8
  43.5 0.1 copy.10.lat_ref
  43.6 5.1 %collective-permute-done.5 = f32[128,128]{1,0:T(8,128)S(1)} collective-permute-done((f32[128,128]{1,0:T(8,128)S(1)}, f32[128,128]{1,0:T(8,128)S(1)}, u32[]{:S(2)}, u32[]{:S(2)}) %collective-permute-start.5) | collective-permute-done | bytes 65568 | tf_op jit(solution)/shard_map/coupled_over_tp/ppermute | solution.py:246
  48.7 0.0 copy-start.1
  48.7 0.0 copy-start.3
  48.8 6.1 %collective-permute-start.6 = (f32[128,128]{1,0:T(8,128)S(1)}, f32[128,128]{1,0:T(8,128)S(1)}, u32[]{:S(2)}, u32[]{:S(2)}) collective-permute-start(f32[128,128]{1,0:T(8,128)S(1)} %add.7.acc_ref), channel_id=1, source_target_pairs={{0,1},{1,0},{2,3},{3,2},{4,5},{5,4},{6,7},{7,6},{8,9},{9,8},{10,11... | collective-permute-start | bytes 196616 | tf_op jit(solution)/shard_map/coupled_over_tp/ppermute | solution.py:246
  54.8 0.0 collective-permute-done.3.kvb_ref
  54.8 0.0 all-to-all-done.qg_ref
  54.9 1.9 %stats.1.st_ref = bf16[48,128]{1,0:T(8,128)(2,1)S(1)} custom-call(bf16[8,144,256]{2,1,0:T(8,128)(2,1)S(1)} %all-to-all-done.qg_ref, bf16[4,272,256]{2,1,0:T(8,128)(2,1)S(1)} %pad_maximum_fusion.kva_ref, bf16[4,272,256]{2,1,0:T(8,128)(2,1)S(1)} %collective-permute-done.3.kvb_ref), custom_call_target="tpu_custom_call" | custom-call | flops 1000000000 | bytes 2097152 | tf_op jit(solution)/shard_map/stats/pallas_call | solution.py:232
  56.8 2.9 %collective-permute-done.6.recv_ref = f32[128,128]{1,0:T(8,128)S(1)} collective-permute-done((f32[128,128]{1,0:T(8,128)S(1)}, f32[128,128]{1,0:T(8,128)S(1)}, u32[]{:S(2)}, u32[]{:S(2)}) %collective-permute-start.6) | collective-permute-done | bytes 65568 | tf_op jit(solution)/shard_map/coupled_over_tp/ppermute | solution.py:246
  59.7 0.0 copy-done.1
  59.7 0.0 copy-done.3
  59.7 0.4 pack.1
  60.1 18.8 %all_to_all.15.g_ref = bf16[8,192,128]{2,1,0:T(8,128)(2,1)S(1)} all-to-all(bf16[8,192,128]{2,1,0:T(8,128)(2,1)S(1)} %pack.1), channel_id=1, replica_groups=mesh['y'=4,'z'=8,'c'=2,'tp'=8] {'z'}, dimensions={0} | all-to-all | bytes 786432 | tf_op jit(solution)/shard_map/upstream_over_z/all_to_all | solution.py:283
  78.9 5.1 %main.1 = (bf16[8,128,256]{2,1,0:T(8,128)(2,1)}, bf16[4,256,256]{2,1,0:T(8,128)(2,1)S(1)}, bf16[4,256,256]{2,1,0:T(8,128)(2,1)S(1)}) custom-call(bf16[8,144,256]{2,1,0:T(8,128)(2,1)S(1)} %all-to-all-done.qg_ref, bf16[4,272,256]{2,1,0:T(8,128)(2,1)S(1)} %pad_maximum_fusion.kva_ref, bf16[4,272,256]{2,1,0:T(8,128)(2,1)S(1)} %collective-permute-done.3.kvb_ref, ...), custom_call_target="tpu_custom_call" | custom-call | flops 4000000000 | bytes 2097152 | tf_op jit(solution)/shard_map/main/pallas_call | solution.py:232
  83.9 3.5 %all-to-all-start.2 = ((bf16[8,128,256]{2,1,0:T(8,128)(2,1)}), bf16[8,128,256]{2,1,0:T(8,128)(2,1)S(1)}, u32[]{:S(2)}, u32[]{:S(2)}) async-start(bf16[8,128,256]{2,1,0:T(8,128)(2,1)} %get-tuple-element.22), calls=%async_computation.2 | async-start | bytes 1048576 | tf_op jit(solution)/shard_map/dq_over_z/all_to_all | solution.py:299
  87.4 1.9 %collective-permute-start.7 = (bf16[4,256,256]{2,1,0:T(8,128)(2,1)S(1)}, bf16[4,256,256]{2,1,0:T(8,128)(2,1)S(1)}, u32[]{:S(2)}, u32[]{:S(2)}) collective-permute-start(bf16[4,256,256]{2,1,0:T(8,128)(2,1)S(1)} %get-tuple-element.17), channel_id=1, source_target_pairs={{0,8},{8,0},{1,9},{9,1},{2,10},{10,2},{3,11},{11,3},{4,12},{12,4},... | collective-permute-start | bytes 1572872 | tf_op jit(solution)/shard_map/dkv_over_core/ppermute | solution.py:246
  89.4 1.9 %collective-permute-done.7.recv_ref = bf16[4,256,256]{2,1,0:T(8,128)(2,1)S(1)} collective-permute-done((bf16[4,256,256]{2,1,0:T(8,128)(2,1)S(1)}, bf16[4,256,256]{2,1,0:T(8,128)(2,1)S(1)}, u32[]{:S(2)}, u32[]{:S(2)}) %collective-permute-start.7) | collective-permute-done | bytes 524320 | tf_op jit(solution)/shard_map/dkv_over_core/ppermute | solution.py:246
  91.3 0.1 dkv_over_core.1
  91.4 4.1 %collective-permute-start.8 = (bf16[256,256]{1,0:T(8,128)(2,1)S(1)}, bf16[256,256]{1,0:T(8,128)(2,1)S(1)}, u32[]{:S(2)}, u32[]{:S(2)}) collective-permute-start(bf16[256,256]{1,0:T(8,128)(2,1)S(1)} %get-tuple-element.19), channel_id=1, source_target_pairs={{0,128},{128,0},{256,384},{384,256},{1,129},{129,1},{257,385},{385... | collective-permute-start | bytes 393224 | tf_op jit(solution)/shard_map/dkv_over_y/ppermute | solution.py:246
  95.5 2.6 %collective-permute-start.9 = (bf16[256,256]{1,0:T(8,128)(2,1)S(1)}, bf16[256,256]{1,0:T(8,128)(2,1)S(1)}, u32[]{:S(2)}, u32[]{:S(2)}) collective-permute-start(bf16[256,256]{1,0:T(8,128)(2,1)S(1)} %get-tuple-element.20), channel_id=1, source_target_pairs={{0,256},{128,384},{256,0},{384,128},{1,257},{129,385},{257,1},{385... | collective-permute-start | bytes 393224 | tf_op jit(solution)/shard_map/dkv_over_y/ppermute | solution.py:246
  98.1 2.7 %collective-permute-start.10 = (bf16[256,256]{1,0:T(8,128)(2,1)S(1)}, bf16[256,256]{1,0:T(8,128)(2,1)S(1)}, u32[]{:S(2)}, u32[]{:S(2)}) collective-permute-start(bf16[256,256]{1,0:T(8,128)(2,1)S(1)} %get-tuple-element.21), channel_id=1, source_target_pairs={{0,384},{128,256},{256,128},{384,0},{1,385},{129,257},{257,129},{3... | collective-permute-start | bytes 393224 | tf_op jit(solution)/shard_map/dkv_over_y/ppermute | solution.py:246
  100.8 0.0 collective-permute-done.8.r1_ref
  100.8 6.7 %collective-permute-done.9.r2_ref = bf16[256,256]{1,0:T(8,128)(2,1)S(1)} collective-permute-done((bf16[256,256]{1,0:T(8,128)(2,1)S(1)}, bf16[256,256]{1,0:T(8,128)(2,1)S(1)}, u32[]{:S(2)}, u32[]{:S(2)}) %collective-permute-start.9) | collective-permute-done | bytes 131104 | tf_op jit(solution)/shard_map/dkv_over_y/ppermute | solution.py:246
  107.5 3.3 %collective-permute-done.10.r3_ref = bf16[256,256]{1,0:T(8,128)(2,1)S(1)} collective-permute-done((bf16[256,256]{1,0:T(8,128)(2,1)S(1)}, bf16[256,256]{1,0:T(8,128)(2,1)S(1)}, u32[]{:S(2)}, u32[]{:S(2)}) %collective-permute-start.10) | collective-permute-done | bytes 131104 | tf_op jit(solution)/shard_map/dkv_over_y/ppermute | solution.py:246
  110.8 0.0 all-to-all-done.2.dq_ref
  110.8 0.8 final.1
  (2 shorter events, 0.0 us)
Async XLA Ops:
  0.6 0.8 copy-start
  1.5 0.8 copy-start.2
  2.3 0.8 copy-start.4
  3.2 0.8 copy-start.5
  4.0 0.8 copy-start.6
  4.8 0.7 copy-start.7
  6.9 47.9 %all-to-all-start = ((bf16[8,144,256]{2,1,0:T(8,128)(2,1)}), bf16[8,144,256]{2,1,0:T(8,128)(2,1)S(1)}, u32[]{:S(2)}, u32[]{:S(2)}) async-start(bf16[8,144,256]{2,1,0:T(8,128)(2,1)} %get-tuple-element.13), calls=%async_computation | async-start | bytes 1179648 | tf_op jit(solution)/shard_map/q_over_z/all_to_all | solution.py:267
  17.3 14.0 %collective-permute-start.2 = (bf16[272,256]{1,0:T(8,128)(2,1)S(1)}, bf16[272,256]{1,0:T(8,128)(2,1)S(1)}, u32[]{:S(2)}, u32[]{:S(2)}) collective-permute-start(bf16[272,256]{1,0:T(8,128)(2,1)S(1)} %get-tuple-element.14), channel_id=1, source_target_pairs={{0,384},{128,256},{256,128},{384,0},{1,385},{129,257},{257,129},{3... | collective-permute-start | bytes 417800 | tf_op jit(solution)/shard_map/kv_over_y/ppermute | solution.py:246
  20.7 11.6 %collective-permute-start.1 = (bf16[272,256]{1,0:T(8,128)(2,1)S(1)}, bf16[272,256]{1,0:T(8,128)(2,1)S(1)}, u32[]{:S(2)}, u32[]{:S(2)}) collective-permute-start(bf16[272,256]{1,0:T(8,128)(2,1)S(1)} %get-tuple-element.14), channel_id=1, source_target_pairs={{0,256},{128,384},{256,0},{384,128},{1,257},{129,385},{257,1},{385... | collective-permute-start | bytes 417800 | tf_op jit(solution)/shard_map/kv_over_y/ppermute | solution.py:246
  23.9 8.7 %collective-permute-start = (bf16[272,256]{1,0:T(8,128)(2,1)S(1)}, bf16[272,256]{1,0:T(8,128)(2,1)S(1)}, u32[]{:S(2)}, u32[]{:S(2)}) collective-permute-start(bf16[272,256]{1,0:T(8,128)(2,1)S(1)} %get-tuple-element.14), channel_id=1, source_target_pairs={{0,128},{128,0},{256,384},{384,256},{1,129},{129,1},{257,385},{385... | collective-permute-start | bytes 417800 | tf_op jit(solution)/shard_map/kv_over_y/ppermute | solution.py:246
  32.7 22.1 %collective-permute-start.3 = (bf16[4,272,256]{2,1,0:T(8,128)(2,1)S(1)}, bf16[4,272,256]{2,1,0:T(8,128)(2,1)S(1)}, u32[]{:S(2)}, u32[]{:S(2)}) collective-permute-start(bf16[4,272,256]{2,1,0:T(8,128)(2,1)S(1)} %pad_maximum_fusion.kva_ref), channel_id=1, source_target_pairs={{0,8},{8,0},{1,9},{9,1},{2,10},{10,2},{3,11},{11,3},{4,12},{12,4},... | collective-permute-start | bytes 1671176 | tf_op jit(solution)/shard_map/kv_over_core/ppermute | solution.py:246
  34.6 8.8 %copy-start.8 = (f32[128,64]{0,1:T(8,128)S(1)}, f32[128,64]{0,1:T(8,128)}, u32[]{:S(2)}) copy-start(f32[128,64]{0,1:T(8,128)} %param.7) | copy-start | bytes 98308
  34.6 6.4 %collective-permute-start.4 = (f32[128,128]{1,0:T(8,128)S(1)}, f32[128,128]{1,0:T(8,128)S(1)}, u32[]{:S(2)}, u32[]{:S(2)}) collective-permute-start(f32[128,128]{1,0:T(8,128)S(1)} %get-tuple-element.15), channel_id=1, source_target_pairs={{0,2},{1,3},{2,0},{3,1},{4,6},{5,7},{6,4},{7,5},{8,10},{9,11},{10,... | collective-permute-start | bytes 196616 | tf_op jit(solution)/shard_map/coupled_over_tp/ppermute | solution.py:246
  41.1 7.7 %collective-permute-start.5 = (f32[128,128]{1,0:T(8,128)S(1)}, f32[128,128]{1,0:T(8,128)S(1)}, u32[]{:S(2)}, u32[]{:S(2)}) collective-permute-start(f32[128,128]{1,0:T(8,128)S(1)} %add.6), channel_id=1, source_target_pairs={{0,4},{1,5},{2,6},{3,7},{4,0},{5,1},{6,2},{7,3},{8,12},{9,13},{10,... | collective-permute-start | bytes 196616 | tf_op jit(solution)/shard_map/coupled_over_tp/ppermute | solution.py:246
  48.7 10.9 %copy-start.1 = (bf16[128,256]{1,0:T(8,128)(2,1)S(1)}, bf16[128,256]{1,0:T(8,128)(2,1)}, u32[]{:S(2)}) copy-start(bf16[128,256]{1,0:T(8,128)(2,1)} %o_ref.3) | copy-start | bytes 196612
  48.7 10.9 %copy-start.3 = (bf16[256,128]{1,0:T(8,128)(2,1)S(1)}, bf16[256,128]{1,0:T(8,128)(2,1)}, u32[]{:S(2)}) copy-start(bf16[256,128]{1,0:T(8,128)(2,1)} %proj_ref.5) | copy-start | bytes 196612
  48.8 10.9 %collective-permute-start.6 = (f32[128,128]{1,0:T(8,128)S(1)}, f32[128,128]{1,0:T(8,128)S(1)}, u32[]{:S(2)}, u32[]{:S(2)}) collective-permute-start(f32[128,128]{1,0:T(8,128)S(1)} %add.7.acc_ref), channel_id=1, source_target_pairs={{0,1},{1,0},{2,3},{3,2},{4,5},{5,4},{6,7},{7,6},{8,9},{9,8},{10,11... | collective-permute-start | bytes 196616 | tf_op jit(solution)/shard_map/coupled_over_tp/ppermute | solution.py:246
  83.9 26.8 %all-to-all-start.2 = ((bf16[8,128,256]{2,1,0:T(8,128)(2,1)}), bf16[8,128,256]{2,1,0:T(8,128)(2,1)S(1)}, u32[]{:S(2)}, u32[]{:S(2)}) async-start(bf16[8,128,256]{2,1,0:T(8,128)(2,1)} %get-tuple-element.22), calls=%async_computation.2 | async-start | bytes 1048576 | tf_op jit(solution)/shard_map/dq_over_z/all_to_all | solution.py:299
  87.4 3.8 %collective-permute-start.7 = (bf16[4,256,256]{2,1,0:T(8,128)(2,1)S(1)}, bf16[4,256,256]{2,1,0:T(8,128)(2,1)S(1)}, u32[]{:S(2)}, u32[]{:S(2)}) collective-permute-start(bf16[4,256,256]{2,1,0:T(8,128)(2,1)S(1)} %get-tuple-element.17), channel_id=1, source_target_pairs={{0,8},{8,0},{1,9},{9,1},{2,10},{10,2},{3,11},{11,3},{4,12},{12,4},... | collective-permute-start | bytes 1572872 | tf_op jit(solution)/shard_map/dkv_over_core/ppermute | solution.py:246
  91.4 9.4 %collective-permute-start.8 = (bf16[256,256]{1,0:T(8,128)(2,1)S(1)}, bf16[256,256]{1,0:T(8,128)(2,1)S(1)}, u32[]{:S(2)}, u32[]{:S(2)}) collective-permute-start(bf16[256,256]{1,0:T(8,128)(2,1)S(1)} %get-tuple-element.19), channel_id=1, source_target_pairs={{0,128},{128,0},{256,384},{384,256},{1,129},{129,1},{257,385},{385... | collective-permute-start | bytes 393224 | tf_op jit(solution)/shard_map/dkv_over_y/ppermute | solution.py:246
  95.5 12.1 %collective-permute-start.9 = (bf16[256,256]{1,0:T(8,128)(2,1)S(1)}, bf16[256,256]{1,0:T(8,128)(2,1)S(1)}, u32[]{:S(2)}, u32[]{:S(2)}) collective-permute-start(bf16[256,256]{1,0:T(8,128)(2,1)S(1)} %get-tuple-element.20), channel_id=1, source_target_pairs={{0,256},{128,384},{256,0},{384,128},{1,257},{129,385},{257,1},{385... | collective-permute-start | bytes 393224 | tf_op jit(solution)/shard_map/dkv_over_y/ppermute | solution.py:246
  98.1 12.7 %collective-permute-start.10 = (bf16[256,256]{1,0:T(8,128)(2,1)S(1)}, bf16[256,256]{1,0:T(8,128)(2,1)S(1)}, u32[]{:S(2)}, u32[]{:S(2)}) collective-permute-start(bf16[256,256]{1,0:T(8,128)(2,1)S(1)} %get-tuple-element.21), channel_id=1, source_target_pairs={{0,384},{128,256},{256,128},{384,0},{1,385},{129,257},{257,129},{3... | collective-permute-start | bytes 393224 | tf_op jit(solution)/shard_map/dkv_over_y/ppermute | solution.py:246

commit v2 on v1

--- a/solution.py
+++ b/solution.py
@@ -18,6 +18,8 @@
 BF16 = jnp.bfloat16
 NT = (((1,), (1,)), ((), ()))
 MIB = 1 << 20
+JOIN_COST = 1_000_000
+FOLD_COST = 20_000_000_000
 
 
 def dot_nt(a, b):
@@ -28,16 +30,29 @@
     return jnp.dot(a, b, preferred_element_type=F32)
 
 
-def prep_kernel(pos_ref, q_ref, k_ref, v_ref, o_ref, proj_ref, qpay_ref, kvpay_ref, part_ref):
+def prep_kernel(
+    pos_ref, q_hbm, k_hbm, v_hbm, o_hbm, proj_hbm, qpay_ref, kvpay_ref, part_ref, *scratch
+):
+    buffers, sems = scratch[:-1], scratch[-1]
+    sources = (k_hbm, v_hbm, q_hbm, o_hbm, proj_hbm)
+    copies = [
+        pltpu.make_async_copy(src, dst, sems.at[n])
+        for n, (src, dst) in enumerate(zip(sources, buffers))
+    ]
+    for copy in copies:
+        copy.start()
+    k_ref, v_ref, q_ref, o_ref, proj_ref = buffers
     block = lax.shift_right_logical(pos_ref[0], 6).astype(F32)
     tag = jnp.full((16, 256), block, F32).astype(BF16)
-    q = q_ref[...]
+    for copy in copies:
+        copy.wait()
+    k, v, q = k_ref[...], v_ref[...], q_ref[...]
+    kvpay_ref[0:128, :] = k
+    kvpay_ref[128:256, :] = v
+    kvpay_ref[256:272, :] = tag
     for i in range(NZ):
         qpay_ref[i, 0:128, :] = q
         qpay_ref[i, 128:144, :] = tag
-    kvpay_ref[0:128, :] = k_ref[...]
-    kvpay_ref[128:256, :] = v_ref[...]
-    kvpay_ref[256:272, :] = tag
     part_ref[...] = dot(o_ref[...], proj_ref[...])
 
 
@@ -108,12 +123,18 @@
     out_ref[...] = st_ref[...].astype(BF16)
 
 
-def pack_kernel(acc_ref, recv_ref, lat_ref, proj_ref, o_ref, st_ref, out_ref, d_ref):
-    coupled = acc_ref[...] + recv_ref[...]
+def join_kernel(own_ref, r1_ref, r2_ref, r3_ref, total_ref, recv_ref, kv_ref, sum_ref):
+    for n, ref in enumerate((own_ref, r1_ref, r2_ref, r3_ref)):
+        kv_ref[n] = ref[...]
+    sum_ref[...] = total_ref[...] + recv_ref[...]
+
+
+def pack_kernel(total_ref, recv_ref, lat_ref, proj_ref, o_ref, st_ref, out_ref, d_ref):
+    coupled = total_ref[...] + recv_ref[...]
     shifts = coupled[:, 0:64]
     log_scale = coupled[:, 64:128]
     damping = jnp.exp(-log_scale)
-    normed = (lat_ref[...] - shifts) * damping
+    normed = (lat_ref[...].T - shifts) * damping
     upstream = jnp.concatenate([-normed * damping, 1.0 - normed * normed], axis=1).astype(BF16)
     d_ref[...] = jnp.zeros((16, 128), F32)
     for head in range(2):
@@ -222,17 +243,14 @@
     qo_ref[...] = dq.astype(BF16)
 
 
-def call(kernel, outs, cost, scratch=(), smem=0, limit=48):
+def call(kernel, outs, cost, scratch=(), specs=None, limit=48):
     vmem = pl.BlockSpec(memory_space=pltpu.VMEM)
 
     def run(*args):
-        specs = [vmem] * len(args)
-        if smem:
-            specs[0] = pl.BlockSpec(memory_space=pltpu.SMEM)
         return pl.pallas_call(
             kernel,
             out_shape=[jax.ShapeDtypeStruct(s, d) for s, d in outs],
-            in_specs=specs,
+            in_specs=specs or [vmem] * len(args),
             out_specs=[vmem] * len(outs),
             scratch_shapes=list(scratch),
             compiler_params=pltpu.CompilerParams(vmem_limit_bytes=limit * MIB),
@@ -246,27 +264,32 @@
     return lax.ppermute(x, axis, [(i, i ^ k) for i in range(size)])
 
 
-def local(n_tp, latent, positions, queries, keys, values, attention_out, projection):
+def local(n_x, n_h, latent, positions, queries, keys, values, attention_out, projection):
     with jax.named_scope("prep"):
         qpay, kvpay, total = call(
             prep_kernel,
             [((NZ, 144, 256), BF16), ((272, 256), BF16), ((128, 128), F32)],
             10_000_000,
-            smem=1,
+            [pltpu.VMEM((128, 256), BF16)] * 4
+            + [pltpu.VMEM((256, 128), BF16), pltpu.SemaphoreType.DMA((5,))],
+            [pl.BlockSpec(memory_space=pltpu.SMEM)] + [pl.BlockSpec(memory_space=pltpu.HBM)] * 5,
+            limit=62,
         )(positions, queries, keys, values, attention_out, projection)
     with jax.named_scope("kv_over_y"):
         arrived = [swap(kvpay, "y", NY, k) for k in (1, 2, 3)]
-    rounds = [k for k in (2, 4, 1) if k < n_tp]
-    extra = jnp.zeros_like(total)
-    for n, k in enumerate(rounds):
-        with jax.named_scope("coupled_over_tp"):
-            extra = swap(total, "tp", n_tp, k)
-            if n < len(rounds) - 1:
-                total = total + extra
+    with jax.named_scope("coupled_over_h"):
+        total = total + swap(total, "h", n_h, 1) if n_h > 1 else total
+    with jax.named_scope("coupled_over_x"):
+        first = swap(total, "x", n_x, 1) if n_x > 1 else jnp.zeros_like(total)
     with jax.named_scope("q_over_z"):
         qg = lax.all_to_all(qpay, "z", 0, 0)
+    with jax.named_scope("join"):
+        kva, total = call(
+            join_kernel, [((NY, 272, 256), BF16), ((128, 128), F32)], JOIN_COST
+        )(kvpay, *arrived, total, first)
+    with jax.named_scope("coupled_over_x"):
+        second = swap(total, "x", n_x, 2) if n_x > 1 else jnp.zeros_like(total)
     with jax.named_scope("kv_over_core"):
-        kva = jnp.stack([kvpay] + arrived)
         kvb = swap(kva, "c", NC, 1)
     with jax.named_scope("stats"):
         (stats,) = call(
@@ -278,7 +301,7 @@
     with jax.named_scope("pack"):
         (pay,) = call(
             pack_kernel, [((NZ, 192, 128), BF16)], 10_000_000, [pltpu.VMEM((16, 128), F32)]
-        )(total, extra, latent, projection, attention_out, stats)
+        )(total, second, latent.T, projection, attention_out, stats)
     with jax.named_scope("upstream_over_z"):
         gathered = lax.all_to_all(pay, "z", 0, 0)
     with jax.named_scope("main"):
@@ -290,9 +313,9 @@
         )(qg, kva, kvb, gathered, projection)
     with jax.named_scope("dkv_over_core"):
         other = swap(db, "c", NC, 1)
-        own, *send = call(fold_kernel, [((256, 256), F32)] + [((256, 256), BF16)] * 3, 1_000_000)(
-            da, other
-        )
+        own, *send = call(
+            fold_kernel, [((256, 256), F32)] + [((256, 256), BF16)] * 3, FOLD_COST
+        )(da, other)
     with jax.named_scope("dkv_over_y"):
         back = [swap(s, "y", NY, k) for k, s in zip((1, 2, 3), send)]
     with jax.named_scope("dq_over_z"):
@@ -304,22 +327,24 @@
 
 
 def solution(mesh):
-    n_tp = mesh.shape["tp"]
-    fine = Mesh(mesh.devices.reshape(NY, NZ, NC, n_tp), ("y", "z", "c", "tp"))
+    n_h = min(2, mesh.shape["tp"])
+    n_x = mesh.shape["tp"] // n_h
+    fine = Mesh(mesh.devices.reshape(NY, NZ, NC, n_x, n_h), ("y", "z", "c", "x", "h"))
     ctx = ("y", "z", "c")
+    tp = ("x", "h")
     placed = (
         P(ctx, None),
         P(ctx),
-        P(ctx, "tp"),
-        P(ctx, "tp"),
-        P(ctx, "tp"),
-        P(ctx, "tp"),
-        P("tp", None),
+        P(ctx, tp),
+        P(ctx, tp),
+        P(ctx, tp),
+        P(ctx, tp),
+        P(tp, None),
     )
     return jax.shard_map(
-        functools.partial(local, n_tp),
+        functools.partial(local, n_x, n_h),
         mesh=fine,
         in_specs=placed,
-        out_specs=(P(ctx, "tp"), P(ctx, "tp"), P(ctx, "tp")),
+        out_specs=(P(ctx, tp), P(ctx, tp), P(ctx, tp)),
         check_vma=False,
     )

time: 112 us -> 106 us (0.946)
  the two profiles are of different devices: /device:TPU:12 before, /device:TPU:1 now
where the time goes in v2:
time: 106 us; the launch traced here: 105 us
  starting transfers between devices  60 us (57%)
  blocking collectives  20 us (19%)
  waiting for transfers between devices  12.7 us (12%)
  Pallas kernels  11 us (10%)
    ppermute x11, starting transfers between devices, swap(): return lax.ppermute(x, axis, [(i, i ^ k) for i in range(size)])  45.5 us
    all_to_all x1, blocking collectives, local(): gathered = lax.all_to_all(pay, 'z', 0, 0)  20 us
    ppermute x11, waiting for transfers between devices, swap(): return lax.ppermute(x, axis, [(i, i ^ k) for i in range(size)])  12.6 us
    all_to_all x1, starting transfers between devices, local(): qg = lax.all_to_all(qpay, 'z', 0, 0)  11 us
    pallas_call x7, Pallas kernels, run(): pl.pallas_call(kernel, out_shape=[jax.ShapeDtypeStruct(s, d) for s, d in...  11 us
    all_to_all x1, starting transfers between devices, local(): dqs = lax.all_to_all(dq, 'z', 0, 0)  3.5 us
  transfers between devices with their start and end apart: 13, of which 4 were waited for; matrix products, arithmetic and copies ran while one was open for 0% of the time, Pallas kernels for 2%

profile of v2, /device:TPU:1, one launch (start us, length us, event | category | flops | bytes accessed | tf_op | source)
XLA Modules:
  0.0 104.6 jit_solution(17909206380703091873)
XLA Ops:
  0.6 2.6 %prep.1 = (bf16[8,144,256]{2,1,0:T(8,128)(2,1)}, bf16[272,256]{1,0:T(8,128)(2,1)}, f32[128,128]{1,0:T(8,128)}) custom-call(s32[128]{0:T(128)} %pos_ref.1, bf16[128,256]{1,0:T(8,128)(2,1)} %q_hbm.1, bf16[128,256]{1,0:T(8,128)(2,1)} %k_hbm.1, bf16[128,256]{1,0:T(8,128)(2,1)} %v_hbm.1, bf16[128,256]{1,0:T(8,128)(2,1)} %o_ref.1, bf16[256,128]{1,0:T(8,128)(2,1)} %proj_ref.3), custom_call_target="tpu_custom_call" | custom-call | flops 10000000 | bytes 2097152 | tf_op jit(solution)/shard_map/prep/pallas_call | solution.py:250
  3.2 0.0 copy-start.2
  3.2 0.0 copy-start.4
  3.2 11.0 %all-to-all-start = ((bf16[8,144,256]{2,1,0:T(8,128)(2,1)}), bf16[8,144,256]{2,1,0:T(8,128)(2,1)S(1)}, u32[]{:S(2)}, u32[]{:S(2)}) async-start(bf16[8,144,256]{2,1,0:T(8,128)(2,1)} %get-tuple-element.15), calls=%async_computation | async-start | bytes 1179648 | tf_op jit(solution)/shard_map/q_over_z/all_to_all | solution.py:285
  14.2 0.0 copy-done.2
  14.2 5.2 %collective-permute-start.2 = (bf16[272,256]{1,0:T(8,128)(2,1)S(1)}, bf16[272,256]{1,0:T(8,128)(2,1)S(1)}, u32[]{:S(2)}, u32[]{:S(2)}) collective-permute-start(bf16[272,256]{1,0:T(8,128)(2,1)S(1)} %copy-done.2), channel_id=1, source_target_pairs={{0,384},{128,256},{256,128},{384,0},{1,385},{129,257},{257,129},{3... | collective-permute-start | bytes 417800 | tf_op jit(solution)/shard_map/kv_over_y/ppermute | solution.py:264
  19.5 1.9 %collective-permute-start.1 = (bf16[272,256]{1,0:T(8,128)(2,1)S(1)}, bf16[272,256]{1,0:T(8,128)(2,1)S(1)}, u32[]{:S(2)}, u32[]{:S(2)}) collective-permute-start(bf16[272,256]{1,0:T(8,128)(2,1)S(1)} %copy-done.2), channel_id=1, source_target_pairs={{0,256},{128,384},{256,0},{384,128},{1,257},{129,385},{257,1},{385... | collective-permute-start | bytes 417800 | tf_op jit(solution)/shard_map/kv_over_y/ppermute | solution.py:264
  21.4 2.2 %collective-permute-start = (bf16[272,256]{1,0:T(8,128)(2,1)S(1)}, bf16[272,256]{1,0:T(8,128)(2,1)S(1)}, u32[]{:S(2)}, u32[]{:S(2)}) collective-permute-start(bf16[272,256]{1,0:T(8,128)(2,1)S(1)} %copy-done.2), channel_id=1, source_target_pairs={{0,128},{128,0},{256,384},{384,256},{1,129},{129,1},{257,385},{385... | collective-permute-start | bytes 417800 | tf_op jit(solution)/shard_map/kv_over_y/ppermute | solution.py:264
  23.6 0.0 copy-done.4
  23.6 7.4 %collective-permute-start.3 = (f32[128,128]{1,0:T(8,128)S(1)}, f32[128,128]{1,0:T(8,128)S(1)}, u32[]{:S(2)}, u32[]{:S(2)}) collective-permute-start(f32[128,128]{1,0:T(8,128)S(1)} %copy-done.4), channel_id=1, source_target_pairs={{0,1},{1,0},{2,3},{3,2},{4,5},{5,4},{6,7},{7,6},{8,9},{9,8},{10,11... | collective-permute-start | bytes 196616 | tf_op jit(solution)/shard_map/coupled_over_h/ppermute | solution.py:264
  31.0 2.6 %collective-permute-done.3 = f32[128,128]{1,0:T(8,128)S(1)} collective-permute-done((f32[128,128]{1,0:T(8,128)S(1)}, f32[128,128]{1,0:T(8,128)S(1)}, u32[]{:S(2)}, u32[]{:S(2)}) %collective-permute-start.3) | collective-permute-done | bytes 65568 | tf_op jit(solution)/shard_map/coupled_over_h/ppermute | solution.py:264
  33.6 3.1 %collective-permute-start.4 = (f32[128,128]{1,0:T(8,128)S(1)}, f32[128,128]{1,0:T(8,128)S(1)}, u32[]{:S(2)}, u32[]{:S(2)}) collective-permute-start(f32[128,128]{1,0:T(8,128)S(1)} %add.3.total_ref), channel_id=1, source_target_pairs={{0,2},{2,0},{4,6},{6,4},{1,3},{3,1},{5,7},{7,5},{8,10},{10,8},{12,... | collective-permute-start | bytes 196616 | tf_op jit(solution)/shard_map/coupled_over_x/ppermute | solution.py:264
  36.7 1.9 %collective-permute-done.4.recv_ref = f32[128,128]{1,0:T(8,128)S(1)} collective-permute-done((f32[128,128]{1,0:T(8,128)S(1)}, f32[128,128]{1,0:T(8,128)S(1)}, u32[]{:S(2)}, u32[]{:S(2)}) %collective-permute-start.4) | collective-permute-done | bytes 65568 | tf_op jit(solution)/shard_map/coupled_over_x/ppermute | solution.py:264
  38.6 0.0 collective-permute-done.2.r3_ref
  38.6 0.0 collective-permute-done.1.r2_ref
  38.6 0.0 collective-permute-done.r1_ref
  38.7 5.1 %collective-permute-start.5 = (bf16[4,272,256]{2,1,0:T(8,128)(2,1)S(1)}, bf16[4,272,256]{2,1,0:T(8,128)(2,1)S(1)}, u32[]{:S(2)}, u32[]{:S(2)}) collective-permute-start(bf16[4,272,256]{2,1,0:T(8,128)(2,1)S(1)} %get-tuple-element.18.kva_ref), channel_id=1, source_target_pairs={{0,8},{8,0},{1,9},{9,1},{2,10},{10,2},{3,11},{11,3},{4,12},{12,4},... | collective-permute-start | bytes 1671176 | tf_op jit(solution)/shard_map/kv_over_core/ppermute | solution.py:264
  43.8 0.0 copy-start
  43.8 0.0 copy-start.1
  43.8 0.0 copy-start.3
  43.8 4.8 %collective-permute-start.6 = (f32[128,128]{1,0:T(8,128)S(1)}, f32[128,128]{1,0:T(8,128)S(1)}, u32[]{:S(2)}, u32[]{:S(2)}) collective-permute-start(f32[128,128]{1,0:T(8,128)S(1)} %get-tuple-element.19.total_ref), channel_id=1, source_target_pairs={{0,4},{2,6},{4,0},{6,2},{1,5},{3,7},{5,1},{7,3},{8,12},{10,14},{12... | collective-permute-start | bytes 196616 | tf_op jit(solution)/shard_map/coupled_over_x/ppermute | solution.py:264
  48.6 0.0 collective-permute-done.5.kvb_ref
  48.6 0.0 all-to-all-done.qg_ref
  48.6 1.9 %stats.1.st_ref = bf16[48,128]{1,0:T(8,128)(2,1)S(1)} custom-call(bf16[8,144,256]{2,1,0:T(8,128)(2,1)S(1)} %all-to-all-done.qg_ref, bf16[4,272,256]{2,1,0:T(8,128)(2,1)S(1)} %get-tuple-element.18.kva_ref, bf16[4,272,256]{2,1,0:T(8,128)(2,1)S(1)} %collective-permute-done.5.kvb_ref), custom_call_target="tpu_custom_call" | custom-call | flops 1000000000 | bytes 2097152 | tf_op jit(solution)/shard_map/stats/pallas_call | solution.py:250
  50.6 0.5 collective-permute-done.6.recv_ref
  51.1 0.0 copy-done
  51.1 0.0 copy-done.1
  51.1 0.0 copy-done.3
  51.1 0.4 pack.1
  51.5 20.0 %all_to_all.15.g_ref = bf16[8,192,128]{2,1,0:T(8,128)(2,1)S(1)} all-to-all(bf16[8,192,128]{2,1,0:T(8,128)(2,1)S(1)} %pack.1), channel_id=1, replica_groups=mesh['y'=4,'z'=8,'c'=2,'x'=4,'h'=2] {'z'}, dimensions={0} | all-to-all | bytes 786432 | tf_op jit(solution)/shard_map/upstream_over_z/all_to_all | solution.py:306
  71.5 5.1 %main.1 = (bf16[8,128,256]{2,1,0:T(8,128)(2,1)}, bf16[4,256,256]{2,1,0:T(8,128)(2,1)S(1)}, bf16[4,256,256]{2,1,0:T(8,128)(2,1)S(1)}) custom-call(bf16[8,144,256]{2,1,0:T(8,128)(2,1)S(1)} %all-to-all-done.qg_ref, bf16[4,272,256]{2,1,0:T(8,128)(2,1)S(1)} %get-tuple-element.18.kva_ref, bf16[4,272,256]{2,1,0:T(8,128)(2,1)S(1)} %collective-permute-done.5.kvb_ref, ...), custom_call_target="tpu_custom_call" | custom-call | flops 4000000000 | bytes 2097152 | tf_op jit(solution)/shard_map/main/pallas_call | solution.py:250
  76.7 4.1 %collective-permute-start.7 = (bf16[4,256,256]{2,1,0:T(8,128)(2,1)S(1)}, bf16[4,256,256]{2,1,0:T(8,128)(2,1)S(1)}, u32[]{:S(2)}, u32[]{:S(2)}) collective-permute-start(bf16[4,256,256]{2,1,0:T(8,128)(2,1)S(1)} %get-tuple-element.21), channel_id=1, source_target_pairs={{0,8},{8,0},{1,9},{9,1},{2,10},{10,2},{3,11},{11,3},{4,12},{12,4},... | collective-permute-start | bytes 1572872 | tf_op jit(solution)/shard_map/dkv_over_core/ppermute | solution.py:264
  80.8 3.5 %all-to-all-start.2 = ((bf16[8,128,256]{2,1,0:T(8,128)(2,1)}), bf16[8,128,256]{2,1,0:T(8,128)(2,1)S(1)}, u32[]{:S(2)}, u32[]{:S(2)}) async-start(bf16[8,128,256]{2,1,0:T(8,128)(2,1)} %get-tuple-element.26), calls=%async_computation.2 | async-start | bytes 1048576 | tf_op jit(solution)/shard_map/dq_over_z/all_to_all | solution.py:322
  84.3 0.0 collective-permute-done.7.recv_ref
  84.3 0.1 dkv_over_core.1
  84.4 5.8 %collective-permute-start.8 = (bf16[256,256]{1,0:T(8,128)(2,1)S(1)}, bf16[256,256]{1,0:T(8,128)(2,1)S(1)}, u32[]{:S(2)}, u32[]{:S(2)}) collective-permute-start(bf16[256,256]{1,0:T(8,128)(2,1)S(1)} %get-tuple-element.23), channel_id=1, source_target_pairs={{0,128},{128,0},{256,384},{384,256},{1,129},{129,1},{257,385},{385... | collective-permute-start | bytes 393224 | tf_op jit(solution)/shard_map/dkv_over_y/ppermute | solution.py:264
  90.2 2.2 %collective-permute-start.9 = (bf16[256,256]{1,0:T(8,128)(2,1)S(1)}, bf16[256,256]{1,0:T(8,128)(2,1)S(1)}, u32[]{:S(2)}, u32[]{:S(2)}) collective-permute-start(bf16[256,256]{1,0:T(8,128)(2,1)S(1)} %get-tuple-element.24), channel_id=1, source_target_pairs={{0,256},{128,384},{256,0},{384,128},{1,257},{129,385},{257,1},{385... | collective-permute-start | bytes 393224 | tf_op jit(solution)/shard_map/dkv_over_y/ppermute | solution.py:264
  92.5 3.7 %collective-permute-start.10 = (bf16[256,256]{1,0:T(8,128)(2,1)S(1)}, bf16[256,256]{1,0:T(8,128)(2,1)S(1)}, u32[]{:S(2)}, u32[]{:S(2)}) collective-permute-start(bf16[256,256]{1,0:T(8,128)(2,1)S(1)} %get-tuple-element.25), channel_id=1, source_target_pairs={{0,384},{128,256},{256,128},{384,0},{1,385},{129,257},{257,129},{3... | collective-permute-start | bytes 393224 | tf_op jit(solution)/shard_map/dkv_over_y/ppermute | solution.py:264
  96.1 0.0 collective-permute-done.8.r1_ref
  96.1 7.7 %collective-permute-done.9.r2_ref = bf16[256,256]{1,0:T(8,128)(2,1)S(1)} collective-permute-done((bf16[256,256]{1,0:T(8,128)(2,1)S(1)}, bf16[256,256]{1,0:T(8,128)(2,1)S(1)}, u32[]{:S(2)}, u32[]{:S(2)}) %collective-permute-start.9) | collective-permute-done | bytes 131104 | tf_op jit(solution)/shard_map/dkv_over_y/ppermute | solution.py:264
  103.8 0.0 collective-permute-done.10.r3_ref
  103.8 0.0 all-to-all-done.2.dq_ref
  103.8 0.8 final.1
  (2 shorter events, 0.1 us)
Async XLA Ops:
  3.2 11.0 %copy-start.2 = (bf16[272,256]{1,0:T(8,128)(2,1)S(1)}, bf16[272,256]{1,0:T(8,128)(2,1)}, u32[]{:S(2)}) copy-start(bf16[272,256]{1,0:T(8,128)(2,1)} %get-tuple-element.16.own_ref) | copy-start | bytes 417796
  3.2 20.4 %copy-start.4 = (f32[128,128]{1,0:T(8,128)S(1)}, f32[128,128]{1,0:T(8,128)}, u32[]{:S(2)}) copy-start(f32[128,128]{1,0:T(8,128)} %get-tuple-element.17) | copy-start | bytes 196612
  3.2 45.4 %all-to-all-start = ((bf16[8,144,256]{2,1,0:T(8,128)(2,1)}), bf16[8,144,256]{2,1,0:T(8,128)(2,1)S(1)}, u32[]{:S(2)}, u32[]{:S(2)}) async-start(bf16[8,144,256]{2,1,0:T(8,128)(2,1)} %get-tuple-element.15), calls=%async_computation | async-start | bytes 1179648 | tf_op jit(solution)/shard_map/q_over_z/all_to_all | solution.py:285
  14.2 24.4 %collective-permute-start.2 = (bf16[272,256]{1,0:T(8,128)(2,1)S(1)}, bf16[272,256]{1,0:T(8,128)(2,1)S(1)}, u32[]{:S(2)}, u32[]{:S(2)}) collective-permute-start(bf16[272,256]{1,0:T(8,128)(2,1)S(1)} %copy-done.2), channel_id=1, source_target_pairs={{0,384},{128,256},{256,128},{384,0},{1,385},{129,257},{257,129},{3... | collective-permute-start | bytes 417800 | tf_op jit(solution)/shard_map/kv_over_y/ppermute | solution.py:264
  19.5 19.2 %collective-permute-start.1 = (bf16[272,256]{1,0:T(8,128)(2,1)S(1)}, bf16[272,256]{1,0:T(8,128)(2,1)S(1)}, u32[]{:S(2)}, u32[]{:S(2)}) collective-permute-start(bf16[272,256]{1,0:T(8,128)(2,1)S(1)} %copy-done.2), channel_id=1, source_target_pairs={{0,256},{128,384},{256,0},{384,128},{1,257},{129,385},{257,1},{385... | collective-permute-start | bytes 417800 | tf_op jit(solution)/shard_map/kv_over_y/ppermute | solution.py:264
  21.4 17.2 %collective-permute-start = (bf16[272,256]{1,0:T(8,128)(2,1)S(1)}, bf16[272,256]{1,0:T(8,128)(2,1)S(1)}, u32[]{:S(2)}, u32[]{:S(2)}) collective-permute-start(bf16[272,256]{1,0:T(8,128)(2,1)S(1)} %copy-done.2), channel_id=1, source_target_pairs={{0,128},{128,0},{256,384},{384,256},{1,129},{129,1},{257,385},{385... | collective-permute-start | bytes 417800 | tf_op jit(solution)/shard_map/kv_over_y/ppermute | solution.py:264
  23.6 10.0 %collective-permute-start.3 = (f32[128,128]{1,0:T(8,128)S(1)}, f32[128,128]{1,0:T(8,128)S(1)}, u32[]{:S(2)}, u32[]{:S(2)}) collective-permute-start(f32[128,128]{1,0:T(8,128)S(1)} %copy-done.4), channel_id=1, source_target_pairs={{0,1},{1,0},{2,3},{3,2},{4,5},{5,4},{6,7},{7,6},{8,9},{9,8},{10,11... | collective-permute-start | bytes 196616 | tf_op jit(solution)/shard_map/coupled_over_h/ppermute | solution.py:264
  33.6 5.0 %collective-permute-start.4 = (f32[128,128]{1,0:T(8,128)S(1)}, f32[128,128]{1,0:T(8,128)S(1)}, u32[]{:S(2)}, u32[]{:S(2)}) collective-permute-start(f32[128,128]{1,0:T(8,128)S(1)} %add.3.total_ref), channel_id=1, source_target_pairs={{0,2},{2,0},{4,6},{6,4},{1,3},{3,1},{5,7},{7,5},{8,10},{10,8},{12,... | collective-permute-start | bytes 196616 | tf_op jit(solution)/shard_map/coupled_over_x/ppermute | solution.py:264
  38.7 9.9 %collective-permute-start.5 = (bf16[4,272,256]{2,1,0:T(8,128)(2,1)S(1)}, bf16[4,272,256]{2,1,0:T(8,128)(2,1)S(1)}, u32[]{:S(2)}, u32[]{:S(2)}) collective-permute-start(bf16[4,272,256]{2,1,0:T(8,128)(2,1)S(1)} %get-tuple-element.18.kva_ref), channel_id=1, source_target_pairs={{0,8},{8,0},{1,9},{9,1},{2,10},{10,2},{3,11},{11,3},{4,12},{12,4},... | collective-permute-start | bytes 1671176 | tf_op jit(solution)/shard_map/kv_over_core/ppermute | solution.py:264
  43.8 7.3 %copy-start = (bf16[128,256]{1,0:T(8,128)(2,1)S(1)}, bf16[128,256]{1,0:T(8,128)(2,1)}, u32[]{:S(2)}) copy-start(bf16[128,256]{1,0:T(8,128)(2,1)} %o_ref.1) | copy-start | bytes 196612
  43.8 7.3 %copy-start.1 = (bf16[256,128]{1,0:T(8,128)(2,1)S(1)}, bf16[256,128]{1,0:T(8,128)(2,1)}, u32[]{:S(2)}) copy-start(bf16[256,128]{1,0:T(8,128)(2,1)} %proj_ref.3) | copy-start | bytes 196612
  43.8 7.3 %copy-start.3 = (f32[128,64]{0,1:T(8,128)S(1)}, f32[128,64]{0,1:T(8,128)}, u32[]{:S(2)}) copy-start(f32[128,64]{0,1:T(8,128)} %param.7) | copy-start | bytes 98308
  43.8 7.2 %collective-permute-start.6 = (f32[128,128]{1,0:T(8,128)S(1)}, f32[128,128]{1,0:T(8,128)S(1)}, u32[]{:S(2)}, u32[]{:S(2)}) collective-permute-start(f32[128,128]{1,0:T(8,128)S(1)} %get-tuple-element.19.total_ref), channel_id=1, source_target_pairs={{0,4},{2,6},{4,0},{6,2},{1,5},{3,7},{5,1},{7,3},{8,12},{10,14},{12... | collective-permute-start | bytes 196616 | tf_op jit(solution)/shard_map/coupled_over_x/ppermute | solution.py:264
  76.7 7.6 %collective-permute-start.7 = (bf16[4,256,256]{2,1,0:T(8,128)(2,1)S(1)}, bf16[4,256,256]{2,1,0:T(8,128)(2,1)S(1)}, u32[]{:S(2)}, u32[]{:S(2)}) collective-permute-start(bf16[4,256,256]{2,1,0:T(8,128)(2,1)S(1)} %get-tuple-element.21), channel_id=1, source_target_pairs={{0,8},{8,0},{1,9},{9,1},{2,10},{10,2},{3,11},{11,3},{4,12},{12,4},... | collective-permute-start | bytes 1572872 | tf_op jit(solution)/shard_map/dkv_over_core/ppermute | solution.py:264
  80.8 23.0 %all-to-all-start.2 = ((bf16[8,128,256]{2,1,0:T(8,128)(2,1)}), bf16[8,128,256]{2,1,0:T(8,128)(2,1)S(1)}, u32[]{:S(2)}, u32[]{:S(2)}) async-start(bf16[8,128,256]{2,1,0:T(8,128)(2,1)} %get-tuple-element.26), calls=%async_computation.2 | async-start | bytes 1048576 | tf_op jit(solution)/shard_map/dq_over_z/all_to_all | solution.py:322
  84.4 11.7 %collective-permute-start.8 = (bf16[256,256]{1,0:T(8,128)(2,1)S(1)}, bf16[256,256]{1,0:T(8,128)(2,1)S(1)}, u32[]{:S(2)}, u32[]{:S(2)}) collective-permute-start(bf16[256,256]{1,0:T(8,128)(2,1)S(1)} %get-tuple-element.23), channel_id=1, source_target_pairs={{0,128},{128,0},{256,384},{384,256},{1,129},{129,1},{257,385},{385... | collective-permute-start | bytes 393224 | tf_op jit(solution)/shard_map/dkv_over_y/ppermute | solution.py:264
  90.2 13.6 %collective-permute-start.9 = (bf16[256,256]{1,0:T(8,128)(2,1)S(1)}, bf16[256,256]{1,0:T(8,128)(2,1)S(1)}, u32[]{:S(2)}, u32[]{:S(2)}) collective-permute-start(bf16[256,256]{1,0:T(8,128)(2,1)S(1)} %get-tuple-element.24), channel_id=1, source_target_pairs={{0,256},{128,384},{256,0},{384,128},{1,257},{129,385},{257,1},{385... | collective-permute-start | bytes 393224 | tf_op jit(solution)/shard_map/dkv_over_y/ppermute | solution.py:264
  92.5 11.3 %collective-permute-start.10 = (bf16[256,256]{1,0:T(8,128)(2,1)S(1)}, bf16[256,256]{1,0:T(8,128)(2,1)S(1)}, u32[]{:S(2)}, u32[]{:S(2)}) collective-permute-start(bf16[256,256]{1,0:T(8,128)(2,1)S(1)} %get-tuple-element.25), channel_id=1, source_target_pairs={{0,384},{128,256},{256,128},{384,0},{1,385},{129,257},{257,129},{3... | collective-permute-start | bytes 393224 | tf_op jit(solution)/shard_map/dkv_over_y/ppermute | solution.py:264

commit v3 on v2

--- a/solution.py
+++ b/solution.py
@@ -18,7 +18,7 @@
 BF16 = jnp.bfloat16
 NT = (((1,), (1,)), ((), ()))
 MIB = 1 << 20
-JOIN_COST = 1_000_000
+JOIN_COST = 20_000_000_000
 FOLD_COST = 20_000_000_000
 
 
@@ -123,14 +123,22 @@
     out_ref[...] = st_ref[...].astype(BF16)
 
 
-def join_kernel(own_ref, r1_ref, r2_ref, r3_ref, total_ref, recv_ref, kv_ref, sum_ref):
+def join_kernel(own_ref, r1_ref, r2_ref, r3_ref, kv_ref):
     for n, ref in enumerate((own_ref, r1_ref, r2_ref, r3_ref)):
         kv_ref[n] = ref[...]
-    sum_ref[...] = total_ref[...] + recv_ref[...]
-
-
-def pack_kernel(total_ref, recv_ref, lat_ref, proj_ref, o_ref, st_ref, out_ref, d_ref):
-    coupled = total_ref[...] + recv_ref[...]
+
+
+def spread_kernel(part_ref, *refs):
+    out_ref = refs[-1]
+    part = part_ref[...]
+    for n in range(out_ref.shape[0]):
+        out_ref[n] = part
+
+
+def pack_kernel(parts_ref, lat_ref, proj_ref, o_ref, st_ref, out_ref, d_ref):
+    coupled = parts_ref[0]
+    for n in range(1, parts_ref.shape[0]):
+        coupled = coupled + parts_ref[n]
     shifts = coupled[:, 0:64]
     log_scale = coupled[:, 64:128]
     damping = jnp.exp(-log_scale)
@@ -264,31 +272,31 @@
     return lax.ppermute(x, axis, [(i, i ^ k) for i in range(size)])
 
 
-def local(n_x, n_h, latent, positions, queries, keys, values, attention_out, projection):
+def local(n_tp, latent, positions, queries, keys, values, attention_out, projection):
+    vmem, hbm, anywhere = (
+        pl.BlockSpec(memory_space=m) for m in (pltpu.VMEM, pltpu.HBM, pl.ANY)
+    )
     with jax.named_scope("prep"):
-        qpay, kvpay, total = call(
+        qpay, kvpay, part = call(
             prep_kernel,
             [((NZ, 144, 256), BF16), ((272, 256), BF16), ((128, 128), F32)],
             10_000_000,
             [pltpu.VMEM((128, 256), BF16)] * 4
             + [pltpu.VMEM((256, 128), BF16), pltpu.SemaphoreType.DMA((5,))],
-            [pl.BlockSpec(memory_space=pltpu.SMEM)] + [pl.BlockSpec(memory_space=pltpu.HBM)] * 5,
+            [pl.BlockSpec(memory_space=pltpu.SMEM)] + [hbm] * 5,
             limit=62,
         )(positions, queries, keys, values, attention_out, projection)
     with jax.named_scope("kv_over_y"):
         arrived = [swap(kvpay, "y", NY, k) for k in (1, 2, 3)]
-    with jax.named_scope("coupled_over_h"):
-        total = total + swap(total, "h", n_h, 1) if n_h > 1 else total
-    with jax.named_scope("coupled_over_x"):
-        first = swap(total, "x", n_x, 1) if n_x > 1 else jnp.zeros_like(total)
     with jax.named_scope("q_over_z"):
         qg = lax.all_to_all(qpay, "z", 0, 0)
+    with jax.named_scope("coupled_over_tp"):
+        (spread,) = call(
+            spread_kernel, [((n_tp, 128, 128), F32)], 1_000_000, specs=[vmem, anywhere]
+        )(part, qg)
+        parts = lax.all_to_all(spread, ("x", "h"), 0, 0)
     with jax.named_scope("join"):
-        kva, total = call(
-            join_kernel, [((NY, 272, 256), BF16), ((128, 128), F32)], JOIN_COST
-        )(kvpay, *arrived, total, first)
-    with jax.named_scope("coupled_over_x"):
-        second = swap(total, "x", n_x, 2) if n_x > 1 else jnp.zeros_like(total)
+        (kva,) = call(join_kernel, [((NY, 272, 256), BF16)], JOIN_COST)(kvpay, *arrived)
     with jax.named_scope("kv_over_core"):
         kvb = swap(kva, "c", NC, 1)
     with jax.named_scope("stats"):
@@ -301,7 +309,7 @@
     with jax.named_scope("pack"):
         (pay,) = call(
             pack_kernel, [((NZ, 192, 128), BF16)], 10_000_000, [pltpu.VMEM((16, 128), F32)]
-        )(total, second, latent.T, projection, attention_out, stats)
+        )(parts, latent.T, projection, attention_out, stats)
     with jax.named_scope("upstream_over_z"):
         gathered = lax.all_to_all(pay, "z", 0, 0)
     with jax.named_scope("main"):
@@ -342,7 +350,7 @@
         P(tp, None),
     )
     return jax.shard_map(
-        functools.partial(local, n_x, n_h),
+        functools.partial(local, n_x * n_h),
         mesh=fine,
         in_specs=placed,
         out_specs=(P(ctx, tp), P(ctx, tp), P(ctx, tp)),

time: 106 us -> 111 us (1.047)
  waiting for transfers between devices: 12.7 us -> 27.8 us
  starting transfers between devices: 60 us -> 54.2 us
  blocking collectives: 20 us -> 14.7 us
    ppermute x11 -> x8, starting transfers between devices: 45.5 us -> 30.4 us  [swap(): return lax.ppermute(x, axis, [(i, i ^ k) for i in range(size)])]
    all_to_all x1, waiting for transfers between devices: 0.01 us -> 9.99 us  [local(): qg = lax.all_to_all(qpay, 'z', 0, 0)]
    all_to_all x0 -> x1, starting transfers between devices: none -> 9.28 us  [local(): parts = lax.all_to_all(spread, ('x', 'h'), 0, 0)]
    all_to_all x0 -> x1, waiting for transfers between devices: none -> 8.61 us  [local(): parts = lax.all_to_all(spread, ('x', 'h'), 0, 0)]
    all_to_all x1, blocking collectives: 20 us -> 14.7 us  [local(): gathered = lax.all_to_all(pay, 'z', 0, 0)]
    ppermute x11 -> x8, waiting for transfers between devices: 12.6 us -> 9.23 us  [swap(): return lax.ppermute(x, axis, [(i, i ^ k) for i in range(size)])]
    pallas_call x7 -> x8, Pallas kernels: 11 us -> 11.7 us  [run(): pl.pallas_call(kernel, out_shape=[jax.ShapeDtypeStruct(s, d) for s, d in...]
  transfers between devices with their start and end apart: 13 -> 11, of which waited for: 4 -> 4; matrix products, arithmetic and copies ran while one was open for 0% -> 0% of each run, Pallas kernels for 2% -> 3%
where the time goes in v3:
time: 111 us; the launch traced here: 109 us
  starting transfers between devices  54.2 us (49%)
  waiting for transfers between devices  27.8 us (25%)
  blocking collectives  14.7 us (13%)
  Pallas kernels  11.7 us (11%)
    ppermute x8, starting transfers between devices, swap(): return lax.ppermute(x, axis, [(i, i ^ k) for i in range(size)])  30.4 us
    all_to_all x1, blocking collectives, local(): gathered = lax.all_to_all(pay, 'z', 0, 0)  14.7 us
    pallas_call x8, Pallas kernels, run(): pl.pallas_call(kernel, out_shape=[jax.ShapeDtypeStruct(s, d) for s, d in...  11.7 us
    all_to_all x1, starting transfers between devices, local(): qg = lax.all_to_all(qpay, 'z', 0, 0)  11 us
    all_to_all x1, waiting for transfers between devices, local(): qg = lax.all_to_all(qpay, 'z', 0, 0)  9.99 us
    all_to_all x1, starting transfers between devices, local(): parts = lax.all_to_all(spread, ('x', 'h'), 0, 0)  9.28 us
    ppermute x8, waiting for transfers between devices, swap(): return lax.ppermute(x, axis, [(i, i ^ k) for i in range(size)])  9.23 us
    all_to_all x1, waiting for transfers between devices, local(): parts = lax.all_to_all(spread, ('x', 'h'), 0, 0)  8.61 us
  transfers between devices with their start and end apart: 11, of which 4 were waited for; matrix products, arithmetic and copies ran while one was open for 0% of the time, Pallas kernels for 3%

profile of v3, /device:TPU:1, one launch (start us, length us, event | category | flops | bytes accessed | tf_op | source)
XLA Modules:
  0.0 109.3 jit_solution(11581119587647952659)
XLA Ops:
  0.6 2.6 %prep.1 = (bf16[8,144,256]{2,1,0:T(8,128)(2,1)}, bf16[272,256]{1,0:T(8,128)(2,1)}, f32[128,128]{1,0:T(8,128)}) custom-call(s32[128]{0:T(128)} %pos_ref.1, bf16[128,256]{1,0:T(8,128)(2,1)} %q_hbm.1, bf16[128,256]{1,0:T(8,128)(2,1)} %k_hbm.1, bf16[128,256]{1,0:T(8,128)(2,1)} %v_hbm.1, bf16[128,256]{1,0:T(8,128)(2,1)} %o_ref.1, bf16[256,128]{1,0:T(8,128)(2,1)} %proj_ref.3), custom_call_target="tpu_custom_call" | custom-call | flops 10000000 | bytes 2097152 | tf_op jit(solution)/shard_map/prep/pallas_call | solution.py:258
  3.2 0.0 copy-start.4
  3.2 0.0 copy-start.2
  3.2 11.0 %all-to-all-start = ((bf16[8,144,256]{2,1,0:T(8,128)(2,1)}), bf16[8,144,256]{2,1,0:T(8,128)(2,1)S(1)}, u32[]{:S(2)}, u32[]{:S(2)}) async-start(bf16[8,144,256]{2,1,0:T(8,128)(2,1)} %get-tuple-element.13), calls=%async_computation | async-start | bytes 1179648 | tf_op jit(solution)/shard_map/q_over_z/all_to_all | solution.py:292
  14.2 0.0 copy-done.4
  14.2 5.2 %collective-permute-start.2 = (bf16[272,256]{1,0:T(8,128)(2,1)S(1)}, bf16[272,256]{1,0:T(8,128)(2,1)S(1)}, u32[]{:S(2)}, u32[]{:S(2)}) collective-permute-start(bf16[272,256]{1,0:T(8,128)(2,1)S(1)} %copy-done.4), channel_id=1, source_target_pairs={{0,384},{128,256},{256,128},{384,0},{1,385},{129,257},{257,129},{3... | collective-permute-start | bytes 417800 | tf_op jit(solution)/shard_map/kv_over_y/ppermute | solution.py:272
  19.5 1.9 %collective-permute-start.1 = (bf16[272,256]{1,0:T(8,128)(2,1)S(1)}, bf16[272,256]{1,0:T(8,128)(2,1)S(1)}, u32[]{:S(2)}, u32[]{:S(2)}) collective-permute-start(bf16[272,256]{1,0:T(8,128)(2,1)S(1)} %copy-done.4), channel_id=1, source_target_pairs={{0,256},{128,384},{256,0},{384,128},{1,257},{129,385},{257,1},{385... | collective-permute-start | bytes 417800 | tf_op jit(solution)/shard_map/kv_over_y/ppermute | solution.py:272
  21.4 2.2 %collective-permute-start = (bf16[272,256]{1,0:T(8,128)(2,1)S(1)}, bf16[272,256]{1,0:T(8,128)(2,1)S(1)}, u32[]{:S(2)}, u32[]{:S(2)}) collective-permute-start(bf16[272,256]{1,0:T(8,128)(2,1)S(1)} %copy-done.4), channel_id=1, source_target_pairs={{0,128},{128,0},{256,384},{384,256},{1,129},{129,1},{257,385},{385... | collective-permute-start | bytes 417800 | tf_op jit(solution)/shard_map/kv_over_y/ppermute | solution.py:272
  23.6 10.0 %all-to-all-done.refs_0_.qg_ref = bf16[8,144,256]{2,1,0:T(8,128)(2,1)S(1)} async-done(((bf16[8,144,256]{2,1,0:T(8,128)(2,1)}), bf16[8,144,256]{2,1,0:T(8,128)(2,1)S(1)}, u32[]{:S(2)}, u32[]{:S(2)}) %all-to-all-start) | async-done | bytes 589856 | tf_op jit(solution)/shard_map/q_over_z/all_to_all | solution.py:292
  33.6 0.0 copy-done.2
  33.6 0.8 coupled_over_tp.1
  34.4 9.3 %all-to-all-start.1 = ((f32[8,128,128]{2,1,0:T(8,128)}), f32[8,128,128]{2,1,0:T(8,128)S(1)}, u32[]{:S(2)}, u32[]{:S(2)}) async-start(f32[8,128,128]{2,1,0:T(8,128)} %coupled_over_tp.1), calls=%async_computation.1 | async-start | bytes 1048576 | tf_op jit(solution)/shard_map/coupled_over_tp/all_to_all | solution.py:297
  43.7 0.0 collective-permute-done.2.r3_ref
  43.7 0.0 collective-permute-done.1.r2_ref
  43.7 0.0 collective-permute-done.r1_ref
  43.8 0.0 copy-start
  43.8 0.0 copy-start.1
  43.8 0.0 copy-start.3
  43.8 2.8 %collective-permute-start.3 = (bf16[4,272,256]{2,1,0:T(8,128)(2,1)S(1)}, bf16[4,272,256]{2,1,0:T(8,128)(2,1)S(1)}, u32[]{:S(2)}, u32[]{:S(2)}) collective-permute-start(bf16[4,272,256]{2,1,0:T(8,128)(2,1)S(1)} %join.1.kva_ref), channel_id=1, source_target_pairs={{0,8},{8,0},{1,9},{9,1},{2,10},{10,2},{3,11},{11,3},{4,12},{12,4},... | collective-permute-start | bytes 1671176 | tf_op jit(solution)/shard_map/kv_over_core/ppermute | solution.py:272
  46.6 1.6 %collective-permute-done.3.kvb_ref = bf16[4,272,256]{2,1,0:T(8,128)(2,1)S(1)} collective-permute-done((bf16[4,272,256]{2,1,0:T(8,128)(2,1)S(1)}, bf16[4,272,256]{2,1,0:T(8,128)(2,1)S(1)}, u32[]{:S(2)}, u32[]{:S(2)}) %collective-permute-start.3) | collective-permute-done | bytes 557088 | tf_op jit(solution)/shard_map/kv_over_core/ppermute | solution.py:272
  48.2 1.9 %stats.1.st_ref = bf16[48,128]{1,0:T(8,128)(2,1)S(1)} custom-call(bf16[8,144,256]{2,1,0:T(8,128)(2,1)S(1)} %all-to-all-done.refs_0_.qg_ref, bf16[4,272,256]{2,1,0:T(8,128)(2,1)S(1)} %join.1.kva_ref, bf16[4,272,256]{2,1,0:T(8,128)(2,1)S(1)} %collective-permute-done.3.kvb_ref), custom_call_target="tpu_custom_call" | custom-call | flops 1000000000 | bytes 2097152 | tf_op jit(solution)/shard_map/stats/pallas_call | solution.py:258
  50.1 8.6 %all-to-all-done.1.parts_ref = f32[8,128,128]{2,1,0:T(8,128)S(1)} async-done(((f32[8,128,128]{2,1,0:T(8,128)}), f32[8,128,128]{2,1,0:T(8,128)S(1)}, u32[]{:S(2)}, u32[]{:S(2)}) %all-to-all-start.1) | async-done | bytes 524320 | tf_op jit(solution)/shard_map/coupled_over_tp/all_to_all | solution.py:297
  58.7 0.0 copy-done
  58.7 0.0 copy-done.1
  58.7 0.0 copy-done.3
  58.7 0.4 pack.1
  59.2 14.7 %all_to_all.20.g_ref = bf16[8,192,128]{2,1,0:T(8,128)(2,1)S(1)} all-to-all(bf16[8,192,128]{2,1,0:T(8,128)(2,1)S(1)} %pack.1), channel_id=1, replica_groups=mesh['y'=4,'z'=8,'c'=2,'x'=4,'h'=2] {'z'}, dimensions={0} | all-to-all | bytes 786432 | tf_op jit(solution)/shard_map/upstream_over_z/all_to_all | solution.py:314
  73.8 5.1 %main.1 = (bf16[8,128,256]{2,1,0:T(8,128)(2,1)}, bf16[4,256,256]{2,1,0:T(8,128)(2,1)S(1)}, bf16[4,256,256]{2,1,0:T(8,128)(2,1)S(1)}) custom-call(bf16[8,144,256]{2,1,0:T(8,128)(2,1)S(1)} %all-to-all-done.refs_0_.qg_ref, bf16[4,272,256]{2,1,0:T(8,128)(2,1)S(1)} %join.1.kva_ref, bf16[4,272,256]{2,1,0:T(8,128)(2,1)S(1)} %collective-permute-done.3.kvb_ref, ...), custom_call_target="tpu_custom_call" | custom-call | flops 4000000000 | bytes 2097152 | tf_op jit(solution)/shard_map/main/pallas_call | solution.py:258
  78.9 5.3 %collective-permute-start.4 = (bf16[4,256,256]{2,1,0:T(8,128)(2,1)S(1)}, bf16[4,256,256]{2,1,0:T(8,128)(2,1)S(1)}, u32[]{:S(2)}, u32[]{:S(2)}) collective-permute-start(bf16[4,256,256]{2,1,0:T(8,128)(2,1)S(1)} %get-tuple-element.17), channel_id=1, source_target_pairs={{0,8},{8,0},{1,9},{9,1},{2,10},{10,2},{3,11},{11,3},{4,12},{12,4},... | collective-permute-start | bytes 1572872 | tf_op jit(solution)/shard_map/dkv_over_core/ppermute | solution.py:272
  84.2 3.5 %all-to-all-start.3 = ((bf16[8,128,256]{2,1,0:T(8,128)(2,1)}), bf16[8,128,256]{2,1,0:T(8,128)(2,1)S(1)}, u32[]{:S(2)}, u32[]{:S(2)}) async-start(bf16[8,128,256]{2,1,0:T(8,128)(2,1)} %get-tuple-element.22), calls=%async_computation.3 | async-start | bytes 1048576 | tf_op jit(solution)/shard_map/dq_over_z/all_to_all | solution.py:330
  87.7 0.0 collective-permute-done.4.recv_ref
  87.7 0.1 dkv_over_core.1
  87.8 7.1 %collective-permute-start.5 = (bf16[256,256]{1,0:T(8,128)(2,1)S(1)}, bf16[256,256]{1,0:T(8,128)(2,1)S(1)}, u32[]{:S(2)}, u32[]{:S(2)}) collective-permute-start(bf16[256,256]{1,0:T(8,128)(2,1)S(1)} %get-tuple-element.19), channel_id=1, source_target_pairs={{0,128},{128,0},{256,384},{384,256},{1,129},{129,1},{257,385},{385... | collective-permute-start | bytes 393224 | tf_op jit(solution)/shard_map/dkv_over_y/ppermute | solution.py:272
  95.0 1.9 %collective-permute-start.6 = (bf16[256,256]{1,0:T(8,128)(2,1)S(1)}, bf16[256,256]{1,0:T(8,128)(2,1)S(1)}, u32[]{:S(2)}, u32[]{:S(2)}) collective-permute-start(bf16[256,256]{1,0:T(8,128)(2,1)S(1)} %get-tuple-element.20), channel_id=1, source_target_pairs={{0,256},{128,384},{256,0},{384,128},{1,257},{129,385},{257,1},{385... | collective-permute-start | bytes 393224 | tf_op jit(solution)/shard_map/dkv_over_y/ppermute | solution.py:272
  96.9 4.0 %collective-permute-start.7 = (bf16[256,256]{1,0:T(8,128)(2,1)S(1)}, bf16[256,256]{1,0:T(8,128)(2,1)S(1)}, u32[]{:S(2)}, u32[]{:S(2)}) collective-permute-start(bf16[256,256]{1,0:T(8,128)(2,1)S(1)} %get-tuple-element.21), channel_id=1, source_target_pairs={{0,384},{128,256},{256,128},{384,0},{1,385},{129,257},{257,129},{3... | collective-permute-start | bytes 393224 | tf_op jit(solution)/shard_map/dkv_over_y/ppermute | solution.py:272
  100.9 0.0 collective-permute-done.5.r1_ref
  100.9 7.6 %collective-permute-done.6.r2_ref = bf16[256,256]{1,0:T(8,128)(2,1)S(1)} collective-permute-done((bf16[256,256]{1,0:T(8,128)(2,1)S(1)}, bf16[256,256]{1,0:T(8,128)(2,1)S(1)}, u32[]{:S(2)}, u32[]{:S(2)}) %collective-permute-start.6) | collective-permute-done | bytes 131104 | tf_op jit(solution)/shard_map/dkv_over_y/ppermute | solution.py:272
  108.6 0.0 collective-permute-done.7.r3_ref
  108.6 0.0 all-to-all-done.3.dq_ref
  108.6 0.8 final.1
  (1 shorter events, 0.0 us)
Async XLA Ops:
  3.2 11.0 %copy-start.4 = (bf16[272,256]{1,0:T(8,128)(2,1)S(1)}, bf16[272,256]{1,0:T(8,128)(2,1)}, u32[]{:S(2)}) copy-start(bf16[272,256]{1,0:T(8,128)(2,1)} %get-tuple-element.14.own_ref) | copy-start | bytes 417796
  3.2 30.4 %copy-start.2 = (f32[128,128]{1,0:T(8,128)S(1)}, f32[128,128]{1,0:T(8,128)}, u32[]{:S(2)}) copy-start(f32[128,128]{1,0:T(8,128)} %get-tuple-element.15.part_ref) | copy-start | bytes 196612
  3.2 30.4 %all-to-all-start = ((bf16[8,144,256]{2,1,0:T(8,128)(2,1)}), bf16[8,144,256]{2,1,0:T(8,128)(2,1)S(1)}, u32[]{:S(2)}, u32[]{:S(2)}) async-start(bf16[8,144,256]{2,1,0:T(8,128)(2,1)} %get-tuple-element.13), calls=%async_computation | async-start | bytes 1179648 | tf_op jit(solution)/shard_map/q_over_z/all_to_all | solution.py:292
  14.2 29.5 %collective-permute-start.2 = (bf16[272,256]{1,0:T(8,128)(2,1)S(1)}, bf16[272,256]{1,0:T(8,128)(2,1)S(1)}, u32[]{:S(2)}, u32[]{:S(2)}) collective-permute-start(bf16[272,256]{1,0:T(8,128)(2,1)S(1)} %copy-done.4), channel_id=1, source_target_pairs={{0,384},{128,256},{256,128},{384,0},{1,385},{129,257},{257,129},{3... | collective-permute-start | bytes 417800 | tf_op jit(solution)/shard_map/kv_over_y/ppermute | solution.py:272
  19.5 24.3 %collective-permute-start.1 = (bf16[272,256]{1,0:T(8,128)(2,1)S(1)}, bf16[272,256]{1,0:T(8,128)(2,1)S(1)}, u32[]{:S(2)}, u32[]{:S(2)}) collective-permute-start(bf16[272,256]{1,0:T(8,128)(2,1)S(1)} %copy-done.4), channel_id=1, source_target_pairs={{0,256},{128,384},{256,0},{384,128},{1,257},{129,385},{257,1},{385... | collective-permute-start | bytes 417800 | tf_op jit(solution)/shard_map/kv_over_y/ppermute | solution.py:272
  21.4 22.3 %collective-permute-start = (bf16[272,256]{1,0:T(8,128)(2,1)S(1)}, bf16[272,256]{1,0:T(8,128)(2,1)S(1)}, u32[]{:S(2)}, u32[]{:S(2)}) collective-permute-start(bf16[272,256]{1,0:T(8,128)(2,1)S(1)} %copy-done.4), channel_id=1, source_target_pairs={{0,128},{128,0},{256,384},{384,256},{1,129},{129,1},{257,385},{385... | collective-permute-start | bytes 417800 | tf_op jit(solution)/shard_map/kv_over_y/ppermute | solution.py:272
  34.4 24.3 %all-to-all-start.1 = ((f32[8,128,128]{2,1,0:T(8,128)}), f32[8,128,128]{2,1,0:T(8,128)S(1)}, u32[]{:S(2)}, u32[]{:S(2)}) async-start(f32[8,128,128]{2,1,0:T(8,128)} %coupled_over_tp.1), calls=%async_computation.1 | async-start | bytes 1048576 | tf_op jit(solution)/shard_map/coupled_over_tp/all_to_all | solution.py:297
  43.8 14.9 %copy-start = (bf16[128,256]{1,0:T(8,128)(2,1)S(1)}, bf16[128,256]{1,0:T(8,128)(2,1)}, u32[]{:S(2)}) copy-start(bf16[128,256]{1,0:T(8,128)(2,1)} %o_ref.1) | copy-start | bytes 196612
  43.8 14.9 %copy-start.1 = (bf16[256,128]{1,0:T(8,128)(2,1)S(1)}, bf16[256,128]{1,0:T(8,128)(2,1)}, u32[]{:S(2)}) copy-start(bf16[256,128]{1,0:T(8,128)(2,1)} %proj_ref.3) | copy-start | bytes 196612
  43.8 14.9 %copy-start.3 = (f32[128,64]{0,1:T(8,128)S(1)}, f32[128,64]{0,1:T(8,128)}, u32[]{:S(2)}) copy-start(f32[128,64]{0,1:T(8,128)} %param.7) | copy-start | bytes 98308
  43.8 4.4 %collective-permute-start.3 = (bf16[4,272,256]{2,1,0:T(8,128)(2,1)S(1)}, bf16[4,272,256]{2,1,0:T(8,128)(2,1)S(1)}, u32[]{:S(2)}, u32[]{:S(2)}) collective-permute-start(bf16[4,272,256]{2,1,0:T(8,128)(2,1)S(1)} %join.1.kva_ref), channel_id=1, source_target_pairs={{0,8},{8,0},{1,9},{9,1},{2,10},{10,2},{3,11},{11,3},{4,12},{12,4},... | collective-permute-start | bytes 1671176 | tf_op jit(solution)/shard_map/kv_over_core/ppermute | solution.py:272
  78.9 8.8 %collective-permute-start.4 = (bf16[4,256,256]{2,1,0:T(8,128)(2,1)S(1)}, bf16[4,256,256]{2,1,0:T(8,128)(2,1)S(1)}, u32[]{:S(2)}, u32[]{:S(2)}) collective-permute-start(bf16[4,256,256]{2,1,0:T(8,128)(2,1)S(1)} %get-tuple-element.17), channel_id=1, source_target_pairs={{0,8},{8,0},{1,9},{9,1},{2,10},{10,2},{3,11},{11,3},{4,12},{12,4},... | collective-permute-start | bytes 1572872 | tf_op jit(solution)/shard_map/dkv_over_core/ppermute | solution.py:272
  84.2 24.4 %all-to-all-start.3 = ((bf16[8,128,256]{2,1,0:T(8,128)(2,1)}), bf16[8,128,256]{2,1,0:T(8,128)(2,1)S(1)}, u32[]{:S(2)}, u32[]{:S(2)}) async-start(bf16[8,128,256]{2,1,0:T(8,128)(2,1)} %get-tuple-element.22), calls=%async_computation.3 | async-start | bytes 1048576 | tf_op jit(solution)/shard_map/dq_over_z/all_to_all | solution.py:330
  87.8 13.1 %collective-permute-start.5 = (bf16[256,256]{1,0:T(8,128)(2,1)S(1)}, bf16[256,256]{1,0:T(8,128)(2,1)S(1)}, u32[]{:S(2)}, u32[]{:S(2)}) collective-permute-start(bf16[256,256]{1,0:T(8,128)(2,1)S(1)} %get-tuple-element.19), channel_id=1, source_target_pairs={{0,128},{128,0},{256,384},{384,256},{1,129},{129,1},{257,385},{385... | collective-permute-start | bytes 393224 | tf_op jit(solution)/shard_map/dkv_over_y/ppermute | solution.py:272
  95.0 13.6 %collective-permute-start.6 = (bf16[256,256]{1,0:T(8,128)(2,1)S(1)}, bf16[256,256]{1,0:T(8,128)(2,1)S(1)}, u32[]{:S(2)}, u32[]{:S(2)}) collective-permute-start(bf16[256,256]{1,0:T(8,128)(2,1)S(1)} %get-tuple-element.20), channel_id=1, source_target_pairs={{0,256},{128,384},{256,0},{384,128},{1,257},{129,385},{257,1},{385... | collective-permute-start | bytes 393224 | tf_op jit(solution)/shard_map/dkv_over_y/ppermute | solution.py:272
  96.9 11.7 %collective-permute-start.7 = (bf16[256,256]{1,0:T(8,128)(2,1)S(1)}, bf16[256,256]{1,0:T(8,128)(2,1)S(1)}, u32[]{:S(2)}, u32[]{:S(2)}) collective-permute-start(bf16[256,256]{1,0:T(8,128)(2,1)S(1)} %get-tuple-element.21), channel_id=1, source_target_pairs={{0,384},{128,256},{256,128},{384,0},{1,385},{129,257},{257,129},{3... | collective-permute-start | bytes 393224 | tf_op jit(solution)/shard_map/dkv_over_y/ppermute | solution.py:272

commit v4 on v2

--- a/solution.py
+++ b/solution.py
@@ -10,6 +10,7 @@
 HEAD = 128
 SPAN = 64
 NZ, NY, NC = 8, 4, 2
+NQ = NY * NC
 LOG2E = 1.4426950408889634
 FACTOR = HEAD ** (-0.5)
 SCALE = FACTOR * LOG2E
@@ -19,7 +20,7 @@
 NT = (((1,), (1,)), ((), ()))
 MIB = 1 << 20
 JOIN_COST = 1_000_000
-FOLD_COST = 20_000_000_000
+FOLD_COST = 1_000_000
 
 
 def dot_nt(a, b):
@@ -46,13 +47,13 @@
     tag = jnp.full((16, 256), block, F32).astype(BF16)
     for copy in copies:
         copy.wait()
-    k, v, q = k_ref[...], v_ref[...], q_ref[...]
-    kvpay_ref[0:128, :] = k
-    kvpay_ref[128:256, :] = v
-    kvpay_ref[256:272, :] = tag
+    k, v = k_ref[...], v_ref[...]
     for i in range(NZ):
-        qpay_ref[i, 0:128, :] = q
-        qpay_ref[i, 128:144, :] = tag
+        kvpay_ref[i, 0:128, :] = k
+        kvpay_ref[i, 128:256, :] = v
+        kvpay_ref[i, 256:272, :] = tag
+    qpay_ref[0:128, :] = q_ref[...]
+    qpay_ref[128:144, :] = tag
     part_ref[...] = dot(o_ref[...], proj_ref[...])
 
 
@@ -61,7 +62,7 @@
     low = lane < SPAN
     row = (lane & (SPAN - 1)).astype(F32)
     early, late = [], []
-    for p in range(NZ // 2):
+    for p in range(NQ // 2):
         first = qg_ref[2 * p, 128:144, 0:128].astype(F32)[0:1, :]
         second = qg_ref[2 * p + 1, 128:144, 0:128].astype(F32)[0:1, :]
         block = jnp.where(low, first, second)
@@ -73,7 +74,7 @@
 def key_positions(kv_ref, late):
     row = lax.broadcasted_iota(jnp.int32, (SPAN, 128), 0).astype(F32)
     out = []
-    for j in range(NY):
+    for j in range(kv_ref.shape[0]):
         block = kv_ref[j, 256:272, 0:128].astype(F32)[0:1, :]
         base = (127.0 - block) * SPAN if late else block * SPAN
         out.append(base + row)
@@ -86,9 +87,16 @@
     return part.reshape(part.shape[0] * SPAN, HEAD)
 
 
-def stats_kernel(qg_ref, kva_ref, kvb_ref, out_ref, s_ref, st_ref):
+def stats_kernel(
+    q0_ref, q1_ref, q2_ref, q3_ref, kv_ref, p0_ref, p1_ref, lat_ref, proj_ref, o_ref,
+    out_ref, qg_ref, s_ref, st_ref, d_ref,
+):
+    here = lax.axis_index("y")
+    for k, ref in enumerate((q0_ref, q1_ref, q2_ref, q3_ref)):
+        for core in range(NC):
+            qg_ref[2 * (here ^ k) + core] = ref[core]
     q_early, q_late = query_positions(qg_ref)
-    sides = (kva_ref, kvb_ref)
+    sides = (kv_ref.at[0:4], kv_ref.at[4:8])
     for head in range(2):
         for part in range(2):
             q = rows_of(qg_ref, part * SPAN, head)
@@ -120,17 +128,8 @@
                 st_ref[base + r : base + r + 1, :] = top[:, lanes]
                 st_ref[base + 4 + r : base + 5 + r, :] = high[:, lanes]
                 st_ref[base + 8 + r : base + 9 + r, :] = low[:, lanes]
-    out_ref[...] = st_ref[...].astype(BF16)
-
-
-def join_kernel(own_ref, r1_ref, r2_ref, r3_ref, total_ref, recv_ref, kv_ref, sum_ref):
-    for n, ref in enumerate((own_ref, r1_ref, r2_ref, r3_ref)):
-        kv_ref[n] = ref[...]
-    sum_ref[...] = total_ref[...] + recv_ref[...]
-
-
-def pack_kernel(total_ref, recv_ref, lat_ref, proj_ref, o_ref, st_ref, out_ref, d_ref):
-    coupled = total_ref[...] + recv_ref[...]
+    stats = st_ref[...].astype(BF16)
+    coupled = p0_ref[...] + p1_ref[...]
     shifts = coupled[:, 0:64]
     log_scale = coupled[:, 64:128]
     damping = jnp.exp(-log_scale)
@@ -146,25 +145,30 @@
         d_ref[2 * head : 2 * head + 1, :] = high
         d_ref[2 * head + 1 : 2 * head + 2, :] = delta - high
     deltas = d_ref[...].astype(BF16)
-    stats = st_ref[...]
-    for i in range(NZ):
+    for i in range(NQ):
         out_ref[i, 0:128, :] = upstream
         out_ref[i, 128:144, :] = deltas
         out_ref[i, 144:192, :] = stats
 
 
-def main_kernel(qg_ref, kva_ref, kvb_ref, g_ref, proj_ref, dq_ref, da_ref, db_ref, ds_ref):
+def join_kernel(own_ref, recv_ref, out_ref):
+    core = lax.axis_index("c")
+    out_ref[core] = own_ref[...]
+    out_ref[1 - core] = recv_ref[...]
+
+
+def main_kernel(qg_ref, kv_ref, g_ref, proj_ref, dkv_ref, qa_ref, qb_ref, ds_ref, dq_ref):
     q_early, q_late = query_positions(qg_ref)
     lane = lax.broadcasted_iota(jnp.int32, (1, 128), 1)
     low = lane < SPAN
     upstream = [
-        g_ref[:, part * SPAN : (part + 1) * SPAN, :].reshape(NZ * SPAN, HEAD) for part in range(2)
+        g_ref[:, part * SPAN : (part + 1) * SPAN, :].reshape(NQ * SPAN, HEAD) for part in range(2)
     ]
-    tails = [g_ref[i, 128:144, :].astype(F32) for i in range(NZ)]
+    tails = [g_ref[i, 128:144, :].astype(F32) for i in range(NQ)]
     turned = [pltpu.roll(t, SPAN, 1) for t in tails]
     stats = g_ref[:, 144:192, :].astype(F32)
-    sides = (kva_ref, kvb_ref)
-    grads = (da_ref, db_ref)
+    sides = (kv_ref.at[0:4], kv_ref.at[4:8])
+    grads = (dkv_ref.at[0:4], dkv_ref.at[4:8])
     for head in range(2):
         cols = slice(head * HEAD, (head + 1) * HEAD)
         proj = proj_ref[cols, :]
@@ -178,7 +182,7 @@
             value = top + jnp.log(total) * LOG2E
             lse.append(jnp.concatenate([value[r : r + 1, :] for r in range(4)], axis=1))
             pieces = []
-            for p in range(NZ // 2):
+            for p in range(NQ // 2):
                 left = (tails if part == 0 else turned)[2 * p]
                 right = (turned if part == 0 else tails)[2 * p + 1]
                 both = jnp.where(low, left, right)
@@ -221,26 +225,31 @@
         late_t = jnp.concatenate([rows_of(kv, 64, head) for kv in sides], axis=0).T
         dqe = dot(early_t, ds_ref[0:512, 0:512])
         dql = dot(early_t, ds_ref[0:512, 512:1024]) + dot(late_t, ds_ref[512:1024, 512:1024])
-        dq_ref[:, 0:64, cols] = (dqe * FACTOR).T.astype(BF16).reshape(NZ, SPAN, HEAD)
-        dq_ref[:, 64:128, cols] = (dql * FACTOR).T.astype(BF16).reshape(NZ, SPAN, HEAD)
+        dq_ref[:, 0:64, cols] = (dqe * FACTOR).T.astype(BF16).reshape(NQ, SPAN, HEAD)
+        dq_ref[:, 64:128, cols] = (dql * FACTOR).T.astype(BF16).reshape(NQ, SPAN, HEAD)
+    core = lax.axis_index("c")
+    for y in range(NY):
+        qa_ref[y] = dq_ref[2 * y + core]
+        qb_ref[y] = dq_ref[2 * y + 1 - core]
 
 
 def fold_kernel(own_ref, recv_ref, o0_ref, o1_ref, o2_ref, o3_ref):
-    o0_ref[...] = own_ref[0].astype(F32) + recv_ref[0].astype(F32)
-    for k, ref in ((1, o1_ref), (2, o2_ref), (3, o3_ref)):
-        ref[...] = (own_ref[k].astype(F32) + recv_ref[k].astype(F32)).astype(BF16)
-
-
-def final_kernel(own_ref, r1_ref, r2_ref, r3_ref, dq_ref, qo_ref, ko_ref, vo_ref):
+    here = lax.axis_index("y")
+    for k, ref in enumerate((o0_ref, o1_ref, o2_ref, o3_ref)):
+        total = own_ref[here ^ k].astype(F32) + recv_ref[here ^ k].astype(F32)
+        ref[...] = total.astype(ref.dtype)
+
+
+def final_kernel(own_ref, r1_ref, r2_ref, r3_ref, kv_ref, qo_ref, ko_ref, vo_ref):
     total = own_ref[...]
     for ref in (r1_ref, r2_ref, r3_ref):
         total = total + ref[...].astype(F32)
+    qo_ref[...] = total.astype(BF16)
+    total = kv_ref[0].astype(F32)
+    for i in range(1, NZ):
+        total = total + kv_ref[i].astype(F32)
     ko_ref[...] = total[0:128, :].astype(BF16)
     vo_ref[...] = total[128:256, :].astype(BF16)
-    dq = dq_ref[0].astype(F32)
-    for i in range(1, NZ):
-        dq = dq + dq_ref[i].astype(F32)
-    qo_ref[...] = dq.astype(BF16)
 
 
 def call(kernel, outs, cost, scratch=(), specs=None, limit=48):
@@ -264,65 +273,62 @@
     return lax.ppermute(x, axis, [(i, i ^ k) for i in range(size)])
 
 
-def local(n_x, n_h, latent, positions, queries, keys, values, attention_out, projection):
+def local(n_tp, latent, positions, queries, keys, values, attention_out, projection):
+    hbm = pl.BlockSpec(memory_space=pltpu.HBM)
     with jax.named_scope("prep"):
         qpay, kvpay, total = call(
             prep_kernel,
-            [((NZ, 144, 256), BF16), ((272, 256), BF16), ((128, 128), F32)],
+            [((144, 256), BF16), ((NZ, 272, 256), BF16), ((128, 128), F32)],
             10_000_000,
             [pltpu.VMEM((128, 256), BF16)] * 4
             + [pltpu.VMEM((256, 128), BF16), pltpu.SemaphoreType.DMA((5,))],
-            [pl.BlockSpec(memory_space=pltpu.SMEM)] + [pl.BlockSpec(memory_space=pltpu.HBM)] * 5,
+            [pl.BlockSpec(memory_space=pltpu.SMEM)] + [hbm] * 5,
             limit=62,
         )(positions, queries, keys, values, attention_out, projection)
-    with jax.named_scope("kv_over_y"):
-        arrived = [swap(kvpay, "y", NY, k) for k in (1, 2, 3)]
+    with jax.named_scope("kv_over_z"):
+        kvg = lax.all_to_all(kvpay, "z", 0, 0)
     with jax.named_scope("coupled_over_h"):
-        total = total + swap(total, "h", n_h, 1) if n_h > 1 else total
+        near = [swap(total, ("x", "h"), n_tp, k) for k in (1, 2, 3) if k < n_tp]
+        total = sum(near, total)
+    with jax.named_scope("q_over_core"):
+        other = swap(qpay, "c", NC, 1)
+        (pair,) = call(join_kernel, [((NC, 144, 256), BF16)], JOIN_COST)(qpay, other)
+    with jax.named_scope("q_over_y"):
+        arrived = [swap(pair, "y", NY, k) for k in (1, 2, 3)]
     with jax.named_scope("coupled_over_x"):
-        first = swap(total, "x", n_x, 1) if n_x > 1 else jnp.zeros_like(total)
-    with jax.named_scope("q_over_z"):
-        qg = lax.all_to_all(qpay, "z", 0, 0)
-    with jax.named_scope("join"):
-        kva, total = call(
-            join_kernel, [((NY, 272, 256), BF16), ((128, 128), F32)], JOIN_COST
-        )(kvpay, *arrived, total, first)
-    with jax.named_scope("coupled_over_x"):
-        second = swap(total, "x", n_x, 2) if n_x > 1 else jnp.zeros_like(total)
-    with jax.named_scope("kv_over_core"):
-        kvb = swap(kva, "c", NC, 1)
+        far = swap(total, ("x", "h"), n_tp, 4) if n_tp > 4 else jnp.zeros_like(total)
     with jax.named_scope("stats"):
-        (stats,) = call(
+        pay, qg = call(
             stats_kernel,
-            [((48, 128), BF16)],
+            [((NQ, 192, 128), BF16), ((NQ, 144, 256), BF16)],
             1_000_000_000,
-            [pltpu.VMEM((4, 256, 512), F32), pltpu.VMEM((48, 128), F32)],
-        )(qg, kva, kvb)
-    with jax.named_scope("pack"):
-        (pay,) = call(
-            pack_kernel, [((NZ, 192, 128), BF16)], 10_000_000, [pltpu.VMEM((16, 128), F32)]
-        )(total, second, latent.T, projection, attention_out, stats)
-    with jax.named_scope("upstream_over_z"):
-        gathered = lax.all_to_all(pay, "z", 0, 0)
+            [
+                pltpu.VMEM((4, 256, 512), F32),
+                pltpu.VMEM((48, 128), F32),
+                pltpu.VMEM((16, 128), F32),
+            ],
+        )(pair, *arrived, kvg, total, far, latent.T, projection, attention_out)
+    with jax.named_scope("upstream_over_yc"):
+        gathered = lax.all_to_all(pay, ("y", "c"), 0, 0)
     with jax.named_scope("main"):
-        dq, da, db = call(
+        dkv, dqa, dqb = call(
             main_kernel,
-            [((NZ, 128, 256), BF16), ((NY, 256, 256), BF16), ((NY, 256, 256), BF16)],
+            [((NZ, 256, 256), BF16), ((NY, 128, 256), BF16), ((NY, 128, 256), BF16)],
             4_000_000_000,
-            [pltpu.VMEM((1024, 1024), BF16)],
-        )(qg, kva, kvb, gathered, projection)
-    with jax.named_scope("dkv_over_core"):
-        other = swap(db, "c", NC, 1)
+            [pltpu.VMEM((1024, 1024), BF16), pltpu.VMEM((NQ, 128, 256), BF16)],
+        )(qg, kvg, gathered, projection)
+    with jax.named_scope("dkv_over_z"):
+        dkvs = lax.all_to_all(dkv, "z", 0, 0)
+    with jax.named_scope("dq_over_core"):
+        other = swap(dqb, "c", NC, 1)
         own, *send = call(
-            fold_kernel, [((256, 256), F32)] + [((256, 256), BF16)] * 3, FOLD_COST
-        )(da, other)
-    with jax.named_scope("dkv_over_y"):
+            fold_kernel, [((128, 256), F32)] + [((128, 256), BF16)] * 3, FOLD_COST
+        )(dqa, other)
+    with jax.named_scope("dq_over_y"):
         back = [swap(s, "y", NY, k) for k, s in zip((1, 2, 3), send)]
-    with jax.named_scope("dq_over_z"):
-        dqs = lax.all_to_all(dq, "z", 0, 0)
     with jax.named_scope("final"):
         return tuple(
-            call(final_kernel, [((128, 256), BF16)] * 3, 1_000_000)(own, *back, dqs)
+            call(final_kernel, [((128, 256), BF16)] * 3, 1_000_000)(own, *back, dkvs)
         )
 
 
@@ -342,7 +348,7 @@
         P(tp, None),
     )
     return jax.shard_map(
-        functools.partial(local, n_x, n_h),
+        functools.partial(local, n_x * n_h),
         mesh=fine,
         in_specs=placed,
         out_specs=(P(ctx, tp), P(ctx, tp), P(ctx, tp)),

time: 106 us -> 110 us (1.038)
  waiting for transfers between devices: 12.7 us -> 22.4 us
  blocking collectives: 20 us -> 15.5 us
    all_to_all x2, waiting for transfers between devices: 0.01 us -> 12.7 us  [the longest x1 12.7 us: local(): dkvs = lax.all_to_all(dkv, 'z', 0, 0)]
    all_to_all x1, blocking collectives: 20 us -> 15.5 us  [local(): gathered = lax.all_to_all(pay, ('y', 'c'), 0, 0)]
    ppermute x11 -> x12, starting transfers between devices: 45.5 us -> 41.6 us  [swap(): return lax.ppermute(x, axis, [(i, i ^ k) for i in range(size)])]
    all_to_all x2, starting transfers between devices: 14.5 us -> 17.9 us  [the longest x1 11 us: local(): kvg = lax.all_to_all(kvpay, 'z', 0, 0)]
    ppermute x11 -> x12, waiting for transfers between devices: 12.6 us -> 9.66 us  [swap(): return lax.ppermute(x, axis, [(i, i ^ k) for i in range(size)])]
    pallas_call x7 -> x6, Pallas kernels: 11 us -> 10.7 us  [run(): pl.pallas_call(kernel, out_shape=[jax.ShapeDtypeStruct(s, d) for s, d in...]
  transfers between devices with their start and end apart: 13 -> 14, of which waited for: 4 -> 5; matrix products, arithmetic and copies ran while one was open for 0% -> 0% of each run, Pallas kernels for 2% -> 0%
where the time goes in v4:
time: 110 us; the launch traced here: 109 us
  starting transfers between devices  59.5 us (54%)
  waiting for transfers between devices  22.4 us (20%)
  blocking collectives  15.5 us (14%)
  Pallas kernels  10.7 us (10%)
    ppermute x12, starting transfers between devices, swap(): return lax.ppermute(x, axis, [(i, i ^ k) for i in range(size)])  41.6 us
    all_to_all x1, blocking collectives, local(): gathered = lax.all_to_all(pay, ('y', 'c'), 0, 0)  15.5 us
    all_to_all x1, waiting for transfers between devices, local(): dkvs = lax.all_to_all(dkv, 'z', 0, 0)  12.7 us
    all_to_all x1, starting transfers between devices, local(): kvg = lax.all_to_all(kvpay, 'z', 0, 0)  11 us
    pallas_call x6, Pallas kernels, run(): pl.pallas_call(kernel, out_shape=[jax.ShapeDtypeStruct(s, d) for s, d in...  10.7 us
    ppermute x12, waiting for transfers between devices, swap(): return lax.ppermute(x, axis, [(i, i ^ k) for i in range(size)])  9.66 us
    all_to_all x1, starting transfers between devices, local(): dkvs = lax.all_to_all(dkv, 'z', 0, 0)  6.92 us
  transfers between devices with their start and end apart: 14, of which 5 were waited for; matrix products, arithmetic and copies ran while one was open for 0% of the time, Pallas kernels for 0%

profile of v4, /device:TPU:1, one launch (start us, length us, event | category | flops | bytes accessed | tf_op | source)
XLA Modules:
  0.0 109.0 jit_solution(10064034941654269919)
XLA Ops:
  0.6 2.8 %prep.1 = (bf16[144,256]{1,0:T(8,128)(2,1)}, bf16[8,272,256]{2,1,0:T(8,128)(2,1)}, f32[128,128]{1,0:T(8,128)}) custom-call(s32[128]{0:T(128)} %pos_ref.1, bf16[128,256]{1,0:T(8,128)(2,1)} %q_hbm.1, bf16[128,256]{1,0:T(8,128)(2,1)} %k_hbm.1, bf16[128,256]{1,0:T(8,128)(2,1)} %v_hbm.1, bf16[128,256]{1,0:T(8,128)(2,1)} %o_ref.1, bf16[256,128]{1,0:T(8,128)(2,1)} %proj_ref.3), custom_call_target="tpu_custom_call" | custom-call | flops 10000000 | bytes 2097152 | tf_op jit(solution)/shard_map/prep/pallas_call | solution.py:259
  3.4 0.0 copy-start
  3.5 0.0 copy-start.4
  3.5 0.0 copy-start.1
  3.5 0.0 copy-start.2
  3.5 0.0 copy-start.3
  3.5 11.0 %all-to-all-start = ((bf16[8,272,256]{2,1,0:T(8,128)(2,1)}), bf16[8,272,256]{2,1,0:T(8,128)(2,1)S(1)}, u32[]{:S(2)}, u32[]{:S(2)}) async-start(bf16[8,272,256]{2,1,0:T(8,128)(2,1)} %get-tuple-element.16), calls=%async_computation | async-start | bytes 2228224 | tf_op jit(solution)/shard_map/kv_over_z/all_to_all | solution.py:289
  14.5 0.0 copy-done
  14.5 2.9 %collective-permute-start = (bf16[144,256]{1,0:T(8,128)(2,1)S(1)}, bf16[144,256]{1,0:T(8,128)(2,1)S(1)}, u32[]{:S(2)}, u32[]{:S(2)}) collective-permute-start(bf16[144,256]{1,0:T(8,128)(2,1)S(1)} %copy-done), channel_id=1, source_target_pairs={{0,8},{8,0},{1,9},{9,1},{2,10},{10,2},{3,11},{11,3},{4,12},{12,4},... | collective-permute-start | bytes 221192 | tf_op jit(solution)/shard_map/q_over_core/ppermute | solution.py:273
  17.4 0.0 copy-done.4
  17.4 8.4 %collective-permute-start.6 = (f32[128,128]{1,0:T(8,128)S(1)}, f32[128,128]{1,0:T(8,128)S(1)}, u32[]{:S(2)}, u32[]{:S(2)}) collective-permute-start(f32[128,128]{1,0:T(8,128)S(1)} %copy-done.4), channel_id=1, source_target_pairs={{0,3},{1,2},{2,1},{3,0},{4,7},{5,6},{6,5},{7,4},{8,11},{9,10},{10,... | collective-permute-start | bytes 196616 | tf_op jit(solution)/shard_map/coupled_over_h/ppermute | solution.py:273
  25.8 2.2 %collective-permute-start.5 = (f32[128,128]{1,0:T(8,128)S(1)}, f32[128,128]{1,0:T(8,128)S(1)}, u32[]{:S(2)}, u32[]{:S(2)}) collective-permute-start(f32[128,128]{1,0:T(8,128)S(1)} %copy-done.4), channel_id=1, source_target_pairs={{0,2},{1,3},{2,0},{3,1},{4,6},{5,7},{6,4},{7,5},{8,10},{9,11},{10,... | collective-permute-start | bytes 196616 | tf_op jit(solution)/shard_map/coupled_over_h/ppermute | solution.py:273
  28.0 2.0 %collective-permute-start.4 = (f32[128,128]{1,0:T(8,128)S(1)}, f32[128,128]{1,0:T(8,128)S(1)}, u32[]{:S(2)}, u32[]{:S(2)}) collective-permute-start(f32[128,128]{1,0:T(8,128)S(1)} %copy-done.4), channel_id=1, source_target_pairs={{0,1},{1,0},{2,3},{3,2},{4,5},{5,4},{6,7},{7,6},{8,9},{9,8},{10,11... | collective-permute-start | bytes 196616 | tf_op jit(solution)/shard_map/coupled_over_h/ppermute | solution.py:273
  29.9 0.0 collective-permute-done.recv_ref
  30.0 5.0 %collective-permute-start.3 = (bf16[2,144,256]{2,1,0:T(8,128)(2,1)S(1)}, bf16[2,144,256]{2,1,0:T(8,128)(2,1)S(1)}, u32[]{:S(2)}, u32[]{:S(2)}) collective-permute-start(bf16[2,144,256]{2,1,0:T(8,128)(2,1)S(1)} %q_over_core.1.q0_ref), channel_id=1, source_target_pairs={{0,384},{128,256},{256,128},{384,0},{1,385},{129,257},{257,129},{3... | collective-permute-start | bytes 442376 | tf_op jit(solution)/shard_map/q_over_y/ppermute | solution.py:273
  35.0 1.9 %collective-permute-start.2 = (bf16[2,144,256]{2,1,0:T(8,128)(2,1)S(1)}, bf16[2,144,256]{2,1,0:T(8,128)(2,1)S(1)}, u32[]{:S(2)}, u32[]{:S(2)}) collective-permute-start(bf16[2,144,256]{2,1,0:T(8,128)(2,1)S(1)} %q_over_core.1.q0_ref), channel_id=1, source_target_pairs={{0,256},{128,384},{256,0},{384,128},{1,257},{129,385},{257,1},{385... | collective-permute-start | bytes 442376 | tf_op jit(solution)/shard_map/q_over_y/ppermute | solution.py:273
  36.9 0.0 collective-permute-done.6
  36.9 2.3 %collective-permute-start.1 = (bf16[2,144,256]{2,1,0:T(8,128)(2,1)S(1)}, bf16[2,144,256]{2,1,0:T(8,128)(2,1)S(1)}, u32[]{:S(2)}, u32[]{:S(2)}) collective-permute-start(bf16[2,144,256]{2,1,0:T(8,128)(2,1)S(1)} %q_over_core.1.q0_ref), channel_id=1, source_target_pairs={{0,128},{128,0},{256,384},{384,256},{1,129},{129,1},{257,385},{385... | collective-permute-start | bytes 442376 | tf_op jit(solution)/shard_map/q_over_y/ppermute | solution.py:273
  39.3 0.0 collective-permute-done.5
  39.3 0.0 collective-permute-done.4
  39.3 4.6 %collective-permute-start.7 = (f32[128,128]{1,0:T(8,128)S(1)}, f32[128,128]{1,0:T(8,128)S(1)}, u32[]{:S(2)}, u32[]{:S(2)}) collective-permute-start(f32[128,128]{1,0:T(8,128)S(1)} %add_add_fusion.p0_ref), channel_id=1, source_target_pairs={{0,4},{1,5},{2,6},{3,7},{4,0},{5,1},{6,2},{7,3},{8,12},{9,13},{10,... | collective-permute-start | bytes 196616 | tf_op jit(solution)/shard_map/coupled_over_x/ppermute | solution.py:273
  43.9 1.9 %collective-permute-done.7.p1_ref = f32[128,128]{1,0:T(8,128)S(1)} collective-permute-done((f32[128,128]{1,0:T(8,128)S(1)}, f32[128,128]{1,0:T(8,128)S(1)}, u32[]{:S(2)}, u32[]{:S(2)}) %collective-permute-start.7) | collective-permute-done | bytes 65568 | tf_op jit(solution)/shard_map/coupled_over_x/ppermute | solution.py:273
  45.8 0.0 collective-permute-done.3.q3_ref
  45.8 3.7 %collective-permute-done.2.q2_ref = bf16[2,144,256]{2,1,0:T(8,128)(2,1)S(1)} collective-permute-done((bf16[2,144,256]{2,1,0:T(8,128)(2,1)S(1)}, bf16[2,144,256]{2,1,0:T(8,128)(2,1)S(1)}, u32[]{:S(2)}, u32[]{:S(2)}) %collective-permute-start.2) | collective-permute-done | bytes 147488 | tf_op jit(solution)/shard_map/q_over_y/ppermute | solution.py:273
  49.6 0.0 collective-permute-done.1.q1_ref
  49.6 0.0 all-to-all-done.kv_ref
  49.6 0.0 copy-done.1
  49.6 0.0 copy-done.2
  49.6 0.0 copy-done.3
  49.6 2.0 %stats.1 = (bf16[8,192,128]{2,1,0:T(8,128)(2,1)S(1)}, bf16[8,144,256]{2,1,0:T(8,128)(2,1)S(1)}) custom-call(bf16[2,144,256]{2,1,0:T(8,128)(2,1)S(1)} %q_over_core.1.q0_ref, bf16[2,144,256]{2,1,0:T(8,128)(2,1)S(1)} %collective-permute-done.1.q1_ref, bf16[2,144,256]{2,1,0:T(8,128)(2,1)S(1)} %collective-permute-done.2.q2_ref, ...), custom_call_target="tpu_custom_call" | custom-call | flops 1000000000 | bytes 2097152 | tf_op jit(solution)/shard_map/stats/pallas_call | solution.py:259
  51.6 15.5 %all_to_all.15.g_ref = bf16[8,192,128]{2,1,0:T(8,128)(2,1)S(1)} all-to-all(bf16[8,192,128]{2,1,0:T(8,128)(2,1)S(1)} %get-tuple-element.19), channel_id=1, replica_groups=mesh['y'=4,'z'=8,'c'=2,'x'=4,'h'=2] {'y','c'}, dimensions={0} | all-to-all | bytes 786432 | tf_op jit(solution)/shard_map/upstream_over_yc/all_to_all | solution.py:312
  67.1 5.0 %main.1 = (bf16[8,256,256]{2,1,0:T(8,128)(2,1)}, bf16[4,128,256]{2,1,0:T(8,128)(2,1)S(1)}, bf16[4,128,256]{2,1,0:T(8,128)(2,1)S(1)}) custom-call(bf16[8,144,256]{2,1,0:T(8,128)(2,1)S(1)} %get-tuple-element.18.qg_ref, bf16[8,272,256]{2,1,0:T(8,128)(2,1)S(1)} %all-to-all-done.kv_ref, bf16[8,192,128]{2,1,0:T(8,128)(2,1)S(1)} %all_to_all.15.g_ref, ...), custom_call_target="tpu_custom_call" | custom-call | flops 4000000000 | bytes 2097152 | tf_op jit(solution)/shard_map/main/pallas_call | solution.py:259
  72.1 6.9 %all-to-all-start.2 = ((bf16[8,256,256]{2,1,0:T(8,128)(2,1)}), bf16[8,256,256]{2,1,0:T(8,128)(2,1)S(1)}, u32[]{:S(2)}, u32[]{:S(2)}) async-start(bf16[8,256,256]{2,1,0:T(8,128)(2,1)} %get-tuple-element.26), calls=%async_computation.2 | async-start | bytes 2097152 | tf_op jit(solution)/shard_map/dkv_over_z/all_to_all | solution.py:321
  79.0 3.0 %collective-permute-start.8 = (bf16[4,128,256]{2,1,0:T(8,128)(2,1)S(1)}, bf16[4,128,256]{2,1,0:T(8,128)(2,1)S(1)}, u32[]{:S(2)}, u32[]{:S(2)}) collective-permute-start(bf16[4,128,256]{2,1,0:T(8,128)(2,1)S(1)} %get-tuple-element.21), channel_id=1, source_target_pairs={{0,8},{8,0},{1,9},{9,1},{2,10},{10,2},{3,11},{11,3},{4,12},{12,4},... | collective-permute-start | bytes 786440 | tf_op jit(solution)/shard_map/dq_over_core/ppermute | solution.py:273
  82.1 1.1 %collective-permute-done.8.recv_ref = bf16[4,128,256]{2,1,0:T(8,128)(2,1)S(1)} collective-permute-done((bf16[4,128,256]{2,1,0:T(8,128)(2,1)S(1)}, bf16[4,128,256]{2,1,0:T(8,128)(2,1)S(1)}, u32[]{:S(2)}, u32[]{:S(2)}) %collective-permute-start.8) | collective-permute-done | bytes 262176 | tf_op jit(solution)/shard_map/dq_over_core/ppermute | solution.py:273
  83.2 0.1 dq_over_core.1
  83.3 1.9 %collective-permute-start.9 = (bf16[128,256]{1,0:T(8,128)(2,1)S(1)}, bf16[128,256]{1,0:T(8,128)(2,1)S(1)}, u32[]{:S(2)}, u32[]{:S(2)}) collective-permute-start(bf16[128,256]{1,0:T(8,128)(2,1)S(1)} %get-tuple-element.23), channel_id=1, source_target_pairs={{0,128},{128,0},{256,384},{384,256},{1,129},{129,1},{257,385},{385... | collective-permute-start | bytes 196616 | tf_op jit(solution)/shard_map/dq_over_y/ppermute | solution.py:273
  85.2 3.2 %collective-permute-start.10 = (bf16[128,256]{1,0:T(8,128)(2,1)S(1)}, bf16[128,256]{1,0:T(8,128)(2,1)S(1)}, u32[]{:S(2)}, u32[]{:S(2)}) collective-permute-start(bf16[128,256]{1,0:T(8,128)(2,1)S(1)} %get-tuple-element.24), channel_id=1, source_target_pairs={{0,256},{128,384},{256,0},{384,128},{1,257},{129,385},{257,1},{385... | collective-permute-start | bytes 196616 | tf_op jit(solution)/shard_map/dq_over_y/ppermute | solution.py:273
  88.4 4.2 %collective-permute-start.11 = (bf16[128,256]{1,0:T(8,128)(2,1)S(1)}, bf16[128,256]{1,0:T(8,128)(2,1)S(1)}, u32[]{:S(2)}, u32[]{:S(2)}) collective-permute-start(bf16[128,256]{1,0:T(8,128)(2,1)S(1)} %get-tuple-element.25), channel_id=1, source_target_pairs={{0,384},{128,256},{256,128},{384,0},{1,385},{129,257},{257,129},{3... | collective-permute-start | bytes 196616 | tf_op jit(solution)/shard_map/dq_over_y/ppermute | solution.py:273
  92.6 0.0 collective-permute-done.9.r1_ref
  92.6 0.0 collective-permute-done.10.r2_ref
  92.6 2.9 %collective-permute-done.11.r3_ref = bf16[128,256]{1,0:T(8,128)(2,1)S(1)} collective-permute-done((bf16[128,256]{1,0:T(8,128)(2,1)S(1)}, bf16[128,256]{1,0:T(8,128)(2,1)S(1)}, u32[]{:S(2)}, u32[]{:S(2)}) %collective-permute-start.11) | collective-permute-done | bytes 65568 | tf_op jit(solution)/shard_map/dq_over_y/ppermute | solution.py:273
  95.5 12.7 %all-to-all-done.2.kv_ref = bf16[8,256,256]{2,1,0:T(8,128)(2,1)S(1)} async-done(((bf16[8,256,256]{2,1,0:T(8,128)(2,1)}), bf16[8,256,256]{2,1,0:T(8,128)(2,1)S(1)}, u32[]{:S(2)}, u32[]{:S(2)}) %all-to-all-start.2) | async-done | bytes 1048608 | tf_op jit(solution)/shard_map/dkv_over_z/all_to_all | solution.py:321
  108.2 0.8 final.1
  (2 shorter events, 0.0 us)
Async XLA Ops:
  3.4 11.1 %copy-start = (bf16[144,256]{1,0:T(8,128)(2,1)S(1)}, bf16[144,256]{1,0:T(8,128)(2,1)}, u32[]{:S(2)}) copy-start(bf16[144,256]{1,0:T(8,128)(2,1)} %get-tuple-element.15.own_ref) | copy-start | bytes 221188
  3.5 13.9 %copy-start.4 = (f32[128,128]{1,0:T(8,128)S(1)}, f32[128,128]{1,0:T(8,128)}, u32[]{:S(2)}) copy-start(f32[128,128]{1,0:T(8,128)} %get-tuple-element.17) | copy-start | bytes 196612
  3.5 46.1 %copy-start.1 = (bf16[128,256]{1,0:T(8,128)(2,1)S(1)}, bf16[128,256]{1,0:T(8,128)(2,1)}, u32[]{:S(2)}) copy-start(bf16[128,256]{1,0:T(8,128)(2,1)} %o_ref.1) | copy-start | bytes 196612
  3.5 46.1 %copy-start.2 = (bf16[256,128]{1,0:T(8,128)(2,1)S(1)}, bf16[256,128]{1,0:T(8,128)(2,1)}, u32[]{:S(2)}) copy-start(bf16[256,128]{1,0:T(8,128)(2,1)} %proj_ref.3) | copy-start | bytes 196612
  3.5 46.1 %copy-start.3 = (f32[128,64]{0,1:T(8,128)S(1)}, f32[128,64]{0,1:T(8,128)}, u32[]{:S(2)}) copy-start(f32[128,64]{0,1:T(8,128)} %param.7) | copy-start | bytes 98308
  3.5 46.1 %all-to-all-start = ((bf16[8,272,256]{2,1,0:T(8,128)(2,1)}), bf16[8,272,256]{2,1,0:T(8,128)(2,1)S(1)}, u32[]{:S(2)}, u32[]{:S(2)}) async-start(bf16[8,272,256]{2,1,0:T(8,128)(2,1)} %get-tuple-element.16), calls=%async_computation | async-start | bytes 2228224 | tf_op jit(solution)/shard_map/kv_over_z/all_to_all | solution.py:289
  14.5 15.4 %collective-permute-start = (bf16[144,256]{1,0:T(8,128)(2,1)S(1)}, bf16[144,256]{1,0:T(8,128)(2,1)S(1)}, u32[]{:S(2)}, u32[]{:S(2)}) collective-permute-start(bf16[144,256]{1,0:T(8,128)(2,1)S(1)} %copy-done), channel_id=1, source_target_pairs={{0,8},{8,0},{1,9},{9,1},{2,10},{10,2},{3,11},{11,3},{4,12},{12,4},... | collective-permute-start | bytes 221192 | tf_op jit(solution)/shard_map/q_over_core/ppermute | solution.py:273
  17.4 19.5 %collective-permute-start.6 = (f32[128,128]{1,0:T(8,128)S(1)}, f32[128,128]{1,0:T(8,128)S(1)}, u32[]{:S(2)}, u32[]{:S(2)}) collective-permute-start(f32[128,128]{1,0:T(8,128)S(1)} %copy-done.4), channel_id=1, source_target_pairs={{0,3},{1,2},{2,1},{3,0},{4,7},{5,6},{6,5},{7,4},{8,11},{9,10},{10,... | collective-permute-start | bytes 196616 | tf_op jit(solution)/shard_map/coupled_over_h/ppermute | solution.py:273
  25.8 13.5 %collective-permute-start.5 = (f32[128,128]{1,0:T(8,128)S(1)}, f32[128,128]{1,0:T(8,128)S(1)}, u32[]{:S(2)}, u32[]{:S(2)}) collective-permute-start(f32[128,128]{1,0:T(8,128)S(1)} %copy-done.4), channel_id=1, source_target_pairs={{0,2},{1,3},{2,0},{3,1},{4,6},{5,7},{6,4},{7,5},{8,10},{9,11},{10,... | collective-permute-start | bytes 196616 | tf_op jit(solution)/shard_map/coupled_over_h/ppermute | solution.py:273
  28.0 11.3 %collective-permute-start.4 = (f32[128,128]{1,0:T(8,128)S(1)}, f32[128,128]{1,0:T(8,128)S(1)}, u32[]{:S(2)}, u32[]{:S(2)}) collective-permute-start(f32[128,128]{1,0:T(8,128)S(1)} %copy-done.4), channel_id=1, source_target_pairs={{0,1},{1,0},{2,3},{3,2},{4,5},{5,4},{6,7},{7,6},{8,9},{9,8},{10,11... | collective-permute-start | bytes 196616 | tf_op jit(solution)/shard_map/coupled_over_h/ppermute | solution.py:273
  30.0 15.9 %collective-permute-start.3 = (bf16[2,144,256]{2,1,0:T(8,128)(2,1)S(1)}, bf16[2,144,256]{2,1,0:T(8,128)(2,1)S(1)}, u32[]{:S(2)}, u32[]{:S(2)}) collective-permute-start(bf16[2,144,256]{2,1,0:T(8,128)(2,1)S(1)} %q_over_core.1.q0_ref), channel_id=1, source_target_pairs={{0,384},{128,256},{256,128},{384,0},{1,385},{129,257},{257,129},{3... | collective-permute-start | bytes 442376 | tf_op jit(solution)/shard_map/q_over_y/ppermute | solution.py:273
  35.0 14.6 %collective-permute-start.2 = (bf16[2,144,256]{2,1,0:T(8,128)(2,1)S(1)}, bf16[2,144,256]{2,1,0:T(8,128)(2,1)S(1)}, u32[]{:S(2)}, u32[]{:S(2)}) collective-permute-start(bf16[2,144,256]{2,1,0:T(8,128)(2,1)S(1)} %q_over_core.1.q0_ref), channel_id=1, source_target_pairs={{0,256},{128,384},{256,0},{384,128},{1,257},{129,385},{257,1},{385... | collective-permute-start | bytes 442376 | tf_op jit(solution)/shard_map/q_over_y/ppermute | solution.py:273
  36.9 12.6 %collective-permute-start.1 = (bf16[2,144,256]{2,1,0:T(8,128)(2,1)S(1)}, bf16[2,144,256]{2,1,0:T(8,128)(2,1)S(1)}, u32[]{:S(2)}, u32[]{:S(2)}) collective-permute-start(bf16[2,144,256]{2,1,0:T(8,128)(2,1)S(1)} %q_over_core.1.q0_ref), channel_id=1, source_target_pairs={{0,128},{128,0},{256,384},{384,256},{1,129},{129,1},{257,385},{385... | collective-permute-start | bytes 442376 | tf_op jit(solution)/shard_map/q_over_y/ppermute | solution.py:273
  39.3 6.5 %collective-permute-start.7 = (f32[128,128]{1,0:T(8,128)S(1)}, f32[128,128]{1,0:T(8,128)S(1)}, u32[]{:S(2)}, u32[]{:S(2)}) collective-permute-start(f32[128,128]{1,0:T(8,128)S(1)} %add_add_fusion.p0_ref), channel_id=1, source_target_pairs={{0,4},{1,5},{2,6},{3,7},{4,0},{5,1},{6,2},{7,3},{8,12},{9,13},{10,... | collective-permute-start | bytes 196616 | tf_op jit(solution)/shard_map/coupled_over_x/ppermute | solution.py:273
  72.1 36.1 %all-to-all-start.2 = ((bf16[8,256,256]{2,1,0:T(8,128)(2,1)}), bf16[8,256,256]{2,1,0:T(8,128)(2,1)S(1)}, u32[]{:S(2)}, u32[]{:S(2)}) async-start(bf16[8,256,256]{2,1,0:T(8,128)(2,1)} %get-tuple-element.26), calls=%async_computation.2 | async-start | bytes 2097152 | tf_op jit(solution)/shard_map/dkv_over_z/all_to_all | solution.py:321
  79.0 4.2 %collective-permute-start.8 = (bf16[4,128,256]{2,1,0:T(8,128)(2,1)S(1)}, bf16[4,128,256]{2,1,0:T(8,128)(2,1)S(1)}, u32[]{:S(2)}, u32[]{:S(2)}) collective-permute-start(bf16[4,128,256]{2,1,0:T(8,128)(2,1)S(1)} %get-tuple-element.21), channel_id=1, source_target_pairs={{0,8},{8,0},{1,9},{9,1},{2,10},{10,2},{3,11},{11,3},{4,12},{12,4},... | collective-permute-start | bytes 786440 | tf_op jit(solution)/shard_map/dq_over_core/ppermute | solution.py:273
  83.3 9.3 %collective-permute-start.9 = (bf16[128,256]{1,0:T(8,128)(2,1)S(1)}, bf16[128,256]{1,0:T(8,128)(2,1)S(1)}, u32[]{:S(2)}, u32[]{:S(2)}) collective-permute-start(bf16[128,256]{1,0:T(8,128)(2,1)S(1)} %get-tuple-element.23), channel_id=1, source_target_pairs={{0,128},{128,0},{256,384},{384,256},{1,129},{129,1},{257,385},{385... | collective-permute-start | bytes 196616 | tf_op jit(solution)/shard_map/dq_over_y/ppermute | solution.py:273
  85.2 7.4 %collective-permute-start.10 = (bf16[128,256]{1,0:T(8,128)(2,1)S(1)}, bf16[128,256]{1,0:T(8,128)(2,1)S(1)}, u32[]{:S(2)}, u32[]{:S(2)}) collective-permute-start(bf16[128,256]{1,0:T(8,128)(2,1)S(1)} %get-tuple-element.24), channel_id=1, source_target_pairs={{0,256},{128,384},{256,0},{384,128},{1,257},{129,385},{257,1},{385... | collective-permute-start | bytes 196616 | tf_op jit(solution)/shard_map/dq_over_y/ppermute | solution.py:273
  88.4 7.1 %collective-permute-start.11 = (bf16[128,256]{1,0:T(8,128)(2,1)S(1)}, bf16[128,256]{1,0:T(8,128)(2,1)S(1)}, u32[]{:S(2)}, u32[]{:S(2)}) collective-permute-start(bf16[128,256]{1,0:T(8,128)(2,1)S(1)} %get-tuple-element.25), channel_id=1, source_target_pairs={{0,384},{128,256},{256,128},{384,0},{1,385},{129,257},{257,129},{3... | collective-permute-start | bytes 196616 | tf_op jit(solution)/shard_map/dq_over_y/ppermute | solution.py:273

commit v5 on v2

--- a/solution.py
+++ b/solution.py
@@ -19,6 +19,7 @@
 NT = (((1,), (1,)), ((), ()))
 MIB = 1 << 20
 JOIN_COST = 1_000_000
+PAIR_COST = 2_000_000_000
 FOLD_COST = 20_000_000_000
 
 
@@ -86,7 +87,11 @@
     return part.reshape(part.shape[0] * SPAN, HEAD)
 
 
-def stats_kernel(qg_ref, kva_ref, kvb_ref, out_ref, s_ref, st_ref):
+def stats_kernel(
+    qg_ref, kva_ref, kvb_ref, p0_ref, p1_ref, p2_ref, p3_ref, lat_ref, proj_ref, o_ref,
+    out_ref, prob_ref, top_ref, s_ref, tail_ref,
+):
+    tail_ref[...] = jnp.zeros((48, 128), F32)
     q_early, q_late = query_positions(qg_ref)
     sides = (kva_ref, kvb_ref)
     for head in range(2):
@@ -106,115 +111,114 @@
                 s_ref[slot] = s
                 here = jnp.max(s.reshape(32, 8, 512), axis=0)
                 top = here if top is None else jnp.maximum(top, here)
-            top = jnp.max(top, axis=0, keepdims=True).astype(BF16).astype(F32)
+            top = jnp.max(top, axis=0, keepdims=True)
             total = jnp.zeros((8, 512), F32)
             for slot, kv, start, masked in units:
                 p = jnp.exp2(s_ref[slot] - top)
                 total = total + jnp.sum(p.reshape(32, 8, 512), axis=0)
+                rows = slice(slot * 256, (slot + 1) * 256)
+                prob_ref[head, rows, part * 512 : (part + 1) * 512] = p.astype(BF16)
             total = jnp.sum(total, axis=0, keepdims=True)
-            high = total.astype(BF16).astype(F32)
-            low = total - high
-            base = (head * 2 + part) * 12
+            lse = top + jnp.log(total) * LOG2E
+            high = lse.astype(BF16).astype(F32)
+            low = lse - high
+            group = head * 2 + part
             for r in range(4):
                 lanes = slice(r * 128, (r + 1) * 128)
-                st_ref[base + r : base + r + 1, :] = top[:, lanes]
-                st_ref[base + 4 + r : base + 5 + r, :] = high[:, lanes]
-                st_ref[base + 8 + r : base + 9 + r, :] = low[:, lanes]
-    out_ref[...] = st_ref[...].astype(BF16)
-
-
-def join_kernel(own_ref, r1_ref, r2_ref, r3_ref, total_ref, recv_ref, kv_ref, sum_ref):
-    for n, ref in enumerate((own_ref, r1_ref, r2_ref, r3_ref)):
-        kv_ref[n] = ref[...]
-    sum_ref[...] = total_ref[...] + recv_ref[...]
-
-
-def pack_kernel(total_ref, recv_ref, lat_ref, proj_ref, o_ref, st_ref, out_ref, d_ref):
-    coupled = total_ref[...] + recv_ref[...]
+                top_ref[group * 4 + r : group * 4 + r + 1, :] = top[:, lanes]
+                row = 8 + group * 8 + r
+                tail_ref[row : row + 1, :] = high[:, lanes]
+                tail_ref[row + 4 : row + 5, :] = low[:, lanes]
+    coupled = (p0_ref[...] + p1_ref[...]) + (p2_ref[...] + p3_ref[...])
     shifts = coupled[:, 0:64]
     log_scale = coupled[:, 64:128]
     damping = jnp.exp(-log_scale)
     normed = (lat_ref[...].T - shifts) * damping
     upstream = jnp.concatenate([-normed * damping, 1.0 - normed * normed], axis=1).astype(BF16)
-    d_ref[...] = jnp.zeros((16, 128), F32)
     for head in range(2):
         cols = slice(head * HEAD, (head + 1) * HEAD)
         grad = dot_nt(upstream, proj_ref[cols, :]).astype(BF16)
         product = grad.astype(F32) * o_ref[:, cols].astype(F32)
         delta = jnp.sum(product.T, axis=0, keepdims=True)
         high = delta.astype(BF16).astype(F32)
-        d_ref[2 * head : 2 * head + 1, :] = high
-        d_ref[2 * head + 1 : 2 * head + 2, :] = delta - high
-    deltas = d_ref[...].astype(BF16)
-    stats = st_ref[...]
+        tail_ref[2 * head : 2 * head + 1, :] = high
+        tail_ref[2 * head + 1 : 2 * head + 2, :] = delta - high
+    tail = tail_ref[...].astype(BF16)
     for i in range(NZ):
         out_ref[i, 0:128, :] = upstream
-        out_ref[i, 128:144, :] = deltas
-        out_ref[i, 144:192, :] = stats
-
-
-def main_kernel(qg_ref, kva_ref, kvb_ref, g_ref, proj_ref, dq_ref, da_ref, db_ref, ds_ref):
-    q_early, q_late = query_positions(qg_ref)
-    lane = lax.broadcasted_iota(jnp.int32, (1, 128), 1)
-    low = lane < SPAN
+        out_ref[i, 128:176, :] = tail
+
+
+def pair_kernel(own_ref, far_ref, after_ref, out_ref):
+    out_ref[0] = own_ref[...]
+    out_ref[1] = far_ref[...]
+
+
+def join_kernel(own_ref, recv_ref, *refs):
+    kv_ref = refs[-1]
+    for n in range(2):
+        kv_ref[2 * n] = own_ref[n]
+        kv_ref[2 * n + 1] = recv_ref[n]
+
+
+def main_kernel(
+    qg_ref, kva_ref, kvb_ref, g_ref, proj_ref, prob_ref, top_ref, dq_ref, da_ref, db_ref, ds_ref
+):
+    low = lax.broadcasted_iota(jnp.int32, (1, 128), 1) < SPAN
     upstream = [
         g_ref[:, part * SPAN : (part + 1) * SPAN, :].reshape(NZ * SPAN, HEAD) for part in range(2)
     ]
-    tails = [g_ref[i, 128:144, :].astype(F32) for i in range(NZ)]
-    turned = [pltpu.roll(t, SPAN, 1) for t in tails]
-    stats = g_ref[:, 144:192, :].astype(F32)
+    tails = g_ref[:, 128:176, :].astype(F32)
+    deltas = [tails[i, 0:8, :] for i in range(NZ)]
+    turned = [pltpu.roll(t, SPAN, 1) for t in deltas]
     sides = (kva_ref, kvb_ref)
     grads = (da_ref, db_ref)
     for head in range(2):
         cols = slice(head * HEAD, (head + 1) * HEAD)
         proj = proj_ref[cols, :]
-        lse, delta, q, dout = [], [], [], []
+        delta, q, dout = [], [], []
         for part in range(2):
-            base = (head * 2 + part) * 12
-            tops = stats[:, base : base + 4, :]
-            sums = stats[:, base + 4 : base + 8, :] + stats[:, base + 8 : base + 12, :]
-            top = jnp.max(tops, axis=0)
-            total = jnp.sum(sums * jnp.exp2(tops - top[None]), axis=0)
-            value = top + jnp.log(total) * LOG2E
-            lse.append(jnp.concatenate([value[r : r + 1, :] for r in range(4)], axis=1))
-            pieces = []
+            group = head * 2 + part
+            row = 8 + group * 8
+            partial = tails[:, row : row + 4, :] + tails[:, row + 4 : row + 8, :]
+            top = jnp.max(partial, axis=0)
+            total = jnp.sum(jnp.exp2(partial - top[None]), axis=0)
+            lse = top + jnp.log(total) * LOG2E
+            weight = jnp.exp2(top_ref[group * 4 : group * 4 + 4, :] - lse)
+            lanes, column = [], []
             for p in range(NZ // 2):
-                left = (tails if part == 0 else turned)[2 * p]
-                right = (turned if part == 0 else tails)[2 * p + 1]
+                left = (deltas if part == 0 else turned)[2 * p]
+                right = (turned if part == 0 else deltas)[2 * p + 1]
                 both = jnp.where(low, left, right)
-                pieces.append(both[2 * head : 2 * head + 1, :] + both[2 * head + 1 : 2 * head + 2, :])
-            delta.append(jnp.concatenate(pieces, axis=1))
+                here = both[2 * head : 2 * head + 1, :] + both[2 * head + 1 : 2 * head + 2, :]
+                lanes.append(here * weight[p : p + 1, :])
+                column.append(jnp.broadcast_to(weight[p : p + 1, :], (128, 128)).T)
+            delta.append(jnp.concatenate(lanes, axis=1))
             q.append(rows_of(qg_ref, part * SPAN, head))
-            dout.append(dot_nt(upstream[part], proj).astype(BF16))
-
-        def unit(keys, values, kp, part):
-            t = dot_nt(keys, q[part]) * SCALE - lse[part]
-            if kp is not None:
-                t = jnp.where(kp <= (q_late if part else q_early), t, MASKED)
-            p = jnp.exp2(t)
-            ds = p * (dot_nt(values, dout[part]) - delta[part])
-            return p.astype(BF16), ds.astype(BF16)
+            grad = dot_nt(upstream[part], proj).astype(BF16).astype(F32)
+            dout.append((grad * jnp.concatenate(column, axis=0)).astype(BF16))
+        q_all = jnp.concatenate(q, axis=0)
+        dout_all = jnp.concatenate(dout, axis=0)
+
+        def unit(rows, part, values):
+            span = slice(part * 512, (part + 1) * 512)
+            p = prob_ref[head, rows, span].astype(F32)
+            ds_ref[rows, span] = (p * (dot_nt(values, dout[part]) - delta[part])).astype(BF16)
 
         for n in range(2):
             kv, grad = sides[n], grads[n]
-            keys = rows_of(kv, 0, head)
+            rows = slice(n * 256, (n + 1) * 256)
             values = rows_of(kv, 128, head)
-            pe, se = unit(keys, values, key_positions(kv, False), 0)
-            ds_ref[n * 256 : (n + 1) * 256, 0:512] = se
-            dv = dot(pe, dout[0])
-            dk = dot(se, q[0])
-            pd, sd = unit(keys, values, None, 1)
-            ds_ref[n * 256 : (n + 1) * 256, 512:1024] = sd
-            dv = dv + dot(pd, dout[1])
-            dk = dk + dot(sd, q[1])
+            unit(rows, 0, values)
+            unit(rows, 1, values)
+            dv = dot(prob_ref[head, rows, :], dout_all)
+            dk = dot(ds_ref[rows, :], q_all)
             grad[:, 0:64, cols] = (dk * FACTOR).astype(BF16).reshape(NY, SPAN, HEAD)
             grad[:, 128:192, cols] = dv.astype(BF16).reshape(NY, SPAN, HEAD)
-            keys = rows_of(kv, 64, head)
-            values = rows_of(kv, 192, head)
-            pd, sd = unit(keys, values, key_positions(kv, True), 1)
-            ds_ref[512 + n * 256 : 512 + (n + 1) * 256, 512:1024] = sd
-            dv = dot(pd, dout[1])
-            dk = dot(sd, q[1])
+            rows = slice(512 + n * 256, 512 + (n + 1) * 256)
+            unit(rows, 1, rows_of(kv, 192, head))
+            dv = dot(prob_ref[head, rows, 512:1024], dout[1])
+            dk = dot(ds_ref[rows, 512:1024], q[1])
             grad[:, 64:128, cols] = (dk * FACTOR).astype(BF16).reshape(NY, SPAN, HEAD)
             grad[:, 192:256, cols] = dv.astype(BF16).reshape(NY, SPAN, HEAD)
         early_t = jnp.concatenate([rows_of(kv, 0, head) for kv in sides], axis=0).T
@@ -275,33 +279,32 @@
             [pl.BlockSpec(memory_space=pltpu.SMEM)] + [pl.BlockSpec(memory_space=pltpu.HBM)] * 5,
             limit=62,
         )(positions, queries, keys, values, attention_out, projection)
-    with jax.named_scope("kv_over_y"):
-        arrived = [swap(kvpay, "y", NY, k) for k in (1, 2, 3)]
+    with jax.named_scope("q_over_z"):
+        qg = lax.all_to_all(qpay, "z", 0, 0)
     with jax.named_scope("coupled_over_h"):
         total = total + swap(total, "h", n_h, 1) if n_h > 1 else total
     with jax.named_scope("coupled_over_x"):
-        first = swap(total, "x", n_x, 1) if n_x > 1 else jnp.zeros_like(total)
-    with jax.named_scope("q_over_z"):
-        qg = lax.all_to_all(qpay, "z", 0, 0)
+        if n_x > 1:
+            parts = [swap(total, "x", n_x, k) for k in (1, 2, 3)]
+        else:
+            parts = [jnp.zeros_like(total)] * 3
+    with jax.named_scope("kv_over_y"):
+        (pair,) = call(pair_kernel, [((2, 272, 256), BF16)], PAIR_COST)(
+            kvpay, swap(kvpay, "y", NY, 2), total
+        )
+        other = swap(pair, "y", NY, 1)
     with jax.named_scope("join"):
-        kva, total = call(
-            join_kernel, [((NY, 272, 256), BF16), ((128, 128), F32)], JOIN_COST
-        )(kvpay, *arrived, total, first)
-    with jax.named_scope("coupled_over_x"):
-        second = swap(total, "x", n_x, 2) if n_x > 1 else jnp.zeros_like(total)
+        (kva,) = call(join_kernel, [((NY, 272, 256), BF16)], JOIN_COST)(pair, other, *parts)
     with jax.named_scope("kv_over_core"):
         kvb = swap(kva, "c", NC, 1)
     with jax.named_scope("stats"):
-        (stats,) = call(
+        pay, prob, top = call(
             stats_kernel,
-            [((48, 128), BF16)],
+            [((NZ, 176, 128), BF16), ((2, 1024, 1024), BF16), ((16, 128), F32)],
             1_000_000_000,
             [pltpu.VMEM((4, 256, 512), F32), pltpu.VMEM((48, 128), F32)],
-        )(qg, kva, kvb)
-    with jax.named_scope("pack"):
-        (pay,) = call(
-            pack_kernel, [((NZ, 192, 128), BF16)], 10_000_000, [pltpu.VMEM((16, 128), F32)]
-        )(total, second, latent.T, projection, attention_out, stats)
+            limit=24,
+        )(qg, kva, kvb, total, *parts, latent.T, projection, attention_out)
     with jax.named_scope("upstream_over_z"):
         gathered = lax.all_to_all(pay, "z", 0, 0)
     with jax.named_scope("main"):
@@ -310,14 +313,15 @@
             [((NZ, 128, 256), BF16), ((NY, 256, 256), BF16), ((NY, 256, 256), BF16)],
             4_000_000_000,
             [pltpu.VMEM((1024, 1024), BF16)],
-        )(qg, kva, kvb, gathered, projection)
+            limit=24,
+        )(qg, kva, kvb, gathered, projection, prob, top)
     with jax.named_scope("dkv_over_core"):
         other = swap(db, "c", NC, 1)
         own, *send = call(
             fold_kernel, [((256, 256), F32)] + [((256, 256), BF16)] * 3, FOLD_COST
         )(da, other)
     with jax.named_scope("dkv_over_y"):
-        back = [swap(s, "y", NY, k) for k, s in zip((1, 2, 3), send)]
+        back = [swap(s, "y", NY, k) for k, s in zip((3, 2, 1), (send[2], send[1], send[0]))]
     with jax.named_scope("dq_over_z"):
         dqs = lax.all_to_all(dq, "z", 0, 0)
     with jax.named_scope("final"):

time: 106 us -> 101 us (0.953)
  starting transfers between devices: 60 us -> 53.8 us
    ppermute x11, starting transfers between devices: 45.5 us -> 40.3 us  [swap(): return lax.ppermute(x, axis, [(i, i ^ k) for i in range(size)])]
    all_to_all x1, waiting for transfers between devices: 0.01 us -> 2.63 us  [local(): dqs = lax.all_to_all(dq, 'z', 0, 0)]
    ppermute x11, waiting for transfers between devices: 12.6 us -> 10.4 us  [swap(): return lax.ppermute(x, axis, [(i, i ^ k) for i in range(size)])]
  transfers between devices with their start and end apart: 13 -> 13, of which waited for: 4 -> 5; matrix products, arithmetic and copies ran while one was open for 0% -> 1% of each run, Pallas kernels for 2% -> 0%
where the time goes in v5:
time: 101 us; the launch traced here: 100 us
  starting transfers between devices  53.8 us (53%)
  blocking collectives  20.9 us (21%)
  waiting for transfers between devices  13 us (13%)
  Pallas kernels  10.1 us (10%)
    ppermute x11, starting transfers between devices, swap(): return lax.ppermute(x, axis, [(i, i ^ k) for i in range(size)])  40.3 us
    all_to_all x1, blocking collectives, local(): gathered = lax.all_to_all(pay, 'z', 0, 0)  20.9 us
    ppermute x11, waiting for transfers between devices, swap(): return lax.ppermute(x, axis, [(i, i ^ k) for i in range(size)])  10.4 us
    pallas_call x7, Pallas kernels, run(): pl.pallas_call(kernel, out_shape=[jax.ShapeDtypeStruct(s, d) for s, d in...  10.1 us
    all_to_all x1, starting transfers between devices, local(): qg = lax.all_to_all(qpay, 'z', 0, 0)  10 us
    all_to_all x1, starting transfers between devices, local(): dqs = lax.all_to_all(dq, 'z', 0, 0)  3.5 us
    all_to_all x1, waiting for transfers between devices, local(): dqs = lax.all_to_all(dq, 'z', 0, 0)  2.63 us
  transfers between devices with their start and end apart: 13, of which 5 were waited for; matrix products, arithmetic and copies ran while one was open for 1% of the time, Pallas kernels for 0%

profile of v5, /device:TPU:1, one launch (start us, length us, event | category | flops | bytes accessed | tf_op | source)
XLA Modules:
  0.0 100.5 jit_solution(9655402256051505116)
XLA Ops:
  0.6 2.6 %prep.1 = (bf16[8,144,256]{2,1,0:T(8,128)(2,1)}, bf16[272,256]{1,0:T(8,128)(2,1)}, f32[128,128]{1,0:T(8,128)}) custom-call(s32[128]{0:T(128)} %pos_ref.1, bf16[128,256]{1,0:T(8,128)(2,1)} %q_hbm.1, bf16[128,256]{1,0:T(8,128)(2,1)} %k_hbm.1, bf16[128,256]{1,0:T(8,128)(2,1)} %v_hbm.1, bf16[128,256]{1,0:T(8,128)(2,1)} %o_ref.1, bf16[256,128]{1,0:T(8,128)(2,1)} %proj_ref.3), custom_call_target="tpu_custom_call" | custom-call | flops 10000000 | bytes 2097152 | tf_op jit(solution)/shard_map/prep/pallas_call | solution.py:254
  3.2 5.0 %collective-permute-start = (bf16[272,256]{1,0:T(8,128)(2,1)}, bf16[272,256]{1,0:T(8,128)(2,1)S(1)}, u32[]{:S(2)}, u32[]{:S(2)}) collective-permute-start(bf16[272,256]{1,0:T(8,128)(2,1)} %get-tuple-element.17.own_ref), channel_id=1, source_target_pairs={{0,256},{128,384},{256,0},{384,128},{1,257},{129,385},{257,1},{385... | collective-permute-start | bytes 417800 | tf_op jit(solution)/shard_map/kv_over_y/ppermute | solution.py:268
  8.3 5.7 %collective-permute-start.1 = (f32[128,128]{1,0:T(8,128)}, f32[128,128]{1,0:T(8,128)S(1)}, u32[]{:S(2)}, u32[]{:S(2)}) collective-permute-start(f32[128,128]{1,0:T(8,128)} %get-tuple-element.18), channel_id=1, source_target_pairs={{0,1},{1,0},{2,3},{3,2},{4,5},{5,4},{6,7},{7,6},{8,9},{9,8},{10,11... | collective-permute-start | bytes 196616 | tf_op jit(solution)/shard_map/coupled_over_h/ppermute | solution.py:268
  13.9 10.0 %all-to-all-start = ((bf16[8,144,256]{2,1,0:T(8,128)(2,1)}), bf16[8,144,256]{2,1,0:T(8,128)(2,1)S(1)}, u32[]{:S(2)}, u32[]{:S(2)}) async-start(bf16[8,144,256]{2,1,0:T(8,128)(2,1)} %get-tuple-element.16), calls=%async_computation | async-start | bytes 1179648 | tf_op jit(solution)/shard_map/q_over_z/all_to_all | solution.py:283
  24.0 0.0 collective-permute-done.1
  24.0 0.9 add.3.after_ref.p0_ref
  24.8 0.0 copy-start
  24.8 0.0 copy-start.1
  24.8 0.0 collective-permute-done.far_ref
  24.8 0.0 copy-start.2
  24.9 0.9 copy-done.2
  25.8 0.0 copy-start.3
  25.8 2.3 %collective-permute-start.2 = (bf16[2,272,256]{2,1,0:T(8,128)(2,1)S(1)}, bf16[2,272,256]{2,1,0:T(8,128)(2,1)S(1)}, u32[]{:S(2)}, u32[]{:S(2)}) collective-permute-start(bf16[2,272,256]{2,1,0:T(8,128)(2,1)S(1)} %kv_over_y.1.own_ref), channel_id=1, source_target_pairs={{0,128},{128,0},{256,384},{384,256},{1,129},{129,1},{257,385},{385... | collective-permute-start | bytes 835592 | tf_op jit(solution)/shard_map/kv_over_y/ppermute | solution.py:268
  28.1 4.4 %collective-permute-start.5 = (f32[128,128]{1,0:T(8,128)S(1)}, f32[128,128]{1,0:T(8,128)S(1)}, u32[]{:S(2)}, u32[]{:S(2)}) collective-permute-start(f32[128,128]{1,0:T(8,128)S(1)} %add.3.after_ref.p0_ref), channel_id=1, source_target_pairs={{0,6},{2,4},{4,2},{6,0},{1,7},{3,5},{5,3},{7,1},{8,14},{10,12},{12... | collective-permute-start | bytes 196616 | tf_op jit(solution)/shard_map/coupled_over_x/ppermute | solution.py:268
  32.5 2.4 %collective-permute-start.4 = (f32[128,128]{1,0:T(8,128)S(1)}, f32[128,128]{1,0:T(8,128)S(1)}, u32[]{:S(2)}, u32[]{:S(2)}) collective-permute-start(f32[128,128]{1,0:T(8,128)S(1)} %add.3.after_ref.p0_ref), channel_id=1, source_target_pairs={{0,4},{2,6},{4,0},{6,2},{1,5},{3,7},{5,1},{7,3},{8,12},{10,14},{12... | collective-permute-start | bytes 196616 | tf_op jit(solution)/shard_map/coupled_over_x/ppermute | solution.py:268
  35.0 2.2 %collective-permute-start.3 = (f32[128,128]{1,0:T(8,128)S(1)}, f32[128,128]{1,0:T(8,128)S(1)}, u32[]{:S(2)}, u32[]{:S(2)}) collective-permute-start(f32[128,128]{1,0:T(8,128)S(1)} %add.3.after_ref.p0_ref), channel_id=1, source_target_pairs={{0,2},{2,0},{4,6},{6,4},{1,3},{3,1},{5,7},{7,5},{8,10},{10,8},{12,... | collective-permute-start | bytes 196616 | tf_op jit(solution)/shard_map/coupled_over_x/ppermute | solution.py:268
  37.1 0.0 collective-permute-done.5.refs_2_.p3_ref
  37.1 1.9 %collective-permute-done.4.refs_1_.p2_ref = f32[128,128]{1,0:T(8,128)S(1)} collective-permute-done((f32[128,128]{1,0:T(8,128)S(1)}, f32[128,128]{1,0:T(8,128)S(1)}, u32[]{:S(2)}, u32[]{:S(2)}) %collective-permute-start.4) | collective-permute-done | bytes 65568 | tf_op jit(solution)/shard_map/coupled_over_x/ppermute | solution.py:268
  39.0 1.0 %collective-permute-done.3.refs_0_.p1_ref = f32[128,128]{1,0:T(8,128)S(1)} collective-permute-done((f32[128,128]{1,0:T(8,128)S(1)}, f32[128,128]{1,0:T(8,128)S(1)}, u32[]{:S(2)}, u32[]{:S(2)}) %collective-permute-start.3) | collective-permute-done | bytes 65568 | tf_op jit(solution)/shard_map/coupled_over_x/ppermute | solution.py:268
  40.1 0.0 collective-permute-done.2.recv_ref
  40.1 5.3 %collective-permute-start.6 = (bf16[4,272,256]{2,1,0:T(8,128)(2,1)S(1)}, bf16[4,272,256]{2,1,0:T(8,128)(2,1)S(1)}, u32[]{:S(2)}, u32[]{:S(2)}) collective-permute-start(bf16[4,272,256]{2,1,0:T(8,128)(2,1)S(1)} %join.1.kva_ref), channel_id=1, source_target_pairs={{0,8},{8,0},{1,9},{9,1},{2,10},{10,2},{3,11},{11,3},{4,12},{12,4},... | collective-permute-start | bytes 1671176 | tf_op jit(solution)/shard_map/kv_over_core/ppermute | solution.py:268
  45.4 1.6 %collective-permute-done.6.kvb_ref = bf16[4,272,256]{2,1,0:T(8,128)(2,1)S(1)} collective-permute-done((bf16[4,272,256]{2,1,0:T(8,128)(2,1)S(1)}, bf16[4,272,256]{2,1,0:T(8,128)(2,1)S(1)}, u32[]{:S(2)}, u32[]{:S(2)}) %collective-permute-start.6) | collective-permute-done | bytes 557088 | tf_op jit(solution)/shard_map/kv_over_core/ppermute | solution.py:268
  47.0 0.0 all-to-all-done.qg_ref
  47.0 0.0 copy-done
  47.0 0.0 copy-done.1
  47.0 0.0 copy-done.3
  47.0 2.3 %stats.1 = (bf16[8,176,128]{2,1,0:T(8,128)(2,1)S(1)}, bf16[2,1024,1024]{2,1,0:T(8,128)(2,1)S(1)}, f32[16,128]{1,0:T(8,128)S(1)}) custom-call(bf16[8,144,256]{2,1,0:T(8,128)(2,1)S(1)} %all-to-all-done.qg_ref, bf16[4,272,256]{2,1,0:T(8,128)(2,1)S(1)} %join.1.kva_ref, bf16[4,272,256]{2,1,0:T(8,128)(2,1)S(1)} %collective-permute-done.6.kvb_ref, ...), custom_call_target="tpu_custom_call" | custom-call | flops 1000000000 | bytes 2097152 | tf_op jit(solution)/shard_map/stats/pallas_call | solution.py:254
  49.3 20.9 %all_to_all.15.g_ref = bf16[8,176,128]{2,1,0:T(8,128)(2,1)S(1)} all-to-all(bf16[8,176,128]{2,1,0:T(8,128)(2,1)S(1)} %get-tuple-element.19), channel_id=1, replica_groups=mesh['y'=4,'z'=8,'c'=2,'x'=4,'h'=2] {'z'}, dimensions={0} | all-to-all | bytes 720896 | tf_op jit(solution)/shard_map/upstream_over_z/all_to_all | solution.py:309
  70.2 4.3 %main.1 = (bf16[8,128,256]{2,1,0:T(8,128)(2,1)}, bf16[4,256,256]{2,1,0:T(8,128)(2,1)S(1)}, bf16[4,256,256]{2,1,0:T(8,128)(2,1)S(1)}) custom-call(bf16[8,144,256]{2,1,0:T(8,128)(2,1)S(1)} %all-to-all-done.qg_ref, bf16[4,272,256]{2,1,0:T(8,128)(2,1)S(1)} %join.1.kva_ref, bf16[4,272,256]{2,1,0:T(8,128)(2,1)S(1)} %collective-permute-done.6.kvb_ref, ...), custom_call_target="tpu_custom_call" | custom-call | flops 4000000000 | bytes 2097152 | tf_op jit(solution)/shard_map/main/pallas_call | solution.py:254
  74.5 3.7 %collective-permute-start.7 = (bf16[4,256,256]{2,1,0:T(8,128)(2,1)S(1)}, bf16[4,256,256]{2,1,0:T(8,128)(2,1)S(1)}, u32[]{:S(2)}, u32[]{:S(2)}) collective-permute-start(bf16[4,256,256]{2,1,0:T(8,128)(2,1)S(1)} %get-tuple-element.23), channel_id=1, source_target_pairs={{0,8},{8,0},{1,9},{9,1},{2,10},{10,2},{3,11},{11,3},{4,12},{12,4},... | collective-permute-start | bytes 1572872 | tf_op jit(solution)/shard_map/dkv_over_core/ppermute | solution.py:268
  78.2 3.5 %all-to-all-start.2 = ((bf16[8,128,256]{2,1,0:T(8,128)(2,1)}), bf16[8,128,256]{2,1,0:T(8,128)(2,1)S(1)}, u32[]{:S(2)}, u32[]{:S(2)}) async-start(bf16[8,128,256]{2,1,0:T(8,128)(2,1)} %get-tuple-element.28), calls=%async_computation.2 | async-start | bytes 1048576 | tf_op jit(solution)/shard_map/dq_over_z/all_to_all | solution.py:326
  81.7 0.0 collective-permute-done.7.recv_ref
  81.8 0.1 dkv_over_core.1
  81.9 3.5 %collective-permute-start.8 = (bf16[256,256]{1,0:T(8,128)(2,1)S(1)}, bf16[256,256]{1,0:T(8,128)(2,1)S(1)}, u32[]{:S(2)}, u32[]{:S(2)}) collective-permute-start(bf16[256,256]{1,0:T(8,128)(2,1)S(1)} %get-tuple-element.25), channel_id=1, source_target_pairs={{0,384},{128,256},{256,128},{384,0},{1,385},{129,257},{257,129},{3... | collective-permute-start | bytes 393224 | tf_op jit(solution)/shard_map/dkv_over_y/ppermute | solution.py:268
  85.4 1.9 %collective-permute-start.9 = (bf16[256,256]{1,0:T(8,128)(2,1)S(1)}, bf16[256,256]{1,0:T(8,128)(2,1)S(1)}, u32[]{:S(2)}, u32[]{:S(2)}) collective-permute-start(bf16[256,256]{1,0:T(8,128)(2,1)S(1)} %get-tuple-element.26), channel_id=1, source_target_pairs={{0,256},{128,384},{256,0},{384,128},{1,257},{129,385},{257,1},{385... | collective-permute-start | bytes 393224 | tf_op jit(solution)/shard_map/dkv_over_y/ppermute | solution.py:268
  87.3 3.9 %collective-permute-start.10 = (bf16[256,256]{1,0:T(8,128)(2,1)S(1)}, bf16[256,256]{1,0:T(8,128)(2,1)S(1)}, u32[]{:S(2)}, u32[]{:S(2)}) collective-permute-start(bf16[256,256]{1,0:T(8,128)(2,1)S(1)} %get-tuple-element.27), channel_id=1, source_target_pairs={{0,128},{128,0},{256,384},{384,256},{1,129},{129,1},{257,385},{385... | collective-permute-start | bytes 393224 | tf_op jit(solution)/shard_map/dkv_over_y/ppermute | solution.py:268
  91.2 0.0 collective-permute-done.8.r1_ref
  91.2 5.9 %collective-permute-done.9.r2_ref = bf16[256,256]{1,0:T(8,128)(2,1)S(1)} collective-permute-done((bf16[256,256]{1,0:T(8,128)(2,1)S(1)}, bf16[256,256]{1,0:T(8,128)(2,1)S(1)}, u32[]{:S(2)}, u32[]{:S(2)}) %collective-permute-start.9) | collective-permute-done | bytes 131104 | tf_op jit(solution)/shard_map/dkv_over_y/ppermute | solution.py:268
  97.1 0.0 collective-permute-done.10.r3_ref
  97.1 2.6 %all-to-all-done.2.dq_ref = bf16[8,128,256]{2,1,0:T(8,128)(2,1)S(1)} async-done(((bf16[8,128,256]{2,1,0:T(8,128)(2,1)}), bf16[8,128,256]{2,1,0:T(8,128)(2,1)S(1)}, u32[]{:S(2)}, u32[]{:S(2)}) %all-to-all-start.2) | async-done | bytes 524320 | tf_op jit(solution)/shard_map/dq_over_z/all_to_all | solution.py:326
  99.7 0.8 final.1
  (2 shorter events, 0.1 us)
Async XLA Ops:
  3.2 21.6 %collective-permute-start = (bf16[272,256]{1,0:T(8,128)(2,1)}, bf16[272,256]{1,0:T(8,128)(2,1)S(1)}, u32[]{:S(2)}, u32[]{:S(2)}) collective-permute-start(bf16[272,256]{1,0:T(8,128)(2,1)} %get-tuple-element.17.own_ref), channel_id=1, source_target_pairs={{0,256},{128,384},{256,0},{384,128},{1,257},{129,385},{257,1},{385... | collective-permute-start | bytes 417800 | tf_op jit(solution)/shard_map/kv_over_y/ppermute | solution.py:268
  8.3 15.7 %collective-permute-start.1 = (f32[128,128]{1,0:T(8,128)}, f32[128,128]{1,0:T(8,128)S(1)}, u32[]{:S(2)}, u32[]{:S(2)}) collective-permute-start(f32[128,128]{1,0:T(8,128)} %get-tuple-element.18), channel_id=1, source_target_pairs={{0,1},{1,0},{2,3},{3,2},{4,5},{5,4},{6,7},{7,6},{8,9},{9,8},{10,11... | collective-permute-start | bytes 196616 | tf_op jit(solution)/shard_map/coupled_over_h/ppermute | solution.py:268
  13.9 33.1 %all-to-all-start = ((bf16[8,144,256]{2,1,0:T(8,128)(2,1)}), bf16[8,144,256]{2,1,0:T(8,128)(2,1)S(1)}, u32[]{:S(2)}, u32[]{:S(2)}) async-start(bf16[8,144,256]{2,1,0:T(8,128)(2,1)} %get-tuple-element.16), calls=%async_computation | async-start | bytes 1179648 | tf_op jit(solution)/shard_map/q_over_z/all_to_all | solution.py:283
  24.8 22.2 %copy-start = (bf16[128,256]{1,0:T(8,128)(2,1)S(1)}, bf16[128,256]{1,0:T(8,128)(2,1)}, u32[]{:S(2)}) copy-start(bf16[128,256]{1,0:T(8,128)(2,1)} %o_ref.1) | copy-start | bytes 196612
  24.8 22.2 %copy-start.1 = (bf16[256,128]{1,0:T(8,128)(2,1)S(1)}, bf16[256,128]{1,0:T(8,128)(2,1)}, u32[]{:S(2)}) copy-start(bf16[256,128]{1,0:T(8,128)(2,1)} %proj_ref.3) | copy-start | bytes 196612
  24.8 0.9 copy-start.2
  25.8 21.2 %copy-start.3 = (f32[128,64]{0,1:T(8,128)S(1)}, f32[128,64]{0,1:T(8,128)}, u32[]{:S(2)}) copy-start(f32[128,64]{0,1:T(8,128)} %param.7) | copy-start | bytes 98308
  25.8 14.3 %collective-permute-start.2 = (bf16[2,272,256]{2,1,0:T(8,128)(2,1)S(1)}, bf16[2,272,256]{2,1,0:T(8,128)(2,1)S(1)}, u32[]{:S(2)}, u32[]{:S(2)}) collective-permute-start(bf16[2,272,256]{2,1,0:T(8,128)(2,1)S(1)} %kv_over_y.1.own_ref), channel_id=1, source_target_pairs={{0,128},{128,0},{256,384},{384,256},{1,129},{129,1},{257,385},{385... | collective-permute-start | bytes 835592 | tf_op jit(solution)/shard_map/kv_over_y/ppermute | solution.py:268
  28.1 9.0 %collective-permute-start.5 = (f32[128,128]{1,0:T(8,128)S(1)}, f32[128,128]{1,0:T(8,128)S(1)}, u32[]{:S(2)}, u32[]{:S(2)}) collective-permute-start(f32[128,128]{1,0:T(8,128)S(1)} %add.3.after_ref.p0_ref), channel_id=1, source_target_pairs={{0,6},{2,4},{4,2},{6,0},{1,7},{3,5},{5,3},{7,1},{8,14},{10,12},{12... | collective-permute-start | bytes 196616 | tf_op jit(solution)/shard_map/coupled_over_x/ppermute | solution.py:268
  32.5 6.5 %collective-permute-start.4 = (f32[128,128]{1,0:T(8,128)S(1)}, f32[128,128]{1,0:T(8,128)S(1)}, u32[]{:S(2)}, u32[]{:S(2)}) collective-permute-start(f32[128,128]{1,0:T(8,128)S(1)} %add.3.after_ref.p0_ref), channel_id=1, source_target_pairs={{0,4},{2,6},{4,0},{6,2},{1,5},{3,7},{5,1},{7,3},{8,12},{10,14},{12... | collective-permute-start | bytes 196616 | tf_op jit(solution)/shard_map/coupled_over_x/ppermute | solution.py:268
  35.0 5.1 %collective-permute-start.3 = (f32[128,128]{1,0:T(8,128)S(1)}, f32[128,128]{1,0:T(8,128)S(1)}, u32[]{:S(2)}, u32[]{:S(2)}) collective-permute-start(f32[128,128]{1,0:T(8,128)S(1)} %add.3.after_ref.p0_ref), channel_id=1, source_target_pairs={{0,2},{2,0},{4,6},{6,4},{1,3},{3,1},{5,7},{7,5},{8,10},{10,8},{12,... | collective-permute-start | bytes 196616 | tf_op jit(solution)/shard_map/coupled_over_x/ppermute | solution.py:268
  40.1 6.9 %collective-permute-start.6 = (bf16[4,272,256]{2,1,0:T(8,128)(2,1)S(1)}, bf16[4,272,256]{2,1,0:T(8,128)(2,1)S(1)}, u32[]{:S(2)}, u32[]{:S(2)}) collective-permute-start(bf16[4,272,256]{2,1,0:T(8,128)(2,1)S(1)} %join.1.kva_ref), channel_id=1, source_target_pairs={{0,8},{8,0},{1,9},{9,1},{2,10},{10,2},{3,11},{11,3},{4,12},{12,4},... | collective-permute-start | bytes 1671176 | tf_op jit(solution)/shard_map/kv_over_core/ppermute | solution.py:268
  74.5 7.2 %collective-permute-start.7 = (bf16[4,256,256]{2,1,0:T(8,128)(2,1)S(1)}, bf16[4,256,256]{2,1,0:T(8,128)(2,1)S(1)}, u32[]{:S(2)}, u32[]{:S(2)}) collective-permute-start(bf16[4,256,256]{2,1,0:T(8,128)(2,1)S(1)} %get-tuple-element.23), channel_id=1, source_target_pairs={{0,8},{8,0},{1,9},{9,1},{2,10},{10,2},{3,11},{11,3},{4,12},{12,4},... | collective-permute-start | bytes 1572872 | tf_op jit(solution)/shard_map/dkv_over_core/ppermute | solution.py:268
  78.2 21.5 %all-to-all-start.2 = ((bf16[8,128,256]{2,1,0:T(8,128)(2,1)}), bf16[8,128,256]{2,1,0:T(8,128)(2,1)S(1)}, u32[]{:S(2)}, u32[]{:S(2)}) async-start(bf16[8,128,256]{2,1,0:T(8,128)(2,1)} %get-tuple-element.28), calls=%async_computation.2 | async-start | bytes 1048576 | tf_op jit(solution)/shard_map/dq_over_z/all_to_all | solution.py:326
  81.9 9.3 %collective-permute-start.8 = (bf16[256,256]{1,0:T(8,128)(2,1)S(1)}, bf16[256,256]{1,0:T(8,128)(2,1)S(1)}, u32[]{:S(2)}, u32[]{:S(2)}) collective-permute-start(bf16[256,256]{1,0:T(8,128)(2,1)S(1)} %get-tuple-element.25), channel_id=1, source_target_pairs={{0,384},{128,256},{256,128},{384,0},{1,385},{129,257},{257,129},{3... | collective-permute-start | bytes 393224 | tf_op jit(solution)/shard_map/dkv_over_y/ppermute | solution.py:268
  85.4 11.7 %collective-permute-start.9 = (bf16[256,256]{1,0:T(8,128)(2,1)S(1)}, bf16[256,256]{1,0:T(8,128)(2,1)S(1)}, u32[]{:S(2)}, u32[]{:S(2)}) collective-permute-start(bf16[256,256]{1,0:T(8,128)(2,1)S(1)} %get-tuple-element.26), channel_id=1, source_target_pairs={{0,256},{128,384},{256,0},{384,128},{1,257},{129,385},{257,1},{385... | collective-permute-start | bytes 393224 | tf_op jit(solution)/shard_map/dkv_over_y/ppermute | solution.py:268
  87.3 9.8 %collective-permute-start.10 = (bf16[256,256]{1,0:T(8,128)(2,1)S(1)}, bf16[256,256]{1,0:T(8,128)(2,1)S(1)}, u32[]{:S(2)}, u32[]{:S(2)}) collective-permute-start(bf16[256,256]{1,0:T(8,128)(2,1)S(1)} %get-tuple-element.27), channel_id=1, source_target_pairs={{0,128},{128,0},{256,384},{384,256},{1,129},{129,1},{257,385},{385... | collective-permute-start | bytes 393224 | tf_op jit(solution)/shard_map/dkv_over_y/ppermute | solution.py:268

commit v6 on v5

--- a/solution.py
+++ b/solution.py
@@ -18,8 +18,14 @@
 BF16 = jnp.bfloat16
 NT = (((1,), (1,)), ((), ()))
 MIB = 1 << 20
+RING_Q = [[0, 1, 2, 3, 4, 5, 6, 7]]
+RING_P = [[7, 6, 5, 4, 3, 2, 1, 0]]
+RING_D = [[0, 1, 2, 3, 4, 5, 6, 7]]
+ORDER = (7, 6, 5, 4, 3, 2, 1, 0)
+BACK = (0, 1, 2, 3, 4, 5, 6, 7)
 JOIN_COST = 1_000_000
-PAIR_COST = 2_000_000_000
+PAIR_COST = 5_000_000_000
+ADD_COST = 1_000_000_000
 FOLD_COST = 20_000_000_000
 
 
@@ -149,7 +155,12 @@
         out_ref[i, 128:176, :] = tail
 
 
+def add_kernel(a_ref, b_ref, out_ref):
+    out_ref[...] = a_ref[...] + b_ref[...]
+
+
 def pair_kernel(own_ref, far_ref, after_ref, out_ref):
+    del after_ref
     out_ref[0] = own_ref[...]
     out_ref[1] = far_ref[...]
 
@@ -166,10 +177,11 @@
 ):
     low = lax.broadcasted_iota(jnp.int32, (1, 128), 1) < SPAN
     upstream = [
-        g_ref[:, part * SPAN : (part + 1) * SPAN, :].reshape(NZ * SPAN, HEAD) for part in range(2)
+        jnp.concatenate([g_ref[i, part * SPAN : (part + 1) * SPAN, :] for i in ORDER], axis=0)
+        for part in range(2)
     ]
     tails = g_ref[:, 128:176, :].astype(F32)
-    deltas = [tails[i, 0:8, :] for i in range(NZ)]
+    deltas = [tails[i, 0:8, :] for i in ORDER]
     turned = [pltpu.roll(t, SPAN, 1) for t in deltas]
     sides = (kva_ref, kvb_ref)
     grads = (da_ref, db_ref)
@@ -225,8 +237,11 @@
         late_t = jnp.concatenate([rows_of(kv, 64, head) for kv in sides], axis=0).T
         dqe = dot(early_t, ds_ref[0:512, 0:512])
         dql = dot(early_t, ds_ref[0:512, 512:1024]) + dot(late_t, ds_ref[512:1024, 512:1024])
-        dq_ref[:, 0:64, cols] = (dqe * FACTOR).T.astype(BF16).reshape(NZ, SPAN, HEAD)
-        dq_ref[:, 64:128, cols] = (dql * FACTOR).T.astype(BF16).reshape(NZ, SPAN, HEAD)
+        dqe = (dqe * FACTOR).T.astype(BF16)
+        dql = (dql * FACTOR).T.astype(BF16)
+        for i, place in enumerate(BACK):
+            dq_ref[place, 0:64, cols] = dqe[i * SPAN : (i + 1) * SPAN, :]
+            dq_ref[place, 64:128, cols] = dql[i * SPAN : (i + 1) * SPAN, :]
 
 
 def fold_kernel(own_ref, recv_ref, o0_ref, o1_ref, o2_ref, o3_ref):
@@ -280,19 +295,20 @@
             limit=62,
         )(positions, queries, keys, values, attention_out, projection)
     with jax.named_scope("q_over_z"):
-        qg = lax.all_to_all(qpay, "z", 0, 0)
+        qg = lax.all_to_all(qpay, "z", 0, 0, axis_index_groups=RING_Q)
     with jax.named_scope("coupled_over_h"):
-        total = total + swap(total, "h", n_h, 1) if n_h > 1 else total
+        near = swap(total, "h", n_h, 1) if n_h > 1 else jnp.zeros_like(total)
+        (total,) = call(add_kernel, [((128, 128), F32)], ADD_COST)(total, near)
+    with jax.named_scope("kv_over_y"):
+        (pair,) = call(pair_kernel, [((2, 272, 256), BF16)], PAIR_COST)(
+            kvpay, swap(kvpay, "y", NY, 2), total
+        )
+        other = swap(pair, "y", NY, 1)
     with jax.named_scope("coupled_over_x"):
         if n_x > 1:
             parts = [swap(total, "x", n_x, k) for k in (1, 2, 3)]
         else:
             parts = [jnp.zeros_like(total)] * 3
-    with jax.named_scope("kv_over_y"):
-        (pair,) = call(pair_kernel, [((2, 272, 256), BF16)], PAIR_COST)(
-            kvpay, swap(kvpay, "y", NY, 2), total
-        )
-        other = swap(pair, "y", NY, 1)
     with jax.named_scope("join"):
         (kva,) = call(join_kernel, [((NY, 272, 256), BF16)], JOIN_COST)(pair, other, *parts)
     with jax.named_scope("kv_over_core"):
@@ -306,7 +322,7 @@
             limit=24,
         )(qg, kva, kvb, total, *parts, latent.T, projection, attention_out)
     with jax.named_scope("upstream_over_z"):
-        gathered = lax.all_to_all(pay, "z", 0, 0)
+        gathered = lax.all_to_all(pay, "z", 0, 0, axis_index_groups=RING_P)
     with jax.named_scope("main"):
         dq, da, db = call(
             main_kernel,
@@ -323,7 +339,7 @@
     with jax.named_scope("dkv_over_y"):
         back = [swap(s, "y", NY, k) for k, s in zip((3, 2, 1), (send[2], send[1], send[0]))]
     with jax.named_scope("dq_over_z"):
-        dqs = lax.all_to_all(dq, "z", 0, 0)
+        dqs = lax.all_to_all(dq, "z", 0, 0, axis_index_groups=RING_D)
     with jax.named_scope("final"):
         return tuple(
             call(final_kernel, [((128, 256), BF16)] * 3, 1_000_000)(own, *back, dqs)

time: 101 us -> 98.1 us (0.971)
  blocking collectives: 20.9 us -> 18 us
    all_to_all x1, blocking collectives: 20.9 us -> 18 us  [local(): gathered = lax.all_to_all(pay, 'z', 0, 0, axis_index_groups=RING_P)]
    all_to_all x2, starting transfers between devices: 13.6 us -> 15.3 us  [the longest x1 10 us: local(): qg = lax.all_to_all(qpay, 'z', 0, 0, axis_index_groups=RING_Q)]
    ppermute x11, waiting for transfers between devices: 10.4 us -> 12.1 us  [swap(): return lax.ppermute(x, axis, [(i, i ^ k) for i in range(size)])]
    all_to_all x2, waiting for transfers between devices: 2.64 us -> 1.02 us  [the longest x1 1.02 us: local(): dqs = lax.all_to_all(dq, 'z', 0, 0, axis_index_groups=RING_D)]
    ppermute x11, starting transfers between devices: 40.3 us -> 39.2 us  [swap(): return lax.ppermute(x, axis, [(i, i ^ k) for i in range(size)])]
    pallas_call x7 -> x8, Pallas kernels: 10.1 us -> 10.1 us  [run(): pl.pallas_call(kernel, out_shape=[jax.ShapeDtypeStruct(s, d) for s, d in...]
  transfers between devices with their start and end apart: 13 -> 13, of which waited for: 5 -> 5; matrix products, arithmetic and copies ran while one was open for 1% -> 0% of each run, Pallas kernels for 0% -> 0%
where the time goes in v6:
time: 98.1 us; the launch traced here: 97.4 us
  starting transfers between devices  54.5 us (56%)
  blocking collectives  18 us (18%)
  waiting for transfers between devices  13.1 us (13%)
  Pallas kernels  10.1 us (10%)
    ppermute x11, starting transfers between devices, swap(): return lax.ppermute(x, axis, [(i, i ^ k) for i in range(size)])  39.2 us
    all_to_all x1, blocking collectives, local(): gathered = lax.all_to_all(pay, 'z', 0, 0, axis_index_groups=RING_P)  18 us
    ppermute x11, waiting for transfers between devices, swap(): return lax.ppermute(x, axis, [(i, i ^ k) for i in range(size)])  12.1 us
    pallas_call x8, Pallas kernels, run(): pl.pallas_call(kernel, out_shape=[jax.ShapeDtypeStruct(s, d) for s, d in...  10.1 us
    all_to_all x1, starting transfers between devices, local(): qg = lax.all_to_all(qpay, 'z', 0, 0, axis_index_groups=RING_Q)  10 us
    all_to_all x1, starting transfers between devices, local(): dqs = lax.all_to_all(dq, 'z', 0, 0, axis_index_groups=RING_D)  5.26 us
  transfers between devices with their start and end apart: 13, of which 5 were waited for; matrix products, arithmetic and copies ran while one was open for 0% of the time, Pallas kernels for 0%

profile of v6, /device:TPU:1, one launch (start us, length us, event | category | flops | bytes accessed | tf_op | source)
XLA Modules:
  0.0 97.4 jit_solution(16437710846929975983)
XLA Ops:
  0.6 2.6 %prep.1 = (bf16[8,144,256]{2,1,0:T(8,128)(2,1)}, bf16[272,256]{1,0:T(8,128)(2,1)}, f32[128,128]{1,0:T(8,128)}) custom-call(s32[128]{0:T(128)} %pos_ref.1, bf16[128,256]{1,0:T(8,128)(2,1)} %q_hbm.1, bf16[128,256]{1,0:T(8,128)(2,1)} %k_hbm.1, bf16[128,256]{1,0:T(8,128)(2,1)} %v_hbm.1, bf16[128,256]{1,0:T(8,128)(2,1)} %o_ref.1, bf16[256,128]{1,0:T(8,128)(2,1)} %proj_ref.3), custom_call_target="tpu_custom_call" | custom-call | flops 10000000 | bytes 2097152 | tf_op jit(solution)/shard_map/prep/pallas_call | solution.py:269
  3.2 0.0 copy-start.2
  3.2 8.4 %collective-permute-start.1 = (f32[128,128]{1,0:T(8,128)}, f32[128,128]{1,0:T(8,128)S(1)}, u32[]{:S(2)}, u32[]{:S(2)}) collective-permute-start(f32[128,128]{1,0:T(8,128)} %get-tuple-element.18.a_ref), channel_id=1, source_target_pairs={{0,1},{1,0},{2,3},{3,2},{4,5},{5,4},{6,7},{7,6},{8,9},{9,8},{10,11... | collective-permute-start | bytes 196616 | tf_op jit(solution)/shard_map/coupled_over_h/ppermute | solution.py:283
  11.6 2.4 %collective-permute-start = (bf16[272,256]{1,0:T(8,128)(2,1)}, bf16[272,256]{1,0:T(8,128)(2,1)S(1)}, u32[]{:S(2)}, u32[]{:S(2)}) collective-permute-start(bf16[272,256]{1,0:T(8,128)(2,1)} %get-tuple-element.17.own_ref), channel_id=1, source_target_pairs={{0,256},{128,384},{256,0},{384,128},{1,257},{129,385},{257,1},{385... | collective-permute-start | bytes 417800 | tf_op jit(solution)/shard_map/kv_over_y/ppermute | solution.py:283
  14.1 10.0 %all-to-all-start = ((bf16[8,144,256]{2,1,0:T(8,128)(2,1)}), bf16[8,144,256]{2,1,0:T(8,128)(2,1)S(1)}, u32[]{:S(2)}, u32[]{:S(2)}) async-start(bf16[8,144,256]{2,1,0:T(8,128)(2,1)} %get-tuple-element.16), calls=%async_computation | async-start | bytes 1179648 | tf_op jit(solution)/shard_map/q_over_z/all_to_all | solution.py:298
  24.1 0.0 collective-permute-done.1.b_ref
  24.1 0.0 copy-start.3
  24.1 0.8 copy-done.3
  25.0 0.0 copy-start
  25.0 0.0 copy-start.1
  25.0 0.0 copy-start.4
  25.0 0.0 collective-permute-done.far_ref
  25.0 0.0 copy-done.2
  25.1 2.3 %collective-permute-start.2 = (bf16[2,272,256]{2,1,0:T(8,128)(2,1)S(1)}, bf16[2,272,256]{2,1,0:T(8,128)(2,1)S(1)}, u32[]{:S(2)}, u32[]{:S(2)}) collective-permute-start(bf16[2,272,256]{2,1,0:T(8,128)(2,1)S(1)} %kv_over_y.1.own_ref), channel_id=1, source_target_pairs={{0,128},{128,0},{256,384},{384,256},{1,129},{129,1},{257,385},{385... | collective-permute-start | bytes 835592 | tf_op jit(solution)/shard_map/kv_over_y/ppermute | solution.py:283
  27.4 4.4 %collective-permute-start.5 = (f32[128,128]{1,0:T(8,128)S(1)}, f32[128,128]{1,0:T(8,128)S(1)}, u32[]{:S(2)}, u32[]{:S(2)}) collective-permute-start(f32[128,128]{1,0:T(8,128)S(1)} %coupled_over_h.1.after_ref.p0_ref), channel_id=1, source_target_pairs={{0,6},{2,4},{4,2},{6,0},{1,7},{3,5},{5,3},{7,1},{8,14},{10,12},{12... | collective-permute-start | bytes 196616 | tf_op jit(solution)/shard_map/coupled_over_x/ppermute | solution.py:283
  31.8 2.4 %collective-permute-start.4 = (f32[128,128]{1,0:T(8,128)S(1)}, f32[128,128]{1,0:T(8,128)S(1)}, u32[]{:S(2)}, u32[]{:S(2)}) collective-permute-start(f32[128,128]{1,0:T(8,128)S(1)} %coupled_over_h.1.after_ref.p0_ref), channel_id=1, source_target_pairs={{0,4},{2,6},{4,0},{6,2},{1,5},{3,7},{5,1},{7,3},{8,12},{10,14},{12... | collective-permute-start | bytes 196616 | tf_op jit(solution)/shard_map/coupled_over_x/ppermute | solution.py:283
  34.2 2.2 %collective-permute-start.3 = (f32[128,128]{1,0:T(8,128)S(1)}, f32[128,128]{1,0:T(8,128)S(1)}, u32[]{:S(2)}, u32[]{:S(2)}) collective-permute-start(f32[128,128]{1,0:T(8,128)S(1)} %coupled_over_h.1.after_ref.p0_ref), channel_id=1, source_target_pairs={{0,2},{2,0},{4,6},{6,4},{1,3},{3,1},{5,7},{7,5},{8,10},{10,8},{12,... | collective-permute-start | bytes 196616 | tf_op jit(solution)/shard_map/coupled_over_x/ppermute | solution.py:283
  36.4 0.0 collective-permute-done.5.refs_2_.p3_ref
  36.4 1.9 %collective-permute-done.4.refs_1_.p2_ref = f32[128,128]{1,0:T(8,128)S(1)} collective-permute-done((f32[128,128]{1,0:T(8,128)S(1)}, f32[128,128]{1,0:T(8,128)S(1)}, u32[]{:S(2)}, u32[]{:S(2)}) %collective-permute-start.4) | collective-permute-done | bytes 65568 | tf_op jit(solution)/shard_map/coupled_over_x/ppermute | solution.py:283
  38.3 1.0 %collective-permute-done.3.refs_0_.p1_ref = f32[128,128]{1,0:T(8,128)S(1)} collective-permute-done((f32[128,128]{1,0:T(8,128)S(1)}, f32[128,128]{1,0:T(8,128)S(1)}, u32[]{:S(2)}, u32[]{:S(2)}) %collective-permute-start.3) | collective-permute-done | bytes 65568 | tf_op jit(solution)/shard_map/coupled_over_x/ppermute | solution.py:283
  39.3 0.0 collective-permute-done.2.recv_ref
  39.4 5.3 %collective-permute-start.6 = (bf16[4,272,256]{2,1,0:T(8,128)(2,1)S(1)}, bf16[4,272,256]{2,1,0:T(8,128)(2,1)S(1)}, u32[]{:S(2)}, u32[]{:S(2)}) collective-permute-start(bf16[4,272,256]{2,1,0:T(8,128)(2,1)S(1)} %join.1.kva_ref), channel_id=1, source_target_pairs={{0,8},{8,0},{1,9},{9,1},{2,10},{10,2},{3,11},{11,3},{4,12},{12,4},... | collective-permute-start | bytes 1671176 | tf_op jit(solution)/shard_map/kv_over_core/ppermute | solution.py:283
  44.7 1.6 %collective-permute-done.6.kvb_ref = bf16[4,272,256]{2,1,0:T(8,128)(2,1)S(1)} collective-permute-done((bf16[4,272,256]{2,1,0:T(8,128)(2,1)S(1)}, bf16[4,272,256]{2,1,0:T(8,128)(2,1)S(1)}, u32[]{:S(2)}, u32[]{:S(2)}) %collective-permute-start.6) | collective-permute-done | bytes 557088 | tf_op jit(solution)/shard_map/kv_over_core/ppermute | solution.py:283
  46.2 0.0 all-to-all-done.qg_ref
  46.2 0.0 copy-done
  46.2 0.0 copy-done.1
  46.3 0.0 copy-done.4
  46.3 2.3 %stats.1 = (bf16[8,176,128]{2,1,0:T(8,128)(2,1)S(1)}, bf16[2,1024,1024]{2,1,0:T(8,128)(2,1)S(1)}, f32[16,128]{1,0:T(8,128)S(1)}) custom-call(bf16[8,144,256]{2,1,0:T(8,128)(2,1)S(1)} %all-to-all-done.qg_ref, bf16[4,272,256]{2,1,0:T(8,128)(2,1)S(1)} %join.1.kva_ref, bf16[4,272,256]{2,1,0:T(8,128)(2,1)S(1)} %collective-permute-done.6.kvb_ref, ...), custom_call_target="tpu_custom_call" | custom-call | flops 1000000000 | bytes 2097152 | tf_op jit(solution)/shard_map/stats/pallas_call | solution.py:269
  48.5 18.0 %all_to_all.15.g_ref = bf16[8,176,128]{2,1,0:T(8,128)(2,1)S(1)} all-to-all(bf16[8,176,128]{2,1,0:T(8,128)(2,1)S(1)} %get-tuple-element.19), channel_id=1, replica_groups={{112,96,80,64,48,32,16,0},{113,97,81,65,49,33,17,1},{114,98,82,66,50,34..., dimensions={0} | all-to-all | bytes 720896 | tf_op jit(solution)/shard_map/upstream_over_z/all_to_all | solution.py:325
  66.5 4.3 %main.1 = (bf16[8,128,256]{2,1,0:T(8,128)(2,1)}, bf16[4,256,256]{2,1,0:T(8,128)(2,1)S(1)}, bf16[4,256,256]{2,1,0:T(8,128)(2,1)S(1)}) custom-call(bf16[8,144,256]{2,1,0:T(8,128)(2,1)S(1)} %all-to-all-done.qg_ref, bf16[4,272,256]{2,1,0:T(8,128)(2,1)S(1)} %join.1.kva_ref, bf16[4,272,256]{2,1,0:T(8,128)(2,1)S(1)} %collective-permute-done.6.kvb_ref, ...), custom_call_target="tpu_custom_call" | custom-call | flops 4000000000 | bytes 2097152 | tf_op jit(solution)/shard_map/main/pallas_call | solution.py:269
  70.8 2.5 %collective-permute-start.7 = (bf16[4,256,256]{2,1,0:T(8,128)(2,1)S(1)}, bf16[4,256,256]{2,1,0:T(8,128)(2,1)S(1)}, u32[]{:S(2)}, u32[]{:S(2)}) collective-permute-start(bf16[4,256,256]{2,1,0:T(8,128)(2,1)S(1)} %get-tuple-element.23), channel_id=1, source_target_pairs={{0,8},{8,0},{1,9},{9,1},{2,10},{10,2},{3,11},{11,3},{4,12},{12,4},... | collective-permute-start | bytes 1572872 | tf_op jit(solution)/shard_map/dkv_over_core/ppermute | solution.py:283
  73.4 5.3 %all-to-all-start.2 = ((bf16[8,128,256]{2,1,0:T(8,128)(2,1)}), bf16[8,128,256]{2,1,0:T(8,128)(2,1)S(1)}, u32[]{:S(2)}, u32[]{:S(2)}) async-start(bf16[8,128,256]{2,1,0:T(8,128)(2,1)} %get-tuple-element.28), calls=%async_computation.2 | async-start | bytes 1048576 | tf_op jit(solution)/shard_map/dq_over_z/all_to_all | solution.py:342
  78.6 0.0 collective-permute-done.7.recv_ref
  78.6 0.1 dkv_over_core.1
  78.7 3.9 %collective-permute-start.8 = (bf16[256,256]{1,0:T(8,128)(2,1)S(1)}, bf16[256,256]{1,0:T(8,128)(2,1)S(1)}, u32[]{:S(2)}, u32[]{:S(2)}) collective-permute-start(bf16[256,256]{1,0:T(8,128)(2,1)S(1)} %get-tuple-element.25), channel_id=1, source_target_pairs={{0,384},{128,256},{256,128},{384,0},{1,385},{129,257},{257,129},{3... | collective-permute-start | bytes 393224 | tf_op jit(solution)/shard_map/dkv_over_y/ppermute | solution.py:283
  82.7 2.8 %collective-permute-start.9 = (bf16[256,256]{1,0:T(8,128)(2,1)S(1)}, bf16[256,256]{1,0:T(8,128)(2,1)S(1)}, u32[]{:S(2)}, u32[]{:S(2)}) collective-permute-start(bf16[256,256]{1,0:T(8,128)(2,1)S(1)} %get-tuple-element.26), channel_id=1, source_target_pairs={{0,256},{128,384},{256,0},{384,128},{1,257},{129,385},{257,1},{385... | collective-permute-start | bytes 393224 | tf_op jit(solution)/shard_map/dkv_over_y/ppermute | solution.py:283
  85.5 2.5 %collective-permute-start.10 = (bf16[256,256]{1,0:T(8,128)(2,1)S(1)}, bf16[256,256]{1,0:T(8,128)(2,1)S(1)}, u32[]{:S(2)}, u32[]{:S(2)}) collective-permute-start(bf16[256,256]{1,0:T(8,128)(2,1)S(1)} %get-tuple-element.27), channel_id=1, source_target_pairs={{0,128},{128,0},{256,384},{384,256},{1,129},{129,1},{257,385},{385... | collective-permute-start | bytes 393224 | tf_op jit(solution)/shard_map/dkv_over_y/ppermute | solution.py:283
  88.0 0.0 collective-permute-done.8.r1_ref
  88.1 7.6 %collective-permute-done.9.r2_ref = bf16[256,256]{1,0:T(8,128)(2,1)S(1)} collective-permute-done((bf16[256,256]{1,0:T(8,128)(2,1)S(1)}, bf16[256,256]{1,0:T(8,128)(2,1)S(1)}, u32[]{:S(2)}, u32[]{:S(2)}) %collective-permute-start.9) | collective-permute-done | bytes 131104 | tf_op jit(solution)/shard_map/dkv_over_y/ppermute | solution.py:283
  95.6 0.0 collective-permute-done.10.r3_ref
  95.6 1.0 %all-to-all-done.2.dq_ref = bf16[8,128,256]{2,1,0:T(8,128)(2,1)S(1)} async-done(((bf16[8,128,256]{2,1,0:T(8,128)(2,1)}), bf16[8,128,256]{2,1,0:T(8,128)(2,1)S(1)}, u32[]{:S(2)}, u32[]{:S(2)}) %all-to-all-start.2) | async-done | bytes 524320 | tf_op jit(solution)/shard_map/dq_over_z/all_to_all | solution.py:342
  96.6 0.8 final.1
  (3 shorter events, 0.1 us)
Async XLA Ops:
  3.2 21.8 %copy-start.2 = (bf16[272,256]{1,0:T(8,128)(2,1)S(1)}, bf16[272,256]{1,0:T(8,128)(2,1)}, u32[]{:S(2)}) copy-start(bf16[272,256]{1,0:T(8,128)(2,1)} %get-tuple-element.17.own_ref) | copy-start | bytes 417796
  3.2 20.9 %collective-permute-start.1 = (f32[128,128]{1,0:T(8,128)}, f32[128,128]{1,0:T(8,128)S(1)}, u32[]{:S(2)}, u32[]{:S(2)}) collective-permute-start(f32[128,128]{1,0:T(8,128)} %get-tuple-element.18.a_ref), channel_id=1, source_target_pairs={{0,1},{1,0},{2,3},{3,2},{4,5},{5,4},{6,7},{7,6},{8,9},{9,8},{10,11... | collective-permute-start | bytes 196616 | tf_op jit(solution)/shard_map/coupled_over_h/ppermute | solution.py:283
  11.6 13.4 %collective-permute-start = (bf16[272,256]{1,0:T(8,128)(2,1)}, bf16[272,256]{1,0:T(8,128)(2,1)S(1)}, u32[]{:S(2)}, u32[]{:S(2)}) collective-permute-start(bf16[272,256]{1,0:T(8,128)(2,1)} %get-tuple-element.17.own_ref), channel_id=1, source_target_pairs={{0,256},{128,384},{256,0},{384,128},{1,257},{129,385},{257,1},{385... | collective-permute-start | bytes 417800 | tf_op jit(solution)/shard_map/kv_over_y/ppermute | solution.py:283
  14.1 32.2 %all-to-all-start = ((bf16[8,144,256]{2,1,0:T(8,128)(2,1)}), bf16[8,144,256]{2,1,0:T(8,128)(2,1)S(1)}, u32[]{:S(2)}, u32[]{:S(2)}) async-start(bf16[8,144,256]{2,1,0:T(8,128)(2,1)} %get-tuple-element.16), calls=%async_computation | async-start | bytes 1179648 | tf_op jit(solution)/shard_map/q_over_z/all_to_all | solution.py:298
  24.1 0.8 copy-start.3
  25.0 21.3 %copy-start = (bf16[128,256]{1,0:T(8,128)(2,1)S(1)}, bf16[128,256]{1,0:T(8,128)(2,1)}, u32[]{:S(2)}) copy-start(bf16[128,256]{1,0:T(8,128)(2,1)} %o_ref.1) | copy-start | bytes 196612
  25.0 21.3 %copy-start.1 = (bf16[256,128]{1,0:T(8,128)(2,1)S(1)}, bf16[256,128]{1,0:T(8,128)(2,1)}, u32[]{:S(2)}) copy-start(bf16[256,128]{1,0:T(8,128)(2,1)} %proj_ref.3) | copy-start | bytes 196612
  25.0 21.3 %copy-start.4 = (f32[128,64]{0,1:T(8,128)S(1)}, f32[128,64]{0,1:T(8,128)}, u32[]{:S(2)}) copy-start(f32[128,64]{0,1:T(8,128)} %param.7) | copy-start | bytes 98308
  25.1 14.3 %collective-permute-start.2 = (bf16[2,272,256]{2,1,0:T(8,128)(2,1)S(1)}, bf16[2,272,256]{2,1,0:T(8,128)(2,1)S(1)}, u32[]{:S(2)}, u32[]{:S(2)}) collective-permute-start(bf16[2,272,256]{2,1,0:T(8,128)(2,1)S(1)} %kv_over_y.1.own_ref), channel_id=1, source_target_pairs={{0,128},{128,0},{256,384},{384,256},{1,129},{129,1},{257,385},{385... | collective-permute-start | bytes 835592 | tf_op jit(solution)/shard_map/kv_over_y/ppermute | solution.py:283
  27.4 9.0 %collective-permute-start.5 = (f32[128,128]{1,0:T(8,128)S(1)}, f32[128,128]{1,0:T(8,128)S(1)}, u32[]{:S(2)}, u32[]{:S(2)}) collective-permute-start(f32[128,128]{1,0:T(8,128)S(1)} %coupled_over_h.1.after_ref.p0_ref), channel_id=1, source_target_pairs={{0,6},{2,4},{4,2},{6,0},{1,7},{3,5},{5,3},{7,1},{8,14},{10,12},{12... | collective-permute-start | bytes 196616 | tf_op jit(solution)/shard_map/coupled_over_x/ppermute | solution.py:283
  31.8 6.5 %collective-permute-start.4 = (f32[128,128]{1,0:T(8,128)S(1)}, f32[128,128]{1,0:T(8,128)S(1)}, u32[]{:S(2)}, u32[]{:S(2)}) collective-permute-start(f32[128,128]{1,0:T(8,128)S(1)} %coupled_over_h.1.after_ref.p0_ref), channel_id=1, source_target_pairs={{0,4},{2,6},{4,0},{6,2},{1,5},{3,7},{5,1},{7,3},{8,12},{10,14},{12... | collective-permute-start | bytes 196616 | tf_op jit(solution)/shard_map/coupled_over_x/ppermute | solution.py:283
  34.2 5.1 %collective-permute-start.3 = (f32[128,128]{1,0:T(8,128)S(1)}, f32[128,128]{1,0:T(8,128)S(1)}, u32[]{:S(2)}, u32[]{:S(2)}) collective-permute-start(f32[128,128]{1,0:T(8,128)S(1)} %coupled_over_h.1.after_ref.p0_ref), channel_id=1, source_target_pairs={{0,2},{2,0},{4,6},{6,4},{1,3},{3,1},{5,7},{7,5},{8,10},{10,8},{12,... | collective-permute-start | bytes 196616 | tf_op jit(solution)/shard_map/coupled_over_x/ppermute | solution.py:283
  39.4 6.9 %collective-permute-start.6 = (bf16[4,272,256]{2,1,0:T(8,128)(2,1)S(1)}, bf16[4,272,256]{2,1,0:T(8,128)(2,1)S(1)}, u32[]{:S(2)}, u32[]{:S(2)}) collective-permute-start(bf16[4,272,256]{2,1,0:T(8,128)(2,1)S(1)} %join.1.kva_ref), channel_id=1, source_target_pairs={{0,8},{8,0},{1,9},{9,1},{2,10},{10,2},{3,11},{11,3},{4,12},{12,4},... | collective-permute-start | bytes 1671176 | tf_op jit(solution)/shard_map/kv_over_core/ppermute | solution.py:283
  70.8 7.8 %collective-permute-start.7 = (bf16[4,256,256]{2,1,0:T(8,128)(2,1)S(1)}, bf16[4,256,256]{2,1,0:T(8,128)(2,1)S(1)}, u32[]{:S(2)}, u32[]{:S(2)}) collective-permute-start(bf16[4,256,256]{2,1,0:T(8,128)(2,1)S(1)} %get-tuple-element.23), channel_id=1, source_target_pairs={{0,8},{8,0},{1,9},{9,1},{2,10},{10,2},{3,11},{11,3},{4,12},{12,4},... | collective-permute-start | bytes 1572872 | tf_op jit(solution)/shard_map/dkv_over_core/ppermute | solution.py:283
  73.4 23.3 %all-to-all-start.2 = ((bf16[8,128,256]{2,1,0:T(8,128)(2,1)}), bf16[8,128,256]{2,1,0:T(8,128)(2,1)S(1)}, u32[]{:S(2)}, u32[]{:S(2)}) async-start(bf16[8,128,256]{2,1,0:T(8,128)(2,1)} %get-tuple-element.28), calls=%async_computation.2 | async-start | bytes 1048576 | tf_op jit(solution)/shard_map/dq_over_z/all_to_all | solution.py:342
  78.7 9.3 %collective-permute-start.8 = (bf16[256,256]{1,0:T(8,128)(2,1)S(1)}, bf16[256,256]{1,0:T(8,128)(2,1)S(1)}, u32[]{:S(2)}, u32[]{:S(2)}) collective-permute-start(bf16[256,256]{1,0:T(8,128)(2,1)S(1)} %get-tuple-element.25), channel_id=1, source_target_pairs={{0,384},{128,256},{256,128},{384,0},{1,385},{129,257},{257,129},{3... | collective-permute-start | bytes 393224 | tf_op jit(solution)/shard_map/dkv_over_y/ppermute | solution.py:283
  82.7 13.0 %collective-permute-start.9 = (bf16[256,256]{1,0:T(8,128)(2,1)S(1)}, bf16[256,256]{1,0:T(8,128)(2,1)S(1)}, u32[]{:S(2)}, u32[]{:S(2)}) collective-permute-start(bf16[256,256]{1,0:T(8,128)(2,1)S(1)} %get-tuple-element.26), channel_id=1, source_target_pairs={{0,256},{128,384},{256,0},{384,128},{1,257},{129,385},{257,1},{385... | collective-permute-start | bytes 393224 | tf_op jit(solution)/shard_map/dkv_over_y/ppermute | solution.py:283
  85.5 10.1 %collective-permute-start.10 = (bf16[256,256]{1,0:T(8,128)(2,1)S(1)}, bf16[256,256]{1,0:T(8,128)(2,1)S(1)}, u32[]{:S(2)}, u32[]{:S(2)}) collective-permute-start(bf16[256,256]{1,0:T(8,128)(2,1)S(1)} %get-tuple-element.27), channel_id=1, source_target_pairs={{0,128},{128,0},{256,384},{384,256},{1,129},{129,1},{257,385},{385... | collective-permute-start | bytes 393224 | tf_op jit(solution)/shard_map/dkv_over_y/ppermute | solution.py:283

commit v7 on v6

--- a/solution.py
+++ b/solution.py
@@ -25,6 +25,7 @@
 BACK = (0, 1, 2, 3, 4, 5, 6, 7)
 JOIN_COST = 1_000_000
 PAIR_COST = 5_000_000_000
+SUM_COST = 7_000_000_000
 ADD_COST = 1_000_000_000
 FOLD_COST = 20_000_000_000
 
@@ -94,7 +95,7 @@
 
 
 def stats_kernel(
-    qg_ref, kva_ref, kvb_ref, p0_ref, p1_ref, p2_ref, p3_ref, lat_ref, proj_ref, o_ref,
+    qg_ref, kva_ref, kvb_ref, coupled_ref, lat_ref, proj_ref, o_ref,
     out_ref, prob_ref, top_ref, s_ref, tail_ref,
 ):
     tail_ref[...] = jnp.zeros((48, 128), F32)
@@ -135,7 +136,7 @@
                 row = 8 + group * 8 + r
                 tail_ref[row : row + 1, :] = high[:, lanes]
                 tail_ref[row + 4 : row + 5, :] = low[:, lanes]
-    coupled = (p0_ref[...] + p1_ref[...]) + (p2_ref[...] + p3_ref[...])
+    coupled = coupled_ref[...]
     shifts = coupled[:, 0:64]
     log_scale = coupled[:, 64:128]
     damping = jnp.exp(-log_scale)
@@ -157,6 +158,10 @@
 
 def add_kernel(a_ref, b_ref, out_ref):
     out_ref[...] = a_ref[...] + b_ref[...]
+
+
+def sum_kernel(a_ref, b_ref, c_ref, d_ref, out_ref):
+    out_ref[...] = (a_ref[...] + b_ref[...]) + (c_ref[...] + d_ref[...])
 
 
 def pair_kernel(own_ref, far_ref, after_ref, out_ref):
@@ -310,9 +315,11 @@
         else:
             parts = [jnp.zeros_like(total)] * 3
     with jax.named_scope("join"):
-        (kva,) = call(join_kernel, [((NY, 272, 256), BF16)], JOIN_COST)(pair, other, *parts)
+        (kva,) = call(join_kernel, [((NY, 272, 256), BF16)], JOIN_COST)(pair, other)
     with jax.named_scope("kv_over_core"):
         kvb = swap(kva, "c", NC, 1)
+    with jax.named_scope("coupled_over_x"):
+        (coupled,) = call(sum_kernel, [((128, 128), F32)], SUM_COST)(total, *parts)
     with jax.named_scope("stats"):
         pay, prob, top = call(
             stats_kernel,
@@ -320,7 +327,7 @@
             1_000_000_000,
             [pltpu.VMEM((4, 256, 512), F32), pltpu.VMEM((48, 128), F32)],
             limit=24,
-        )(qg, kva, kvb, total, *parts, latent.T, projection, attention_out)
+        )(qg, kva, kvb, coupled, latent.T, projection, attention_out)
     with jax.named_scope("upstream_over_z"):
         gathered = lax.all_to_all(pay, "z", 0, 0, axis_index_groups=RING_P)
     with jax.named_scope("main"):

time: 98.1 us -> 94.6 us (0.964)
  waiting for transfers between devices: 13.1 us -> 10.1 us
    ppermute x11, waiting for transfers between devices: 12.1 us -> 9.1 us  [swap(): return lax.ppermute(x, axis, [(i, i ^ k) for i in range(size)])]
    pallas_call x8 -> x9, Pallas kernels: 10.1 us -> 10.1 us  [run(): pl.pallas_call(kernel, out_shape=[jax.ShapeDtypeStruct(s, d) for s, d in...]
  transfers between devices with their start and end apart: 13 -> 13, of which waited for: 5 -> 3; matrix products, arithmetic and copies ran while one was open for 0% -> 0% of each run, Pallas kernels for 0% -> 0%
where the time goes in v7:
time: 94.6 us; the launch traced here: 93.9 us
  starting transfers between devices  53.9 us (57%)
  blocking collectives  18 us (19%)
  Pallas kernels  10.1 us (11%)
  waiting for transfers between devices  10.1 us (11%)
    ppermute x11, starting transfers between devices, swap(): return lax.ppermute(x, axis, [(i, i ^ k) for i in range(size)])  38.5 us
    all_to_all x1, blocking collectives, local(): gathered = lax.all_to_all(pay, 'z', 0, 0, axis_index_groups=RING_P)  18 us
    pallas_call x9, Pallas kernels, run(): pl.pallas_call(kernel, out_shape=[jax.ShapeDtypeStruct(s, d) for s, d in...  10.1 us
    all_to_all x1, starting transfers between devices, local(): qg = lax.all_to_all(qpay, 'z', 0, 0, axis_index_groups=RING_Q)  10 us
    ppermute x11, waiting for transfers between devices, swap(): return lax.ppermute(x, axis, [(i, i ^ k) for i in range(size)])  9.1 us
    all_to_all x1, starting transfers between devices, local(): dqs = lax.all_to_all(dq, 'z', 0, 0, axis_index_groups=RING_D)  5.28 us
  transfers between devices with their start and end apart: 13, of which 3 were waited for; matrix products, arithmetic and copies ran while one was open for 0% of the time, Pallas kernels for 0%

profile of v7, /device:TPU:1, one launch (start us, length us, event | category | flops | bytes accessed | tf_op | source)
XLA Modules:
  0.0 93.9 jit_solution(3184403425951366137)
XLA Ops:
  0.6 2.6 %prep.1 = (bf16[8,144,256]{2,1,0:T(8,128)(2,1)}, bf16[272,256]{1,0:T(8,128)(2,1)}, f32[128,128]{1,0:T(8,128)}) custom-call(s32[128]{0:T(128)} %pos_ref.1, bf16[128,256]{1,0:T(8,128)(2,1)} %q_hbm.1, bf16[128,256]{1,0:T(8,128)(2,1)} %k_hbm.1, bf16[128,256]{1,0:T(8,128)(2,1)} %v_hbm.1, bf16[128,256]{1,0:T(8,128)(2,1)} %o_ref.1, bf16[256,128]{1,0:T(8,128)(2,1)} %proj_ref.3), custom_call_target="tpu_custom_call" | custom-call | flops 10000000 | bytes 2097152 | tf_op jit(solution)/shard_map/prep/pallas_call | solution.py:274
  3.2 0.0 copy-start.2
  3.2 8.4 %collective-permute-start.1 = (f32[128,128]{1,0:T(8,128)}, f32[128,128]{1,0:T(8,128)S(1)}, u32[]{:S(2)}, u32[]{:S(2)}) collective-permute-start(f32[128,128]{1,0:T(8,128)} %get-tuple-element.18.a_ref), channel_id=1, source_target_pairs={{0,1},{1,0},{2,3},{3,2},{4,5},{5,4},{6,7},{7,6},{8,9},{9,8},{10,11... | collective-permute-start | bytes 196616 | tf_op jit(solution)/shard_map/coupled_over_h/ppermute | solution.py:288
  11.6 2.4 %collective-permute-start = (bf16[272,256]{1,0:T(8,128)(2,1)}, bf16[272,256]{1,0:T(8,128)(2,1)S(1)}, u32[]{:S(2)}, u32[]{:S(2)}) collective-permute-start(bf16[272,256]{1,0:T(8,128)(2,1)} %get-tuple-element.17.own_ref), channel_id=1, source_target_pairs={{0,256},{128,384},{256,0},{384,128},{1,257},{129,385},{257,1},{385... | collective-permute-start | bytes 417800 | tf_op jit(solution)/shard_map/kv_over_y/ppermute | solution.py:288
  14.1 10.0 %all-to-all-start = ((bf16[8,144,256]{2,1,0:T(8,128)(2,1)}), bf16[8,144,256]{2,1,0:T(8,128)(2,1)S(1)}, u32[]{:S(2)}, u32[]{:S(2)}) async-start(bf16[8,144,256]{2,1,0:T(8,128)(2,1)} %get-tuple-element.16), calls=%async_computation | async-start | bytes 1179648 | tf_op jit(solution)/shard_map/q_over_z/all_to_all | solution.py:303
  24.1 0.0 collective-permute-done.1.b_ref
  24.1 0.0 copy-start.3
  24.1 0.8 copy-done.3
  25.0 0.0 collective-permute-done.far_ref
  25.0 0.0 copy-done.2
  25.0 2.3 %collective-permute-start.2 = (bf16[2,272,256]{2,1,0:T(8,128)(2,1)S(1)}, bf16[2,272,256]{2,1,0:T(8,128)(2,1)S(1)}, u32[]{:S(2)}, u32[]{:S(2)}) collective-permute-start(bf16[2,272,256]{2,1,0:T(8,128)(2,1)S(1)} %kv_over_y.1.own_ref), channel_id=1, source_target_pairs={{0,128},{128,0},{256,384},{384,256},{1,129},{129,1},{257,385},{385... | collective-permute-start | bytes 835592 | tf_op jit(solution)/shard_map/kv_over_y/ppermute | solution.py:288
  27.3 4.4 %collective-permute-start.6 = (f32[128,128]{1,0:T(8,128)S(1)}, f32[128,128]{1,0:T(8,128)S(1)}, u32[]{:S(2)}, u32[]{:S(2)}) collective-permute-start(f32[128,128]{1,0:T(8,128)S(1)} %coupled_over_h.1.after_ref.a_ref), channel_id=1, source_target_pairs={{0,6},{2,4},{4,2},{6,0},{1,7},{3,5},{5,3},{7,1},{8,14},{10,12},{12... | collective-permute-start | bytes 196616 | tf_op jit(solution)/shard_map/coupled_over_x/ppermute | solution.py:288
  31.7 2.4 %collective-permute-start.5 = (f32[128,128]{1,0:T(8,128)S(1)}, f32[128,128]{1,0:T(8,128)S(1)}, u32[]{:S(2)}, u32[]{:S(2)}) collective-permute-start(f32[128,128]{1,0:T(8,128)S(1)} %coupled_over_h.1.after_ref.a_ref), channel_id=1, source_target_pairs={{0,4},{2,6},{4,0},{6,2},{1,5},{3,7},{5,1},{7,3},{8,12},{10,14},{12... | collective-permute-start | bytes 196616 | tf_op jit(solution)/shard_map/coupled_over_x/ppermute | solution.py:288
  34.2 2.2 %collective-permute-start.4 = (f32[128,128]{1,0:T(8,128)S(1)}, f32[128,128]{1,0:T(8,128)S(1)}, u32[]{:S(2)}, u32[]{:S(2)}) collective-permute-start(f32[128,128]{1,0:T(8,128)S(1)} %coupled_over_h.1.after_ref.a_ref), channel_id=1, source_target_pairs={{0,2},{2,0},{4,6},{6,4},{1,3},{3,1},{5,7},{7,5},{8,10},{10,8},{12,... | collective-permute-start | bytes 196616 | tf_op jit(solution)/shard_map/coupled_over_x/ppermute | solution.py:288
  36.3 0.0 collective-permute-done.2.recv_ref
  36.4 0.0 copy-start
  36.4 0.0 copy-start.1
  36.4 0.0 copy-start.4
  36.4 4.7 %collective-permute-start.3 = (bf16[4,272,256]{2,1,0:T(8,128)(2,1)S(1)}, bf16[4,272,256]{2,1,0:T(8,128)(2,1)S(1)}, u32[]{:S(2)}, u32[]{:S(2)}) collective-permute-start(bf16[4,272,256]{2,1,0:T(8,128)(2,1)S(1)} %join.1.kva_ref), channel_id=1, source_target_pairs={{0,8},{8,0},{1,9},{9,1},{2,10},{10,2},{3,11},{11,3},{4,12},{12,4},... | collective-permute-start | bytes 1671176 | tf_op jit(solution)/shard_map/kv_over_core/ppermute | solution.py:288
  41.1 0.0 collective-permute-done.6.d_ref
  41.1 0.0 collective-permute-done.5.c_ref
  41.1 0.0 collective-permute-done.4.b_ref
  41.2 1.5 %collective-permute-done.3.kvb_ref = bf16[4,272,256]{2,1,0:T(8,128)(2,1)S(1)} collective-permute-done((bf16[4,272,256]{2,1,0:T(8,128)(2,1)S(1)}, bf16[4,272,256]{2,1,0:T(8,128)(2,1)S(1)}, u32[]{:S(2)}, u32[]{:S(2)}) %collective-permute-start.3) | collective-permute-done | bytes 557088 | tf_op jit(solution)/shard_map/kv_over_core/ppermute | solution.py:288
  42.7 0.0 all-to-all-done.qg_ref
  42.7 0.0 copy-done
  42.7 0.0 copy-done.1
  42.7 0.0 copy-done.4
  42.7 2.2 %stats.1 = (bf16[8,176,128]{2,1,0:T(8,128)(2,1)S(1)}, bf16[2,1024,1024]{2,1,0:T(8,128)(2,1)S(1)}, f32[16,128]{1,0:T(8,128)S(1)}) custom-call(bf16[8,144,256]{2,1,0:T(8,128)(2,1)S(1)} %all-to-all-done.qg_ref, bf16[4,272,256]{2,1,0:T(8,128)(2,1)S(1)} %join.1.kva_ref, bf16[4,272,256]{2,1,0:T(8,128)(2,1)S(1)} %collective-permute-done.3.kvb_ref, ...), custom_call_target="tpu_custom_call" | custom-call | flops 1000000000 | bytes 2097152 | tf_op jit(solution)/shard_map/stats/pallas_call | solution.py:274
  44.9 18.0 %all_to_all.15.g_ref = bf16[8,176,128]{2,1,0:T(8,128)(2,1)S(1)} all-to-all(bf16[8,176,128]{2,1,0:T(8,128)(2,1)S(1)} %get-tuple-element.19), channel_id=1, replica_groups={{112,96,80,64,48,32,16,0},{113,97,81,65,49,33,17,1},{114,98,82,66,50,34..., dimensions={0} | all-to-all | bytes 720896 | tf_op jit(solution)/shard_map/upstream_over_z/all_to_all | solution.py:332
  63.0 4.3 %main.1 = (bf16[8,128,256]{2,1,0:T(8,128)(2,1)}, bf16[4,256,256]{2,1,0:T(8,128)(2,1)S(1)}, bf16[4,256,256]{2,1,0:T(8,128)(2,1)S(1)}) custom-call(bf16[8,144,256]{2,1,0:T(8,128)(2,1)S(1)} %all-to-all-done.qg_ref, bf16[4,272,256]{2,1,0:T(8,128)(2,1)S(1)} %join.1.kva_ref, bf16[4,272,256]{2,1,0:T(8,128)(2,1)S(1)} %collective-permute-done.3.kvb_ref, ...), custom_call_target="tpu_custom_call" | custom-call | flops 4000000000 | bytes 2097152 | tf_op jit(solution)/shard_map/main/pallas_call | solution.py:274
  67.3 2.5 %collective-permute-start.7 = (bf16[4,256,256]{2,1,0:T(8,128)(2,1)S(1)}, bf16[4,256,256]{2,1,0:T(8,128)(2,1)S(1)}, u32[]{:S(2)}, u32[]{:S(2)}) collective-permute-start(bf16[4,256,256]{2,1,0:T(8,128)(2,1)S(1)} %get-tuple-element.23), channel_id=1, source_target_pairs={{0,8},{8,0},{1,9},{9,1},{2,10},{10,2},{3,11},{11,3},{4,12},{12,4},... | collective-permute-start | bytes 1572872 | tf_op jit(solution)/shard_map/dkv_over_core/ppermute | solution.py:288
  69.8 5.3 %all-to-all-start.2 = ((bf16[8,128,256]{2,1,0:T(8,128)(2,1)}), bf16[8,128,256]{2,1,0:T(8,128)(2,1)S(1)}, u32[]{:S(2)}, u32[]{:S(2)}) async-start(bf16[8,128,256]{2,1,0:T(8,128)(2,1)} %get-tuple-element.28), calls=%async_computation.2 | async-start | bytes 1048576 | tf_op jit(solution)/shard_map/dq_over_z/all_to_all | solution.py:349
  75.1 0.0 collective-permute-done.7.recv_ref
  75.1 0.1 dkv_over_core.1
  75.2 3.9 %collective-permute-start.8 = (bf16[256,256]{1,0:T(8,128)(2,1)S(1)}, bf16[256,256]{1,0:T(8,128)(2,1)S(1)}, u32[]{:S(2)}, u32[]{:S(2)}) collective-permute-start(bf16[256,256]{1,0:T(8,128)(2,1)S(1)} %get-tuple-element.25), channel_id=1, source_target_pairs={{0,384},{128,256},{256,128},{384,0},{1,385},{129,257},{257,129},{3... | collective-permute-start | bytes 393224 | tf_op jit(solution)/shard_map/dkv_over_y/ppermute | solution.py:288
  79.1 2.9 %collective-permute-start.9 = (bf16[256,256]{1,0:T(8,128)(2,1)S(1)}, bf16[256,256]{1,0:T(8,128)(2,1)S(1)}, u32[]{:S(2)}, u32[]{:S(2)}) collective-permute-start(bf16[256,256]{1,0:T(8,128)(2,1)S(1)} %get-tuple-element.26), channel_id=1, source_target_pairs={{0,256},{128,384},{256,0},{384,128},{1,257},{129,385},{257,1},{385... | collective-permute-start | bytes 393224 | tf_op jit(solution)/shard_map/dkv_over_y/ppermute | solution.py:288
  82.0 2.5 %collective-permute-start.10 = (bf16[256,256]{1,0:T(8,128)(2,1)S(1)}, bf16[256,256]{1,0:T(8,128)(2,1)S(1)}, u32[]{:S(2)}, u32[]{:S(2)}) collective-permute-start(bf16[256,256]{1,0:T(8,128)(2,1)S(1)} %get-tuple-element.27), channel_id=1, source_target_pairs={{0,128},{128,0},{256,384},{384,256},{1,129},{129,1},{257,385},{385... | collective-permute-start | bytes 393224 | tf_op jit(solution)/shard_map/dkv_over_y/ppermute | solution.py:288
  84.5 0.0 collective-permute-done.8.r1_ref
  84.5 7.6 %collective-permute-done.9.r2_ref = bf16[256,256]{1,0:T(8,128)(2,1)S(1)} collective-permute-done((bf16[256,256]{1,0:T(8,128)(2,1)S(1)}, bf16[256,256]{1,0:T(8,128)(2,1)S(1)}, u32[]{:S(2)}, u32[]{:S(2)}) %collective-permute-start.9) | collective-permute-done | bytes 131104 | tf_op jit(solution)/shard_map/dkv_over_y/ppermute | solution.py:288
  92.1 0.0 collective-permute-done.10.r3_ref
  92.1 1.0 %all-to-all-done.2.dq_ref = bf16[8,128,256]{2,1,0:T(8,128)(2,1)S(1)} async-done(((bf16[8,128,256]{2,1,0:T(8,128)(2,1)}), bf16[8,128,256]{2,1,0:T(8,128)(2,1)S(1)}, u32[]{:S(2)}, u32[]{:S(2)}) %all-to-all-start.2) | async-done | bytes 524320 | tf_op jit(solution)/shard_map/dq_over_z/all_to_all | solution.py:349
  93.1 0.8 final.1
  (4 shorter events, 0.1 us)
Async XLA Ops:
  3.2 21.8 %copy-start.2 = (bf16[272,256]{1,0:T(8,128)(2,1)S(1)}, bf16[272,256]{1,0:T(8,128)(2,1)}, u32[]{:S(2)}) copy-start(bf16[272,256]{1,0:T(8,128)(2,1)} %get-tuple-element.17.own_ref) | copy-start | bytes 417796
  3.2 20.9 %collective-permute-start.1 = (f32[128,128]{1,0:T(8,128)}, f32[128,128]{1,0:T(8,128)S(1)}, u32[]{:S(2)}, u32[]{:S(2)}) collective-permute-start(f32[128,128]{1,0:T(8,128)} %get-tuple-element.18.a_ref), channel_id=1, source_target_pairs={{0,1},{1,0},{2,3},{3,2},{4,5},{5,4},{6,7},{7,6},{8,9},{9,8},{10,11... | collective-permute-start | bytes 196616 | tf_op jit(solution)/shard_map/coupled_over_h/ppermute | solution.py:288
  11.6 13.3 %collective-permute-start = (bf16[272,256]{1,0:T(8,128)(2,1)}, bf16[272,256]{1,0:T(8,128)(2,1)S(1)}, u32[]{:S(2)}, u32[]{:S(2)}) collective-permute-start(bf16[272,256]{1,0:T(8,128)(2,1)} %get-tuple-element.17.own_ref), channel_id=1, source_target_pairs={{0,256},{128,384},{256,0},{384,128},{1,257},{129,385},{257,1},{385... | collective-permute-start | bytes 417800 | tf_op jit(solution)/shard_map/kv_over_y/ppermute | solution.py:288
  14.1 28.6 %all-to-all-start = ((bf16[8,144,256]{2,1,0:T(8,128)(2,1)}), bf16[8,144,256]{2,1,0:T(8,128)(2,1)S(1)}, u32[]{:S(2)}, u32[]{:S(2)}) async-start(bf16[8,144,256]{2,1,0:T(8,128)(2,1)} %get-tuple-element.16), calls=%async_computation | async-start | bytes 1179648 | tf_op jit(solution)/shard_map/q_over_z/all_to_all | solution.py:303
  24.1 0.8 copy-start.3
  25.0 11.3 %collective-permute-start.2 = (bf16[2,272,256]{2,1,0:T(8,128)(2,1)S(1)}, bf16[2,272,256]{2,1,0:T(8,128)(2,1)S(1)}, u32[]{:S(2)}, u32[]{:S(2)}) collective-permute-start(bf16[2,272,256]{2,1,0:T(8,128)(2,1)S(1)} %kv_over_y.1.own_ref), channel_id=1, source_target_pairs={{0,128},{128,0},{256,384},{384,256},{1,129},{129,1},{257,385},{385... | collective-permute-start | bytes 835592 | tf_op jit(solution)/shard_map/kv_over_y/ppermute | solution.py:288
  27.3 13.8 %collective-permute-start.6 = (f32[128,128]{1,0:T(8,128)S(1)}, f32[128,128]{1,0:T(8,128)S(1)}, u32[]{:S(2)}, u32[]{:S(2)}) collective-permute-start(f32[128,128]{1,0:T(8,128)S(1)} %coupled_over_h.1.after_ref.a_ref), channel_id=1, source_target_pairs={{0,6},{2,4},{4,2},{6,0},{1,7},{3,5},{5,3},{7,1},{8,14},{10,12},{12... | collective-permute-start | bytes 196616 | tf_op jit(solution)/shard_map/coupled_over_x/ppermute | solution.py:288
  31.7 9.4 %collective-permute-start.5 = (f32[128,128]{1,0:T(8,128)S(1)}, f32[128,128]{1,0:T(8,128)S(1)}, u32[]{:S(2)}, u32[]{:S(2)}) collective-permute-start(f32[128,128]{1,0:T(8,128)S(1)} %coupled_over_h.1.after_ref.a_ref), channel_id=1, source_target_pairs={{0,4},{2,6},{4,0},{6,2},{1,5},{3,7},{5,1},{7,3},{8,12},{10,14},{12... | collective-permute-start | bytes 196616 | tf_op jit(solution)/shard_map/coupled_over_x/ppermute | solution.py:288
  34.2 7.0 %collective-permute-start.4 = (f32[128,128]{1,0:T(8,128)S(1)}, f32[128,128]{1,0:T(8,128)S(1)}, u32[]{:S(2)}, u32[]{:S(2)}) collective-permute-start(f32[128,128]{1,0:T(8,128)S(1)} %coupled_over_h.1.after_ref.a_ref), channel_id=1, source_target_pairs={{0,2},{2,0},{4,6},{6,4},{1,3},{3,1},{5,7},{7,5},{8,10},{10,8},{12,... | collective-permute-start | bytes 196616 | tf_op jit(solution)/shard_map/coupled_over_x/ppermute | solution.py:288
  36.4 6.3 %copy-start = (bf16[128,256]{1,0:T(8,128)(2,1)S(1)}, bf16[128,256]{1,0:T(8,128)(2,1)}, u32[]{:S(2)}) copy-start(bf16[128,256]{1,0:T(8,128)(2,1)} %o_ref.1) | copy-start | bytes 196612
  36.4 6.3 %copy-start.1 = (bf16[256,128]{1,0:T(8,128)(2,1)S(1)}, bf16[256,128]{1,0:T(8,128)(2,1)}, u32[]{:S(2)}) copy-start(bf16[256,128]{1,0:T(8,128)(2,1)} %proj_ref.3) | copy-start | bytes 196612
  36.4 6.3 %copy-start.4 = (f32[128,64]{0,1:T(8,128)S(1)}, f32[128,64]{0,1:T(8,128)}, u32[]{:S(2)}) copy-start(f32[128,64]{0,1:T(8,128)} %param.7) | copy-start | bytes 98308
  36.4 6.2 %collective-permute-start.3 = (bf16[4,272,256]{2,1,0:T(8,128)(2,1)S(1)}, bf16[4,272,256]{2,1,0:T(8,128)(2,1)S(1)}, u32[]{:S(2)}, u32[]{:S(2)}) collective-permute-start(bf16[4,272,256]{2,1,0:T(8,128)(2,1)S(1)} %join.1.kva_ref), channel_id=1, source_target_pairs={{0,8},{8,0},{1,9},{9,1},{2,10},{10,2},{3,11},{11,3},{4,12},{12,4},... | collective-permute-start | bytes 1671176 | tf_op jit(solution)/shard_map/kv_over_core/ppermute | solution.py:288
  67.3 7.8 %collective-permute-start.7 = (bf16[4,256,256]{2,1,0:T(8,128)(2,1)S(1)}, bf16[4,256,256]{2,1,0:T(8,128)(2,1)S(1)}, u32[]{:S(2)}, u32[]{:S(2)}) collective-permute-start(bf16[4,256,256]{2,1,0:T(8,128)(2,1)S(1)} %get-tuple-element.23), channel_id=1, source_target_pairs={{0,8},{8,0},{1,9},{9,1},{2,10},{10,2},{3,11},{11,3},{4,12},{12,4},... | collective-permute-start | bytes 1572872 | tf_op jit(solution)/shard_map/dkv_over_core/ppermute | solution.py:288
  69.8 23.3 %all-to-all-start.2 = ((bf16[8,128,256]{2,1,0:T(8,128)(2,1)}), bf16[8,128,256]{2,1,0:T(8,128)(2,1)S(1)}, u32[]{:S(2)}, u32[]{:S(2)}) async-start(bf16[8,128,256]{2,1,0:T(8,128)(2,1)} %get-tuple-element.28), calls=%async_computation.2 | async-start | bytes 1048576 | tf_op jit(solution)/shard_map/dq_over_z/all_to_all | solution.py:349
  75.2 9.3 %collective-permute-start.8 = (bf16[256,256]{1,0:T(8,128)(2,1)S(1)}, bf16[256,256]{1,0:T(8,128)(2,1)S(1)}, u32[]{:S(2)}, u32[]{:S(2)}) collective-permute-start(bf16[256,256]{1,0:T(8,128)(2,1)S(1)} %get-tuple-element.25), channel_id=1, source_target_pairs={{0,384},{128,256},{256,128},{384,0},{1,385},{129,257},{257,129},{3... | collective-permute-start | bytes 393224 | tf_op jit(solution)/shard_map/dkv_over_y/ppermute | solution.py:288
  79.1 13.0 %collective-permute-start.9 = (bf16[256,256]{1,0:T(8,128)(2,1)S(1)}, bf16[256,256]{1,0:T(8,128)(2,1)S(1)}, u32[]{:S(2)}, u32[]{:S(2)}) collective-permute-start(bf16[256,256]{1,0:T(8,128)(2,1)S(1)} %get-tuple-element.26), channel_id=1, source_target_pairs={{0,256},{128,384},{256,0},{384,128},{1,257},{129,385},{257,1},{385... | collective-permute-start | bytes 393224 | tf_op jit(solution)/shard_map/dkv_over_y/ppermute | solution.py:288
  82.0 10.1 %collective-permute-start.10 = (bf16[256,256]{1,0:T(8,128)(2,1)S(1)}, bf16[256,256]{1,0:T(8,128)(2,1)S(1)}, u32[]{:S(2)}, u32[]{:S(2)}) collective-permute-start(bf16[256,256]{1,0:T(8,128)(2,1)S(1)} %get-tuple-element.27), channel_id=1, source_target_pairs={{0,128},{128,0},{256,384},{384,256},{1,129},{129,1},{257,385},{385... | collective-permute-start | bytes 393224 | tf_op jit(solution)/shard_map/dkv_over_y/ppermute | solution.py:288

commit v8 on v7

--- a/solution.py
+++ b/solution.py
@@ -39,29 +39,35 @@
 
 
 def prep_kernel(
-    pos_ref, q_hbm, k_hbm, v_hbm, o_hbm, proj_hbm, qpay_ref, kvpay_ref, part_ref, *scratch
+    pos_ref, k_hbm, v_hbm, o_hbm, proj_hbm, kvpay_ref, part_ref, *scratch
 ):
     buffers, sems = scratch[:-1], scratch[-1]
-    sources = (k_hbm, v_hbm, q_hbm, o_hbm, proj_hbm)
+    sources = (k_hbm, v_hbm, o_hbm, proj_hbm)
     copies = [
         pltpu.make_async_copy(src, dst, sems.at[n])
         for n, (src, dst) in enumerate(zip(sources, buffers))
     ]
     for copy in copies:
         copy.start()
-    k_ref, v_ref, q_ref, o_ref, proj_ref = buffers
+    k_ref, v_ref, o_ref, proj_ref = buffers
     block = lax.shift_right_logical(pos_ref[0], 6).astype(F32)
     tag = jnp.full((16, 256), block, F32).astype(BF16)
     for copy in copies:
         copy.wait()
-    k, v, q = k_ref[...], v_ref[...], q_ref[...]
+    k, v = k_ref[...], v_ref[...]
     kvpay_ref[0:128, :] = k
     kvpay_ref[128:256, :] = v
     kvpay_ref[256:272, :] = tag
+    part_ref[...] = dot(o_ref[...], proj_ref[...])
+
+
+def copies_kernel(pos_ref, q_ref, qpay_ref):
+    block = lax.shift_right_logical(pos_ref[0], 6).astype(F32)
+    tag = jnp.full((16, 256), block, F32).astype(BF16)
+    q = q_ref[...]
     for i in range(NZ):
         qpay_ref[i, 0:128, :] = q
         qpay_ref[i, 128:144, :] = tag
-    part_ref[...] = dot(o_ref[...], proj_ref[...])
 
 
 def query_positions(qg_ref):
@@ -290,15 +296,22 @@
 
 def local(n_x, n_h, latent, positions, queries, keys, values, attention_out, projection):
     with jax.named_scope("prep"):
-        qpay, kvpay, total = call(
+        kvpay, total = call(
             prep_kernel,
-            [((NZ, 144, 256), BF16), ((272, 256), BF16), ((128, 128), F32)],
+            [((272, 256), BF16), ((128, 128), F32)],
             10_000_000,
-            [pltpu.VMEM((128, 256), BF16)] * 4
-            + [pltpu.VMEM((256, 128), BF16), pltpu.SemaphoreType.DMA((5,))],
-            [pl.BlockSpec(memory_space=pltpu.SMEM)] + [pl.BlockSpec(memory_space=pltpu.HBM)] * 5,
+            [pltpu.VMEM((128, 256), BF16)] * 3
+            + [pltpu.VMEM((256, 128), BF16), pltpu.SemaphoreType.DMA((4,))],
+            [pl.BlockSpec(memory_space=pltpu.SMEM)] + [pl.BlockSpec(memory_space=pltpu.HBM)] * 4,
             limit=62,
-        )(positions, queries, keys, values, attention_out, projection)
+        )(positions, keys, values, attention_out, projection)
+    with jax.named_scope("q_copies"):
+        (qpay,) = call(
+            copies_kernel,
+            [((NZ, 144, 256), BF16)],
+            1_000_000,
+            specs=[pl.BlockSpec(memory_space=m) for m in (pltpu.SMEM, pltpu.VMEM)],
+        )(positions, queries)
     with jax.named_scope("q_over_z"):
         qg = lax.all_to_all(qpay, "z", 0, 0, axis_index_groups=RING_Q)
     with jax.named_scope("coupled_over_h"):

time: 94.6 us -> 96.6 us (1.021)
  blocking collectives: 18 us -> 16.4 us
  local copies, waits for them, and re-layouts: 0.86 us -> 2.35 us
  Pallas kernels: 10.1 us -> 11.4 us
    all_to_all x1, blocking collectives: 18 us -> 16.4 us  [local(): gathered = lax.all_to_all(pay, 'z', 0, 0, axis_index_groups=RING_P)]
    unnamed x10 -> x14, local copies, waits for them, and re-layouts: 0.86 us -> 2.35 us
    pallas_call x9 -> x10, Pallas kernels: 10.1 us -> 11.4 us  [run(): pl.pallas_call(kernel, out_shape=[jax.ShapeDtypeStruct(s, d) for s, d in...]
    ppermute x11, starting transfers between devices: 38.5 us -> 39.8 us  [swap(): return lax.ppermute(x, axis, [(i, i ^ k) for i in range(size)])]
  transfers between devices with their start and end apart: 13 -> 13, of which waited for: 3 -> 3; matrix products, arithmetic and copies ran while one was open for 0% -> 0% of each run, Pallas kernels for 0% -> 2%
where the time goes in v8:
time: 96.6 us; the launch traced here: 95.8 us
  starting transfers between devices  54.7 us (57%)
  blocking collectives  16.4 us (17%)
  Pallas kernels  11.4 us (12%)
  waiting for transfers between devices  10.1 us (10%)
  local copies, waits for them, and re-layouts  2.35 us (2%)
    ppermute x11, starting transfers between devices, swap(): return lax.ppermute(x, axis, [(i, i ^ k) for i in range(size)])  39.8 us
    all_to_all x1, blocking collectives, local(): gathered = lax.all_to_all(pay, 'z', 0, 0, axis_index_groups=RING_P)  16.4 us
    pallas_call x10, Pallas kernels, run(): pl.pallas_call(kernel, out_shape=[jax.ShapeDtypeStruct(s, d) for s, d in...  11.4 us
    all_to_all x1, starting transfers between devices, local(): qg = lax.all_to_all(qpay, 'z', 0, 0, axis_index_groups=RING_Q)  10 us
    ppermute x11, waiting for transfers between devices, swap(): return lax.ppermute(x, axis, [(i, i ^ k) for i in range(size)])  8.15 us
    all_to_all x1, starting transfers between devices, local(): dqs = lax.all_to_all(dq, 'z', 0, 0, axis_index_groups=RING_D)  4.82 us
    unnamed x14, local copies, waits for them, and re-layouts  2.35 us
    all_to_all x1, waiting for transfers between devices, local(): dqs = lax.all_to_all(dq, 'z', 0, 0, axis_index_groups=RING_D)  1.97 us
  transfers between devices with their start and end apart: 13, of which 3 were waited for; matrix products, arithmetic and copies ran while one was open for 0% of the time, Pallas kernels for 2%

profile of v8, /device:TPU:1, one launch (start us, length us, event | category | flops | bytes accessed | tf_op | source)
XLA Modules:
  0.0 95.8 jit_solution(11576210324366857861)
XLA Ops:
  0.6 2.4 %prep.1 = (bf16[272,256]{1,0:T(8,128)(2,1)}, f32[128,128]{1,0:T(8,128)}) custom-call(s32[128]{0:T(128)} %pos_ref.3, bf16[128,256]{1,0:T(8,128)(2,1)} %k_hbm.1, bf16[128,256]{1,0:T(8,128)(2,1)} %v_hbm.1, bf16[128,256]{1,0:T(8,128)(2,1)} %o_ref.1, bf16[256,128]{1,0:T(8,128)(2,1)} %proj_ref.3), custom_call_target="tpu_custom_call" | custom-call | flops 10000000 | bytes 2097152 | tf_op jit(solution)/shard_map/prep/pallas_call | solution.py:280
  3.1 8.3 %collective-permute-start.1 = (f32[128,128]{1,0:T(8,128)}, f32[128,128]{1,0:T(8,128)S(1)}, u32[]{:S(2)}, u32[]{:S(2)}) collective-permute-start(f32[128,128]{1,0:T(8,128)} %get-tuple-element.16.a_ref), channel_id=1, source_target_pairs={{0,1},{1,0},{2,3},{3,2},{4,5},{5,4},{6,7},{7,6},{8,9},{9,8},{10,11... | collective-permute-start | bytes 196616 | tf_op jit(solution)/shard_map/coupled_over_h/ppermute | solution.py:294
  11.3 2.4 %collective-permute-start = (bf16[272,256]{1,0:T(8,128)(2,1)}, bf16[272,256]{1,0:T(8,128)(2,1)S(1)}, u32[]{:S(2)}, u32[]{:S(2)}) collective-permute-start(bf16[272,256]{1,0:T(8,128)(2,1)} %get-tuple-element.15.own_ref), channel_id=1, source_target_pairs={{0,256},{128,384},{256,0},{384,128},{1,257},{129,385},{257,1},{385... | collective-permute-start | bytes 417800 | tf_op jit(solution)/shard_map/kv_over_y/ppermute | solution.py:294
  13.8 0.0 copy-start
  13.8 0.8 copy-done
  14.6 0.0 copy-start.3
  14.6 0.7 copy-done.3
  15.3 0.0 copy-start.4
  15.3 1.4 %q_copies.1 = bf16[8,144,256]{2,1,0:T(8,128)(2,1)} custom-call(s32[128]{0:T(128)S(1)} %copy-done.3, bf16[128,256]{1,0:T(8,128)(2,1)S(1)} %copy-done), custom_call_target="tpu_custom_call" | custom-call | flops 1000000 | bytes 2097152 | tf_op jit(solution)/shard_map/q_copies/pallas_call | solution.py:280
  16.7 10.0 %all-to-all-start = ((bf16[8,144,256]{2,1,0:T(8,128)(2,1)}), bf16[8,144,256]{2,1,0:T(8,128)(2,1)S(1)}, u32[]{:S(2)}, u32[]{:S(2)}) async-start(bf16[8,144,256]{2,1,0:T(8,128)(2,1)} %q_copies.1), calls=%async_computation | async-start | bytes 1179648 | tf_op jit(solution)/shard_map/q_over_z/all_to_all | solution.py:316
  26.7 0.0 collective-permute-done.1.b_ref
  26.7 0.0 copy-start.5
  26.7 0.8 copy-done.5
  27.6 0.0 collective-permute-done.far_ref
  27.6 0.0 copy-done.4
  27.6 2.3 %collective-permute-start.2 = (bf16[2,272,256]{2,1,0:T(8,128)(2,1)S(1)}, bf16[2,272,256]{2,1,0:T(8,128)(2,1)S(1)}, u32[]{:S(2)}, u32[]{:S(2)}) collective-permute-start(bf16[2,272,256]{2,1,0:T(8,128)(2,1)S(1)} %kv_over_y.1.own_ref), channel_id=1, source_target_pairs={{0,128},{128,0},{256,384},{384,256},{1,129},{129,1},{257,385},{385... | collective-permute-start | bytes 835592 | tf_op jit(solution)/shard_map/kv_over_y/ppermute | solution.py:294
  29.9 4.4 %collective-permute-start.6 = (f32[128,128]{1,0:T(8,128)S(1)}, f32[128,128]{1,0:T(8,128)S(1)}, u32[]{:S(2)}, u32[]{:S(2)}) collective-permute-start(f32[128,128]{1,0:T(8,128)S(1)} %coupled_over_h.1.after_ref.a_ref), channel_id=1, source_target_pairs={{0,6},{2,4},{4,2},{6,0},{1,7},{3,5},{5,3},{7,1},{8,14},{10,12},{12... | collective-permute-start | bytes 196616 | tf_op jit(solution)/shard_map/coupled_over_x/ppermute | solution.py:294
  34.3 2.4 %collective-permute-start.5 = (f32[128,128]{1,0:T(8,128)S(1)}, f32[128,128]{1,0:T(8,128)S(1)}, u32[]{:S(2)}, u32[]{:S(2)}) collective-permute-start(f32[128,128]{1,0:T(8,128)S(1)} %coupled_over_h.1.after_ref.a_ref), channel_id=1, source_target_pairs={{0,4},{2,6},{4,0},{6,2},{1,5},{3,7},{5,1},{7,3},{8,12},{10,14},{12... | collective-permute-start | bytes 196616 | tf_op jit(solution)/shard_map/coupled_over_x/ppermute | solution.py:294
  36.8 2.2 %collective-permute-start.4 = (f32[128,128]{1,0:T(8,128)S(1)}, f32[128,128]{1,0:T(8,128)S(1)}, u32[]{:S(2)}, u32[]{:S(2)}) collective-permute-start(f32[128,128]{1,0:T(8,128)S(1)} %coupled_over_h.1.after_ref.a_ref), channel_id=1, source_target_pairs={{0,2},{2,0},{4,6},{6,4},{1,3},{3,1},{5,7},{7,5},{8,10},{10,8},{12,... | collective-permute-start | bytes 196616 | tf_op jit(solution)/shard_map/coupled_over_x/ppermute | solution.py:294
  38.9 0.0 collective-permute-done.2.recv_ref
  39.0 0.0 copy-start.1
  39.0 0.0 copy-start.2
  39.0 0.0 copy-start.6
  39.0 4.7 %collective-permute-start.3 = (bf16[4,272,256]{2,1,0:T(8,128)(2,1)S(1)}, bf16[4,272,256]{2,1,0:T(8,128)(2,1)S(1)}, u32[]{:S(2)}, u32[]{:S(2)}) collective-permute-start(bf16[4,272,256]{2,1,0:T(8,128)(2,1)S(1)} %join.1.kva_ref), channel_id=1, source_target_pairs={{0,8},{8,0},{1,9},{9,1},{2,10},{10,2},{3,11},{11,3},{4,12},{12,4},... | collective-permute-start | bytes 1671176 | tf_op jit(solution)/shard_map/kv_over_core/ppermute | solution.py:294
  43.7 0.0 collective-permute-done.6.d_ref
  43.7 0.0 collective-permute-done.5.c_ref
  43.8 0.0 collective-permute-done.4.b_ref
  43.8 1.5 %collective-permute-done.3.kvb_ref = bf16[4,272,256]{2,1,0:T(8,128)(2,1)S(1)} collective-permute-done((bf16[4,272,256]{2,1,0:T(8,128)(2,1)S(1)}, bf16[4,272,256]{2,1,0:T(8,128)(2,1)S(1)}, u32[]{:S(2)}, u32[]{:S(2)}) %collective-permute-start.3) | collective-permute-done | bytes 557088 | tf_op jit(solution)/shard_map/kv_over_core/ppermute | solution.py:294
  45.3 0.0 all-to-all-done.qg_ref
  45.3 0.0 copy-done.1
  45.3 0.0 copy-done.2
  45.3 0.0 copy-done.6
  45.3 2.2 %stats.1 = (bf16[8,176,128]{2,1,0:T(8,128)(2,1)S(1)}, bf16[2,1024,1024]{2,1,0:T(8,128)(2,1)S(1)}, f32[16,128]{1,0:T(8,128)S(1)}) custom-call(bf16[8,144,256]{2,1,0:T(8,128)(2,1)S(1)} %all-to-all-done.qg_ref, bf16[4,272,256]{2,1,0:T(8,128)(2,1)S(1)} %join.1.kva_ref, bf16[4,272,256]{2,1,0:T(8,128)(2,1)S(1)} %collective-permute-done.3.kvb_ref, ...), custom_call_target="tpu_custom_call" | custom-call | flops 1000000000 | bytes 2097152 | tf_op jit(solution)/shard_map/stats/pallas_call | solution.py:280
  47.6 16.4 %all_to_all.15.g_ref = bf16[8,176,128]{2,1,0:T(8,128)(2,1)S(1)} all-to-all(bf16[8,176,128]{2,1,0:T(8,128)(2,1)S(1)} %get-tuple-element.17), channel_id=1, replica_groups={{112,96,80,64,48,32,16,0},{113,97,81,65,49,33,17,1},{114,98,82,66,50,34..., dimensions={0} | all-to-all | bytes 720896 | tf_op jit(solution)/shard_map/upstream_over_z/all_to_all | solution.py:345
  64.0 4.4 %main.1 = (bf16[8,128,256]{2,1,0:T(8,128)(2,1)}, bf16[4,256,256]{2,1,0:T(8,128)(2,1)S(1)}, bf16[4,256,256]{2,1,0:T(8,128)(2,1)S(1)}) custom-call(bf16[8,144,256]{2,1,0:T(8,128)(2,1)S(1)} %all-to-all-done.qg_ref, bf16[4,272,256]{2,1,0:T(8,128)(2,1)S(1)} %join.1.kva_ref, bf16[4,272,256]{2,1,0:T(8,128)(2,1)S(1)} %collective-permute-done.3.kvb_ref, ...), custom_call_target="tpu_custom_call" | custom-call | flops 4000000000 | bytes 2097152 | tf_op jit(solution)/shard_map/main/pallas_call | solution.py:280
  68.3 3.9 %collective-permute-start.7 = (bf16[4,256,256]{2,1,0:T(8,128)(2,1)S(1)}, bf16[4,256,256]{2,1,0:T(8,128)(2,1)S(1)}, u32[]{:S(2)}, u32[]{:S(2)}) collective-permute-start(bf16[4,256,256]{2,1,0:T(8,128)(2,1)S(1)} %get-tuple-element.21), channel_id=1, source_target_pairs={{0,8},{8,0},{1,9},{9,1},{2,10},{10,2},{3,11},{11,3},{4,12},{12,4},... | collective-permute-start | bytes 1572872 | tf_op jit(solution)/shard_map/dkv_over_core/ppermute | solution.py:294
  72.2 4.8 %all-to-all-start.2 = ((bf16[8,128,256]{2,1,0:T(8,128)(2,1)}), bf16[8,128,256]{2,1,0:T(8,128)(2,1)S(1)}, u32[]{:S(2)}, u32[]{:S(2)}) async-start(bf16[8,128,256]{2,1,0:T(8,128)(2,1)} %get-tuple-element.26), calls=%async_computation.2 | async-start | bytes 1048576 | tf_op jit(solution)/shard_map/dq_over_z/all_to_all | solution.py:362
  77.1 0.0 collective-permute-done.7.recv_ref
  77.1 0.1 dkv_over_core.1
  77.2 4.5 %collective-permute-start.8 = (bf16[256,256]{1,0:T(8,128)(2,1)S(1)}, bf16[256,256]{1,0:T(8,128)(2,1)S(1)}, u32[]{:S(2)}, u32[]{:S(2)}) collective-permute-start(bf16[256,256]{1,0:T(8,128)(2,1)S(1)} %get-tuple-element.23), channel_id=1, source_target_pairs={{0,384},{128,256},{256,128},{384,0},{1,385},{129,257},{257,129},{3... | collective-permute-start | bytes 393224 | tf_op jit(solution)/shard_map/dkv_over_y/ppermute | solution.py:294
  81.7 1.9 %collective-permute-start.9 = (bf16[256,256]{1,0:T(8,128)(2,1)S(1)}, bf16[256,256]{1,0:T(8,128)(2,1)S(1)}, u32[]{:S(2)}, u32[]{:S(2)}) collective-permute-start(bf16[256,256]{1,0:T(8,128)(2,1)S(1)} %get-tuple-element.24), channel_id=1, source_target_pairs={{0,256},{128,384},{256,0},{384,128},{1,257},{129,385},{257,1},{385... | collective-permute-start | bytes 393224 | tf_op jit(solution)/shard_map/dkv_over_y/ppermute | solution.py:294
  83.7 2.8 %collective-permute-start.10 = (bf16[256,256]{1,0:T(8,128)(2,1)S(1)}, bf16[256,256]{1,0:T(8,128)(2,1)S(1)}, u32[]{:S(2)}, u32[]{:S(2)}) collective-permute-start(bf16[256,256]{1,0:T(8,128)(2,1)S(1)} %get-tuple-element.25), channel_id=1, source_target_pairs={{0,128},{128,0},{256,384},{384,256},{1,129},{129,1},{257,385},{385... | collective-permute-start | bytes 393224 | tf_op jit(solution)/shard_map/dkv_over_y/ppermute | solution.py:294
  86.5 0.0 collective-permute-done.8.r1_ref
  86.5 6.6 %collective-permute-done.9.r2_ref = bf16[256,256]{1,0:T(8,128)(2,1)S(1)} collective-permute-done((bf16[256,256]{1,0:T(8,128)(2,1)S(1)}, bf16[256,256]{1,0:T(8,128)(2,1)S(1)}, u32[]{:S(2)}, u32[]{:S(2)}) %collective-permute-start.9) | collective-permute-done | bytes 131104 | tf_op jit(solution)/shard_map/dkv_over_y/ppermute | solution.py:294
  93.1 0.0 collective-permute-done.10.r3_ref
  93.1 2.0 %all-to-all-done.2.dq_ref = bf16[8,128,256]{2,1,0:T(8,128)(2,1)S(1)} async-done(((bf16[8,128,256]{2,1,0:T(8,128)(2,1)}), bf16[8,128,256]{2,1,0:T(8,128)(2,1)S(1)}, u32[]{:S(2)}, u32[]{:S(2)}) %all-to-all-start.2) | async-done | bytes 524320 | tf_op jit(solution)/shard_map/dq_over_z/all_to_all | solution.py:362
  95.1 0.8 final.1
  (4 shorter events, 0.1 us)
Async XLA Ops:
  3.1 23.7 %collective-permute-start.1 = (f32[128,128]{1,0:T(8,128)}, f32[128,128]{1,0:T(8,128)S(1)}, u32[]{:S(2)}, u32[]{:S(2)}) collective-permute-start(f32[128,128]{1,0:T(8,128)} %get-tuple-element.16.a_ref), channel_id=1, source_target_pairs={{0,1},{1,0},{2,3},{3,2},{4,5},{5,4},{6,7},{7,6},{8,9},{9,8},{10,11... | collective-permute-start | bytes 196616 | tf_op jit(solution)/shard_map/coupled_over_h/ppermute | solution.py:294
  11.3 16.2 %collective-permute-start = (bf16[272,256]{1,0:T(8,128)(2,1)}, bf16[272,256]{1,0:T(8,128)(2,1)S(1)}, u32[]{:S(2)}, u32[]{:S(2)}) collective-permute-start(bf16[272,256]{1,0:T(8,128)(2,1)} %get-tuple-element.15.own_ref), channel_id=1, source_target_pairs={{0,256},{128,384},{256,0},{384,128},{1,257},{129,385},{257,1},{385... | collective-permute-start | bytes 417800 | tf_op jit(solution)/shard_map/kv_over_y/ppermute | solution.py:294
  13.8 0.8 copy-start
  14.6 0.7 copy-start.3
  15.3 12.3 %copy-start.4 = (bf16[272,256]{1,0:T(8,128)(2,1)S(1)}, bf16[272,256]{1,0:T(8,128)(2,1)}, u32[]{:S(2)}) copy-start(bf16[272,256]{1,0:T(8,128)(2,1)} %get-tuple-element.15.own_ref) | copy-start | bytes 417796
  16.7 28.6 %all-to-all-start = ((bf16[8,144,256]{2,1,0:T(8,128)(2,1)}), bf16[8,144,256]{2,1,0:T(8,128)(2,1)S(1)}, u32[]{:S(2)}, u32[]{:S(2)}) async-start(bf16[8,144,256]{2,1,0:T(8,128)(2,1)} %q_copies.1), calls=%async_computation | async-start | bytes 1179648 | tf_op jit(solution)/shard_map/q_over_z/all_to_all | solution.py:316
  26.7 0.8 copy-start.5
  27.6 11.3 %collective-permute-start.2 = (bf16[2,272,256]{2,1,0:T(8,128)(2,1)S(1)}, bf16[2,272,256]{2,1,0:T(8,128)(2,1)S(1)}, u32[]{:S(2)}, u32[]{:S(2)}) collective-permute-start(bf16[2,272,256]{2,1,0:T(8,128)(2,1)S(1)} %kv_over_y.1.own_ref), channel_id=1, source_target_pairs={{0,128},{128,0},{256,384},{384,256},{1,129},{129,1},{257,385},{385... | collective-permute-start | bytes 835592 | tf_op jit(solution)/shard_map/kv_over_y/ppermute | solution.py:294
  29.9 13.8 %collective-permute-start.6 = (f32[128,128]{1,0:T(8,128)S(1)}, f32[128,128]{1,0:T(8,128)S(1)}, u32[]{:S(2)}, u32[]{:S(2)}) collective-permute-start(f32[128,128]{1,0:T(8,128)S(1)} %coupled_over_h.1.after_ref.a_ref), channel_id=1, source_target_pairs={{0,6},{2,4},{4,2},{6,0},{1,7},{3,5},{5,3},{7,1},{8,14},{10,12},{12... | collective-permute-start | bytes 196616 | tf_op jit(solution)/shard_map/coupled_over_x/ppermute | solution.py:294
  34.3 9.4 %collective-permute-start.5 = (f32[128,128]{1,0:T(8,128)S(1)}, f32[128,128]{1,0:T(8,128)S(1)}, u32[]{:S(2)}, u32[]{:S(2)}) collective-permute-start(f32[128,128]{1,0:T(8,128)S(1)} %coupled_over_h.1.after_ref.a_ref), channel_id=1, source_target_pairs={{0,4},{2,6},{4,0},{6,2},{1,5},{3,7},{5,1},{7,3},{8,12},{10,14},{12... | collective-permute-start | bytes 196616 | tf_op jit(solution)/shard_map/coupled_over_x/ppermute | solution.py:294
  36.8 7.0 %collective-permute-start.4 = (f32[128,128]{1,0:T(8,128)S(1)}, f32[128,128]{1,0:T(8,128)S(1)}, u32[]{:S(2)}, u32[]{:S(2)}) collective-permute-start(f32[128,128]{1,0:T(8,128)S(1)} %coupled_over_h.1.after_ref.a_ref), channel_id=1, source_target_pairs={{0,2},{2,0},{4,6},{6,4},{1,3},{3,1},{5,7},{7,5},{8,10},{10,8},{12,... | collective-permute-start | bytes 196616 | tf_op jit(solution)/shard_map/coupled_over_x/ppermute | solution.py:294
  39.0 6.3 %copy-start.1 = (bf16[128,256]{1,0:T(8,128)(2,1)S(1)}, bf16[128,256]{1,0:T(8,128)(2,1)}, u32[]{:S(2)}) copy-start(bf16[128,256]{1,0:T(8,128)(2,1)} %o_ref.1) | copy-start | bytes 196612
  39.0 6.3 %copy-start.2 = (bf16[256,128]{1,0:T(8,128)(2,1)S(1)}, bf16[256,128]{1,0:T(8,128)(2,1)}, u32[]{:S(2)}) copy-start(bf16[256,128]{1,0:T(8,128)(2,1)} %proj_ref.3) | copy-start | bytes 196612
  39.0 6.3 %copy-start.6 = (f32[128,64]{0,1:T(8,128)S(1)}, f32[128,64]{0,1:T(8,128)}, u32[]{:S(2)}) copy-start(f32[128,64]{0,1:T(8,128)} %param.7) | copy-start | bytes 98308
  39.0 6.3 %collective-permute-start.3 = (bf16[4,272,256]{2,1,0:T(8,128)(2,1)S(1)}, bf16[4,272,256]{2,1,0:T(8,128)(2,1)S(1)}, u32[]{:S(2)}, u32[]{:S(2)}) collective-permute-start(bf16[4,272,256]{2,1,0:T(8,128)(2,1)S(1)} %join.1.kva_ref), channel_id=1, source_target_pairs={{0,8},{8,0},{1,9},{9,1},{2,10},{10,2},{3,11},{11,3},{4,12},{12,4},... | collective-permute-start | bytes 1671176 | tf_op jit(solution)/shard_map/kv_over_core/ppermute | solution.py:294
  68.3 8.7 %collective-permute-start.7 = (bf16[4,256,256]{2,1,0:T(8,128)(2,1)S(1)}, bf16[4,256,256]{2,1,0:T(8,128)(2,1)S(1)}, u32[]{:S(2)}, u32[]{:S(2)}) collective-permute-start(bf16[4,256,256]{2,1,0:T(8,128)(2,1)S(1)} %get-tuple-element.21), channel_id=1, source_target_pairs={{0,8},{8,0},{1,9},{9,1},{2,10},{10,2},{3,11},{11,3},{4,12},{12,4},... | collective-permute-start | bytes 1572872 | tf_op jit(solution)/shard_map/dkv_over_core/ppermute | solution.py:294
  72.2 22.9 %all-to-all-start.2 = ((bf16[8,128,256]{2,1,0:T(8,128)(2,1)}), bf16[8,128,256]{2,1,0:T(8,128)(2,1)S(1)}, u32[]{:S(2)}, u32[]{:S(2)}) async-start(bf16[8,128,256]{2,1,0:T(8,128)(2,1)} %get-tuple-element.26), calls=%async_computation.2 | async-start | bytes 1048576 | tf_op jit(solution)/shard_map/dq_over_z/all_to_all | solution.py:362
  77.2 9.3 %collective-permute-start.8 = (bf16[256,256]{1,0:T(8,128)(2,1)S(1)}, bf16[256,256]{1,0:T(8,128)(2,1)S(1)}, u32[]{:S(2)}, u32[]{:S(2)}) collective-permute-start(bf16[256,256]{1,0:T(8,128)(2,1)S(1)} %get-tuple-element.23), channel_id=1, source_target_pairs={{0,384},{128,256},{256,128},{384,0},{1,385},{129,257},{257,129},{3... | collective-permute-start | bytes 393224 | tf_op jit(solution)/shard_map/dkv_over_y/ppermute | solution.py:294
  81.7 11.4 %collective-permute-start.9 = (bf16[256,256]{1,0:T(8,128)(2,1)S(1)}, bf16[256,256]{1,0:T(8,128)(2,1)S(1)}, u32[]{:S(2)}, u32[]{:S(2)}) collective-permute-start(bf16[256,256]{1,0:T(8,128)(2,1)S(1)} %get-tuple-element.24), channel_id=1, source_target_pairs={{0,256},{128,384},{256,0},{384,128},{1,257},{129,385},{257,1},{385... | collective-permute-start | bytes 393224 | tf_op jit(solution)/shard_map/dkv_over_y/ppermute | solution.py:294
  83.7 9.4 %collective-permute-start.10 = (bf16[256,256]{1,0:T(8,128)(2,1)S(1)}, bf16[256,256]{1,0:T(8,128)(2,1)S(1)}, u32[]{:S(2)}, u32[]{:S(2)}) collective-permute-start(bf16[256,256]{1,0:T(8,128)(2,1)S(1)} %get-tuple-element.25), channel_id=1, source_target_pairs={{0,128},{128,0},{256,384},{384,256},{1,129},{129,1},{257,385},{385... | collective-permute-start | bytes 393224 | tf_op jit(solution)/shard_map/dkv_over_y/ppermute | solution.py:294
